TPU v7x, 32 devices: a whole 2x2x4 slice. The times are simulated.
32 devices in a mesh: section: 2 (over core), seq: 4 (over z), fsdp: 4 (over y, x).
Axes of the slice: x: 2, y: 2, z: 4, core: 2. Of those that a mesh axis runs over, the one named last changes fastest.
Arguments:
- hidden_in: bfloat16 [2, 1024, 640], P(None, ('seq', 'fsdp')), may hold values from -6 to 6
- cotangent: bfloat16 [2, 1024, 640], P(None, ('seq', 'fsdp')), may hold values from -6 to 6
- positions: int32 [2, 1024], P(None, ('seq', 'fsdp')), may hold values from 0 to 1023, as said below
- attn_gain: bfloat16 [2, 640], P('section', 'fsdp'), may hold values from 0.25 to 1.75
- w_query: bfloat16 [2, 640, 1024], P('section', 'fsdp'), may hold values from -0.25 to 0.25
- w_key: bfloat16 [2, 640, 256], P('section', 'fsdp'), may hold values from -0.25 to 0.25
- w_value: bfloat16 [2, 640, 256], P('section', 'fsdp'), may hold values from -0.25 to 0.25
- query_gain: bfloat16 [2, 256], P('section', 'fsdp'), may hold values from 0.25 to 1.75
- key_gain: bfloat16 [2, 256], P('section', 'fsdp'), may hold values from 0.25 to 1.75
- w_output: bfloat16 [2, 1024, 640], P('section', 'fsdp'), may hold values from -0.1875 to 0.1875
- post_attn_gain: bfloat16 [2, 640], P('section', 'fsdp'), may hold values from 0.25 to 1.75
- ffn_gain: bfloat16 [2, 640], P('section', 'fsdp'), may hold values from 0.25 to 1.75
- w_gate: bfloat16 [2, 640, 2048], P('section', 'fsdp'), may hold values from -0.25 to 0.25
- w_up: bfloat16 [2, 640, 2048], P('section', 'fsdp'), may hold values from -0.25 to 0.25
- w_down: bfloat16 [2, 2048, 640], P('section', 'fsdp'), may hold values from -0.125 to 0.125
- post_ffn_gain: bfloat16 [2, 640], P('section', 'fsdp'), may hold values from 0.25 to 1.75
Outputs:
- section_outputs: bfloat16 [2, 2, 1024, 640], P('section', None, ('seq', 'fsdp'))
- input_grads: bfloat16 [2, 2, 1024, 640], P('section', None, ('seq', 'fsdp'))
- grad_attn_gain: float32 [2, 640], P('section', 'fsdp')
- grad_w_query: float32 [2, 640, 1024], P('section', 'fsdp')
- grad_w_key: float32 [2, 640, 256], P('section', 'fsdp')
- grad_w_value: float32 [2, 640, 256], P('section', 'fsdp')
- query_gain_gradient: float32 [2, 256], P('section', 'fsdp')
- grad_key_gain: float32 [2, 256], P('section', 'fsdp')
- grad_w_output: float32 [2, 1024, 640], P('section', 'fsdp')
- grad_post_attn_gain: float32 [2, 640], P('section', 'fsdp')
- grad_ffn_gain: float32 [2, 640], P('section', 'fsdp')
- grad_w_gate: float32 [2, 640, 2048], P('section', 'fsdp')
- grad_w_up: float32 [2, 640, 2048], P('section', 'fsdp')
- grad_w_down: float32 [2, 2048, 640], P('section', 'fsdp')
- grad_post_ffn_gain: float32 [2, 640], P('section', 'fsdp')
Inputs may be any that keep to these rules, and one draw needn't show every extreme that they name: `positions`: in every row a document begins at the first token (place 0) and each later token's place is one more than the one before it unless a new document begins there at place 0; one row, chosen by the seed, is a single document of all 1024 tokens.
All inputs are finite; a program needn't handle non-finite values.
Results may differ from a plain program's by a relative error of at most 0.025.
Values may be sent and summed in bfloat16 or wider, within the bound.
No kernel may reach another device: no remote copies, remote signals or barrier semaphores. Data moves between devices by JAX's collectives and lax.ppermute only.
A program may use at most 192 MiB of HBM per device.

v0:
```python
from functools import partial

import jax
import jax.numpy as jnp
from jax import lax
from jax.sharding import PartitionSpec as P

WIN = 512


EPSILON = 1e-06
ROPE_BASE = 10000.0
NEG_LARGE = -1e30


def shifted(shard, axis, by):
    devices = lax.axis_size(axis)
    pairs = [(i, i + by) for i in range(devices) if 0 <= i + by < devices]
    return lax.ppermute(shard, axis, pairs)


def norm_gain(values, scale_row):
    return (
        values * lax.rsqrt(jnp.mean(values * values, axis=-1, keepdims=True) + EPSILON) * scale_row
    )


def rotate(values, token_pos):
    half_dim = values.shape[-1] // 2
    frequency = ROPE_BASE ** (-2.0 * jnp.arange(half_dim, dtype=jnp.float32) / values.shape[-1])
    angles = token_pos.astype(jnp.float32)[:, None] * frequency[None, :]
    if values.ndim == 3:
        angles = angles[:, None, :]
    cosine = jnp.cos(angles)
    sine_part = jnp.sin(angles)
    first_half = values[..., :half_dim]
    second_half = values[..., half_dim:]
    return jnp.concatenate(
        (
            first_half * cosine - second_half * sine_part,
            second_half * cosine + first_half * sine_part,
        ),
        axis=-1,
    )


def qk_post(query_proj, key_proj, query_scale, key_scale, token_pos):
    return (
        rotate(norm_gain(query_proj, query_scale), token_pos),
        rotate(norm_gain(key_proj, key_scale), token_pos),
    )


def window_mask(token_pos, key_count):
    distance = WIN + jnp.arange(token_pos.shape[0])[:, None] - jnp.arange(key_count)[None, :]
    return (distance >= 0) & (distance < WIN) & (distance <= token_pos[:, None])


def mlp_act(gate_pre, up_pre):
    return jax.nn.gelu(gate_pre, approximate=True) * up_pre


def post_add(residual, branch, scale_row):
    return residual + norm_gain(branch, scale_row)


def attend_forward(query_b, keys_all, token_pos):
    head_dim = query_b.shape[-1]
    scores = jnp.einsum(
        "thd,kd->htk", query_b, keys_all[:, :head_dim], preferred_element_type=jnp.float32
    ) * head_dim ** (-0.5)
    allowed = window_mask(token_pos, keys_all.shape[0])[None]
    masked = jnp.where(allowed, scores, NEG_LARGE)
    row_peak = jnp.max(masked, axis=-1, keepdims=True)
    exponent = jnp.exp(masked - row_peak)
    row_total = jnp.sum(exponent, axis=-1, keepdims=True)
    attention_b = (exponent / row_total).astype(jnp.bfloat16)
    attended = jnp.einsum(
        "htk,kd->thd", attention_b, keys_all[:, head_dim:], preferred_element_type=jnp.float32
    )
    return (attended, row_peak + jnp.log(row_total))


def attend_backward(grad_out, query_b, keys_all, token_pos, log_total):
    head_dim = query_b.shape[-1]
    score_scale = head_dim ** (-0.5)
    key_part = keys_all[:, :head_dim]
    value_part = keys_all[:, head_dim:]
    scores = (
        jnp.einsum("thd,kd->htk", query_b, key_part, preferred_element_type=jnp.float32)
        * score_scale
    )
    allowed = window_mask(token_pos, keys_all.shape[0])[None]
    attention = jnp.where(allowed, jnp.exp(scores - log_total), 0.0)
    attention_b = attention.astype(jnp.bfloat16)
    grad_value = jnp.einsum(
        "htk,thd->kd", attention_b, grad_out, preferred_element_type=jnp.float32
    )
    grad_attention = jnp.einsum(
        "thd,kd->htk", grad_out, value_part, preferred_element_type=jnp.float32
    )
    row_inner = jnp.sum(attention * grad_attention, axis=-1, keepdims=True)
    grad_scores = (attention * (grad_attention - row_inner)).astype(jnp.bfloat16)
    grad_query = (
        jnp.einsum("htk,kd->thd", grad_scores, key_part, preferred_element_type=jnp.float32)
        * score_scale
    )
    grad_key = (
        jnp.einsum("htk,thd->kd", grad_scores, query_b, preferred_element_type=jnp.float32)
        * score_scale
    )
    return (grad_query, jnp.concatenate((grad_key, grad_value), axis=1))


def fetch_window(kv_own):
    neighbours = WIN // kv_own.shape[0]
    pieces = []
    for distance in range(neighbours, 0, -1):
        pieces.append(shifted(kv_own, ("seq", "fsdp"), distance))
    window_rows = jnp.concatenate(pieces, axis=0)
    return window_rows


def return_window(grad_prev, row_count):
    neighbours = grad_prev.shape[0] // row_count
    grad_total = jnp.zeros((row_count, grad_prev.shape[1]), jnp.float32)
    for distance in range(1, neighbours + 1):
        grad_block = grad_prev[
            (neighbours - distance) * row_count : (neighbours - distance + 1) * row_count
        ]
        grad_total = grad_total + shifted(
            grad_block.astype(jnp.bfloat16), ("seq", "fsdp"), -distance
        ).astype(grad_block.dtype)
    return grad_total


def forward_layer(layer_in, token_pos, layer_weights):
    (
        attn_scale,
        query_weight,
        key_weight,
        value_weight,
        query_scale,
        key_scale,
        out_weight,
        post_attn_scale,
        ffn_scale,
        gate_weight,
        up_weight,
        down_weight,
        post_ffn_scale,
    ) = layer_weights
    row_count = layer_in.shape[0]
    heads_width = out_weight.shape[0]
    head_dim = query_scale.shape[0]
    residual = layer_in.astype(jnp.float32)
    normed_b = norm_gain(residual, attn_scale).astype(jnp.bfloat16)
    query_proj = jnp.dot(normed_b, query_weight, preferred_element_type=jnp.float32).reshape(
        row_count, heads_width // head_dim, head_dim
    )
    key_proj = jnp.dot(normed_b, key_weight, preferred_element_type=jnp.float32)
    value_b = jnp.dot(normed_b, value_weight, preferred_element_type=jnp.float32).astype(
        jnp.bfloat16
    )
    query_rot, key_rot = qk_post(query_proj, key_proj, query_scale, key_scale, token_pos)
    query_b = query_rot.astype(jnp.bfloat16)
    kv_own = jnp.concatenate((key_rot.astype(jnp.bfloat16), value_b), axis=1)
    keys_all = jnp.concatenate((fetch_window(kv_own), kv_own), axis=0)
    attended, log_total = attend_forward(query_b, keys_all, token_pos)
    attended_b = attended.astype(jnp.bfloat16).reshape(row_count, heads_width)
    branch = jnp.dot(attended_b, out_weight, preferred_element_type=jnp.float32)
    mixed = post_add(residual, branch, post_attn_scale)
    ffn_in = norm_gain(mixed, ffn_scale).astype(jnp.bfloat16)
    gate_pre = jnp.dot(ffn_in, gate_weight, preferred_element_type=jnp.float32)
    up_pre = jnp.dot(ffn_in, up_weight, preferred_element_type=jnp.float32)
    activated = mlp_act(gate_pre, up_pre).astype(jnp.bfloat16)
    down_out = jnp.dot(activated, down_weight, preferred_element_type=jnp.float32)
    result = post_add(mixed, down_out, post_ffn_scale).astype(jnp.bfloat16)
    saved = (
        layer_in,
        normed_b,
        query_proj,
        key_proj,
        query_b,
        keys_all,
        log_total,
        attended_b,
        branch,
        mixed,
        ffn_in,
        gate_pre,
        up_pre,
        activated,
        down_out,
    )
    return (result, saved)


def backward_layer(upstream, saved, token_pos, layer_weights):
    (
        attn_scale,
        query_weight,
        key_weight,
        value_weight,
        query_scale,
        key_scale,
        out_weight,
        post_attn_scale,
        ffn_scale,
        gate_weight,
        up_weight,
        down_weight,
        post_ffn_scale,
    ) = layer_weights
    (
        layer_in,
        normed_b,
        query_proj,
        key_proj,
        query_b,
        keys_all,
        log_total,
        attended_b,
        branch,
        mixed,
        ffn_in,
        gate_pre,
        up_pre,
        activated,
        down_out,
    ) = saved
    row_count = layer_in.shape[0]
    heads_width = out_weight.shape[0]
    head_dim = query_scale.shape[0]
    residual = layer_in.astype(jnp.float32)
    grad_top = upstream.astype(jnp.float32)
    forward_value, backward_mapping = jax.vjp(post_add, mixed, down_out, post_ffn_scale)
    grad_mixed, grad_down, post_feedforward_gradient = backward_mapping(grad_top)
    grad_down_b = grad_down.astype(jnp.bfloat16)
    grad_act = jnp.einsum("tn,fn->tf", grad_down_b, down_weight, preferred_element_type=jnp.float32)
    forward_value, backward_mapping = jax.vjp(mlp_act, gate_pre, up_pre)
    grad_gate, grad_up = backward_mapping(grad_act)
    grad_gate_b = grad_gate.astype(jnp.bfloat16)
    grad_up_b = grad_up.astype(jnp.bfloat16)
    grad_ffn_in = jnp.einsum(
        "tn,dn->td", grad_gate_b, gate_weight, preferred_element_type=jnp.float32
    ) + jnp.einsum("tn,dn->td", grad_up_b, up_weight, preferred_element_type=jnp.float32)
    forward_value, backward_mapping = jax.vjp(norm_gain, mixed, ffn_scale)
    grad_mixed_two, grad_ffn_scale = backward_mapping(grad_ffn_in)
    grad_mixed = grad_mixed + grad_mixed_two
    forward_value, backward_mapping = jax.vjp(post_add, residual, branch, post_attn_scale)
    grad_resid, grad_branch, grad_post_attn = backward_mapping(grad_mixed)
    grad_branch_b = grad_branch.astype(jnp.bfloat16)
    grad_attended = jnp.einsum(
        "td,nd->tn", grad_branch_b, out_weight, preferred_element_type=jnp.float32
    )
    grad_attended = grad_attended.astype(jnp.bfloat16).reshape(
        row_count, heads_width // head_dim, head_dim
    )
    grad_query, grad_keys = attend_backward(grad_attended, query_b, keys_all, token_pos, log_total)
    window_len = keys_all.shape[0] - row_count
    grad_own = grad_keys[window_len:] + return_window(grad_keys[:window_len], row_count)
    forward_value, backward_mapping = jax.vjp(
        partial(qk_post, token_pos=token_pos), query_proj, key_proj, query_scale, key_scale
    )
    query_projection_gradient, key_projection_gradient, query_scale_gradient, key_scale_gradient = (
        backward_mapping((grad_query, grad_own[:, :head_dim]))
    )
    grad_query_b = query_projection_gradient.reshape(row_count, heads_width).astype(jnp.bfloat16)
    grad_key_b = key_projection_gradient.astype(jnp.bfloat16)
    grad_value_b = grad_own[:, head_dim:].astype(jnp.bfloat16)
    grad_normed = (
        jnp.einsum("tn,dn->td", grad_query_b, query_weight, preferred_element_type=jnp.float32)
        + jnp.einsum("tn,dn->td", grad_key_b, key_weight, preferred_element_type=jnp.float32)
        + jnp.einsum("tn,dn->td", grad_value_b, value_weight, preferred_element_type=jnp.float32)
    )
    forward_value, backward_mapping = jax.vjp(norm_gain, residual, attn_scale)
    grad_resid_two, grad_attn_scale = backward_mapping(grad_normed)
    grad_input = (grad_resid + grad_resid_two).astype(jnp.bfloat16)
    gain_grads = (
        grad_attn_scale,
        query_scale_gradient,
        key_scale_gradient,
        grad_post_attn,
        grad_ffn_scale,
        post_feedforward_gradient,
    )
    product_grads = (
        grad_query_b,
        grad_key_b,
        grad_value_b,
        grad_branch_b,
        grad_gate_b,
        grad_up_b,
        grad_down_b,
    )
    return (grad_input, gain_grads, product_grads)


def stack_leaves(*leaves):
    return jnp.stack(leaves)


def take_entry(entry_index, stacked):
    return lax.dynamic_index_in_dim(stacked, entry_index, 0, keepdims=False)


def regroup(grad_local, shard_count, seq_count):
    leading = grad_local.shape[0]
    grouped = grad_local.reshape(
        (shard_count, seq_count, leading // (shard_count * seq_count)) + grad_local.shape[1:]
    )
    return grouped.swapaxes(0, 1).reshape(grad_local.shape)


def regroup_columns(values, shard_count, seq_count):
    row_count, width = values.shape
    grouped = values.reshape(row_count, shard_count, seq_count, width // (shard_count * seq_count))
    return grouped.swapaxes(1, 2).reshape(row_count, width)


def body(
    hidden_in,
    cotangent,
    positions,
    attn_gain,
    w_query,
    w_key,
    w_value,
    query_gain,
    key_gain,
    w_output,
    post_attn_gain,
    ffn_gain,
    w_gate,
    w_up,
    w_down,
    post_ffn_gain,
):
    section_index = lax.axis_index("section")
    gathered = (
        lax.all_gather(attn_gain, "fsdp", axis=1, tiled=True),
        lax.all_gather(w_query, "fsdp", axis=1, tiled=True),
        lax.all_gather(w_key, "fsdp", axis=1, tiled=True),
        lax.all_gather(w_value, "fsdp", axis=1, tiled=True),
        lax.all_gather(query_gain, "fsdp", axis=1, tiled=True),
        lax.all_gather(key_gain, "fsdp", axis=1, tiled=True),
        lax.all_gather(w_output, "fsdp", axis=1, tiled=True),
        lax.all_gather(post_attn_gain, "fsdp", axis=1, tiled=True),
        lax.all_gather(ffn_gain, "fsdp", axis=1, tiled=True),
        lax.all_gather(w_gate, "fsdp", axis=1, tiled=True),
        lax.all_gather(w_up, "fsdp", axis=1, tiled=True),
        lax.all_gather(w_down, "fsdp", axis=1, tiled=True),
        lax.all_gather(post_ffn_gain, "fsdp", axis=1, tiled=True),
    )
    full_weights = [piece[0] for piece in gathered]
    layer_weights = (
        full_weights[0].astype(jnp.float32),
        full_weights[1],
        full_weights[2],
        full_weights[3],
        full_weights[4].astype(jnp.float32),
        full_weights[5].astype(jnp.float32),
        full_weights[6],
        full_weights[7].astype(jnp.float32),
        full_weights[8].astype(jnp.float32),
        full_weights[9],
        full_weights[10],
        full_weights[11],
        full_weights[12].astype(jnp.float32),
    )
    micro_count, row_count, model_width = hidden_in.shape
    received = jnp.zeros((row_count, model_width), jnp.bfloat16)
    results = []
    saved_list = []
    for tick_index in range(micro_count + 1):
        micro_index = jnp.clip(tick_index - section_index, 0, micro_count - 1)
        token_pos = lax.dynamic_index_in_dim(positions, micro_index, 0, keepdims=False)
        layer_in = jnp.where(
            section_index == 0, hidden_in[min(tick_index, micro_count - 1)], received
        )
        result, saved = forward_layer(layer_in, token_pos, layer_weights)
        results.append(result)
        saved_list.append(saved)
        if tick_index < micro_count:
            received = shifted(result, "section", 1)
    saved_stack = jax.tree.map(stack_leaves, *saved_list)
    back_recv = jnp.zeros((row_count, model_width), jnp.bfloat16)
    input_list = []
    product_list = []
    gain_total = None
    for tick_index in range(micro_count + 1):
        top_grad = (
            cotangent[tick_index] if tick_index < micro_count else jnp.zeros_like(cotangent[0])
        )
        upstream = jnp.where(section_index == 1, top_grad, back_recv)
        saved_index = jnp.clip(tick_index - 1 + 2 * section_index, 0, micro_count)
        micro_index = jnp.clip(tick_index - 1 + section_index, 0, micro_count - 1)
        saved = jax.tree.map(partial(take_entry, saved_index), saved_stack)
        token_pos = lax.dynamic_index_in_dim(positions, micro_index, 0, keepdims=False)
        grad_input, gain_grads, product_grads = backward_layer(
            upstream, saved, token_pos, layer_weights
        )
        input_list.append(grad_input)
        product_list.append(product_grads)
        gain_total = (
            gain_grads if gain_total is None else jax.tree.map(jnp.add, gain_total, gain_grads)
        )
        if tick_index < micro_count:
            back_recv = shifted(grad_input, "section", -1)
    product_stack = jax.tree.map(stack_leaves, *product_list)

    def valid_rows(stacked, start_tick):
        chosen = lax.dynamic_slice_in_dim(stacked, start_tick, micro_count, 0)
        return chosen.reshape((micro_count * row_count, -1))

    seq_count = lax.axis_size("seq")
    shard_count = lax.axis_size("fsdp")
    arrange = partial(regroup_columns, shard_count=shard_count, seq_count=seq_count)
    arrange_gain = partial(regroup, shard_count=shard_count, seq_count=seq_count)
    normed_all = arrange(valid_rows(saved_stack[1], section_index))
    attended_all = arrange(valid_rows(saved_stack[7], section_index))
    ffn_all = arrange(valid_rows(saved_stack[10], section_index))
    activated_all = arrange(valid_rows(saved_stack[13], section_index))

    def contract(left_rows, product_index):
        right_rows = valid_rows(product_stack[product_index], 1 - section_index)
        return jnp.einsum("rd,rn->dn", left_rows, right_rows, preferred_element_type=jnp.float32)

    local_grads = (
        arrange_gain(gain_total[0]),
        contract(normed_all, 0),
        contract(normed_all, 1),
        contract(normed_all, 2),
        arrange_gain(gain_total[1]),
        arrange_gain(gain_total[2]),
        contract(attended_all, 3),
        arrange_gain(gain_total[3]),
        arrange_gain(gain_total[4]),
        contract(ffn_all, 4),
        contract(ffn_all, 5),
        contract(activated_all, 6),
        arrange_gain(gain_total[5]),
    )
    pieces = (
        lax.psum_scatter(local_grads[0], ("seq", "fsdp"), scatter_dimension=0, tiled=True),
        lax.psum_scatter(local_grads[1], ("seq", "fsdp"), scatter_dimension=0, tiled=True),
        lax.psum_scatter(local_grads[2], ("seq", "fsdp"), scatter_dimension=0, tiled=True),
        lax.psum_scatter(local_grads[3], ("seq", "fsdp"), scatter_dimension=0, tiled=True),
        lax.psum_scatter(local_grads[4], ("seq", "fsdp"), scatter_dimension=0, tiled=True),
        lax.psum_scatter(local_grads[5], ("seq", "fsdp"), scatter_dimension=0, tiled=True),
        lax.psum_scatter(local_grads[6], ("seq", "fsdp"), scatter_dimension=0, tiled=True),
        lax.psum_scatter(local_grads[7], ("seq", "fsdp"), scatter_dimension=0, tiled=True),
        lax.psum_scatter(local_grads[8], ("seq", "fsdp"), scatter_dimension=0, tiled=True),
        lax.psum_scatter(local_grads[9], ("seq", "fsdp"), scatter_dimension=0, tiled=True),
        lax.psum_scatter(local_grads[10], ("seq", "fsdp"), scatter_dimension=0, tiled=True),
        lax.psum_scatter(local_grads[11], ("seq", "fsdp"), scatter_dimension=0, tiled=True),
        lax.psum_scatter(local_grads[12], ("seq", "fsdp"), scatter_dimension=0, tiled=True),
    )
    summed = (
        lax.all_gather(pieces[0].astype(jnp.bfloat16), "seq", axis=0, tiled=True).astype(
            jnp.float32
        ),
        lax.all_gather(pieces[1].astype(jnp.bfloat16), "seq", axis=0, tiled=True).astype(
            jnp.float32
        ),
        lax.all_gather(pieces[2].astype(jnp.bfloat16), "seq", axis=0, tiled=True).astype(
            jnp.float32
        ),
        lax.all_gather(pieces[3].astype(jnp.bfloat16), "seq", axis=0, tiled=True).astype(
            jnp.float32
        ),
        lax.all_gather(pieces[4].astype(jnp.bfloat16), "seq", axis=0, tiled=True).astype(
            jnp.float32
        ),
        lax.all_gather(pieces[5].astype(jnp.bfloat16), "seq", axis=0, tiled=True).astype(
            jnp.float32
        ),
        lax.all_gather(pieces[6].astype(jnp.bfloat16), "seq", axis=0, tiled=True).astype(
            jnp.float32
        ),
        lax.all_gather(pieces[7].astype(jnp.bfloat16), "seq", axis=0, tiled=True).astype(
            jnp.float32
        ),
        lax.all_gather(pieces[8].astype(jnp.bfloat16), "seq", axis=0, tiled=True).astype(
            jnp.float32
        ),
        lax.all_gather(pieces[9].astype(jnp.bfloat16), "seq", axis=0, tiled=True).astype(
            jnp.float32
        ),
        lax.all_gather(pieces[10].astype(jnp.bfloat16), "seq", axis=0, tiled=True).astype(
            jnp.float32
        ),
        lax.all_gather(pieces[11].astype(jnp.bfloat16), "seq", axis=0, tiled=True).astype(
            jnp.float32
        ),
        lax.all_gather(pieces[12].astype(jnp.bfloat16), "seq", axis=0, tiled=True).astype(
            jnp.float32
        ),
    )
    section_outputs = lax.dynamic_slice_in_dim(jnp.stack(results), section_index, micro_count, 0)[
        None
    ]
    input_grads = lax.dynamic_slice_in_dim(
        jnp.stack(input_list), 1 - section_index, micro_count, 0
    )[None]
    return (
        section_outputs,
        input_grads,
        summed[0][None],
        summed[1][None],
        summed[2][None],
        summed[3][None],
        summed[4][None],
        summed[5][None],
        summed[6][None],
        summed[7][None],
        summed[8][None],
        summed[9][None],
        summed[10][None],
        summed[11][None],
        summed[12][None],
    )


def solution(mesh):
    in_specs = (
        P(None, ("seq", "fsdp"), None),
        P(None, ("seq", "fsdp"), None),
        P(None, ("seq", "fsdp")),
        P("section", "fsdp"),
        P("section", "fsdp", None),
        P("section", "fsdp", None),
        P("section", "fsdp", None),
        P("section", "fsdp"),
        P("section", "fsdp"),
        P("section", "fsdp", None),
        P("section", "fsdp"),
        P("section", "fsdp"),
        P("section", "fsdp", None),
        P("section", "fsdp", None),
        P("section", "fsdp", None),
        P("section", "fsdp"),
    )
    out_specs = (
        P("section", None, ("seq", "fsdp"), None),
        P("section", None, ("seq", "fsdp"), None),
        P("section", "fsdp"),
        P("section", "fsdp", None),
        P("section", "fsdp", None),
        P("section", "fsdp", None),
        P("section", "fsdp"),
        P("section", "fsdp"),
        P("section", "fsdp", None),
        P("section", "fsdp"),
        P("section", "fsdp"),
        P("section", "fsdp", None),
        P("section", "fsdp", None),
        P("section", "fsdp", None),
        P("section", "fsdp"),
    )
    return jax.shard_map(body, mesh=mesh, in_specs=in_specs, out_specs=out_specs, check_vma=False)
```

profile of v0, /device:TPU:0, one launch (start us, length us, event | category | flops | bytes accessed | tf_op | source)
XLA Modules:
  0.0 1153.4 jit_solution(1479318327881456398)
XLA Ops:
  13.5 11.7 %all-reduce.31 = (bf16[640]{0:T(1024)(128)(2,1)S(1)}, bf16[640]{0:T(1024)(128)(2,1)S(1)}, bf16[640]{0:T(1024)(128)(2,1)S(1)}, bf16[256]{0:T(256)(128)(2,1)S(1)},...) all-reduce(bf16[640]{0:T(1024)(128)(2,1)S(1)} %dynamic-update-slice, ...), channel_id=1, replica_groups=mesh['section'=2,'seq'=4,'fsdp'=4] {'fsdp'}, use_global_device_ids=true, to_apply=%add.16 | all-reduce | flops 3072 | bytes 12288
  25.3 9.1 all_gather.79
  34.5 11.1 all_gather.81
  47.2 2.0 collective-permute-start.7
  49.2 3.8 collective-permute-start.6
  53.0 3.6 collective-permute-start.5
  56.6 3.7 collective-permute-start.4
  60.3 3.0 collective-permute-start
  66.5 1.9 collective-permute-done.1
  68.4 7.2 collective-permute-start.2
  77.5 5.0 collective-permute-start.3
  84.6 1.9 fusion.58
  92.6 25.8 %all-gather.10.cloned.1.call-done = bf16[1,640,2048]{2,1,0:T(8,128)(2,1)} async-done(((bf16[1,160,2048]{2,1,0:T(8,128)(2,1)}), bf16[1,640,2048]{2,1,0:T(8,128)(2,1)}) %all-gather.10.cloned.1.call-update) | async-done | bytes 2621456 | tf_op jit(solution)/shard_map/all_gather | solution.py:351
  118.4 2.3 fusion.34
  120.7 39.0 %all-gather.12.cloned.1.call-done = bf16[1,640,2048]{2,1,0:T(8,128)(2,1)} async-done(((bf16[1,160,2048]{2,1,0:T(8,128)(2,1)}), bf16[1,640,2048]{2,1,0:T(8,128)(2,1)}) %all-gather.12.cloned.1.call-update) | async-done | bytes 2621456 | tf_op jit(solution)/shard_map/all_gather | solution.py:352
  159.7 3.2 fusion.155
  162.9 38.2 %all-gather.14.cloned.1.call-done = bf16[1,2048,640]{2,1,0:T(8,128)(2,1)} async-done(((bf16[1,512,640]{2,1,0:T(8,128)(2,1)}), bf16[1,2048,640]{2,1,0:T(8,128)(2,1)}) %all-gather.14.cloned.1.call-update) | async-done | bytes 2621456 | tf_op jit(solution)/shard_map/all_gather | solution.py:353
  201.1 2.4 multiply_reduce_fusion.12
  203.7 1.9 collective-permute-start.8
  208.8 4.0 collective-permute-start.16
  212.8 2.5 collective-permute-start.15
  215.3 5.2 collective-permute-start.14
  220.4 3.4 collective-permute-start.13
  223.9 2.8 collective-permute-start.9
  232.2 6.0 collective-permute-start.11
  238.2 2.2 collective-permute-done.11
  240.4 16.6 %collective-permute-start.12 = (bf16[64,512]{1,0:T(8,128)(2,1)}, bf16[64,512]{1,0:T(8,128)(2,1)S(1)}, u32[]{:S(2)}, u32[]{:S(2)}) collective-permute-start(bf16[64,512]{1,0:T(8,128)(2,1)} %pad_maximum_fusion.12), channel_id=1, source_target_pairs={{0,5},{1,6},{2,7},{3,8},{4,9},{5,10},{6,11},{7,12},{8,13},{9,14},{... | collective-permute-start | bytes 196616 | tf_op jit(solution)/shard_map/ppermute | solution.py:19
  274.5 5.0 collective-permute-start.25
  279.4 6.7 collective-permute-start.24
  286.2 1.9 collective-permute-start.23
  288.1 1.9 collective-permute-start.22
  290.0 1.9 collective-permute-start.18
  300.7 2.0 constant_dynamic-slice_fusion
  315.9 2.2 collective-permute-done.20
  318.1 5.8 collective-permute-start.21
  324.0 2.2 collective-permute-done.21
  355.8 12.1 %collective-permute-done.33 = bf16[64,512]{1,0:T(8,128)(2,1)S(1)} collective-permute-done((bf16[64,512]{1,0:T(8,128)(2,1)S(1)}, bf16[64,512]{1,0:T(8,128)(2,1)S(1)}, u32[]{:S(2)}, u32[]{:S(2)}) %collective-permute-start.33) | collective-permute-done | bytes 65568 | tf_op jit(solution)/shard_map/ppermute | solution.py:19
  370.6 4.4 collective-permute-done.28
  400.0 1.9 collective-permute-done.42
  406.2 2.9 collective-permute-done.38
  409.1 3.2 collective-permute-done.37
  412.3 2.3 collective-permute-done.36
  439.0 6.2 collective-permute-done.51
  449.3 3.3 collective-permute-done.46
  459.5 2.0 fusion.480
  464.0 2.0 fusion.477
  468.3 3.2 fusion.483
  473.4 3.1 fusion.482
  476.6 3.2 fusion.481
  486.8 77.7 %all-reduce.30 = (bf16[640]{0:T(1024)(128)(2,1)S(1)}, bf16[256]{0:T(256)(128)(2,1)S(1)}, bf16[256]{0:T(256)(128)(2,1)S(1)}, bf16[640]{0:T(1024)(128)(2,1)S(1)}, ...) all-reduce(f32[640]{0:T(1024)S(1)} %reshape.1494, ...), channel_id=2, replica_groups=mesh['section'=2,'seq'=4,'fsdp'=4] {'seq','fsdp'}, use_global_device_ids=true, to_apply=%region_66.67.clone | all-reduce | flops 3072 | bytes 18432
  566.2 8.3 all-reduce.32
  579.3 33.0 %reduce-scatter.12.cloned.1.call-done = f32[40,256]{1,0:T(8,128)} async-done(((f32[640,256]{1,0:T(8,128)}), f32[40,256]{1,0:T(8,128)}) %reduce-scatter.12.cloned.1.call-update) | async-done | bytes 40976 | tf_op jit(solution)/shard_map/reduce_scatter | solution.py:449
  613.0 13.5 %all_gather.93 = bf16[160,256]{1,0:T(8,128)(2,1)S(1)} all-gather(bf16[40,256]{1,0:T(8,128)(2,1)S(1)} %convert_element_type.621), channel_id=1, replica_groups=mesh['section'=2,'seq'=4,'fsdp'=4] {'seq'}, dimensions={0}, use_global_device_ids=true | all-gather | bytes 102400 | tf_op jit(solution)/shard_map/all_gather | solution.py:467
  626.5 13.4 %all_gather.94 = bf16[160,256]{1,0:T(8,128)(2,1)S(1)} all-gather(bf16[40,256]{1,0:T(8,128)(2,1)S(1)} %convert_element_type.622), channel_id=1, replica_groups=mesh['section'=2,'seq'=4,'fsdp'=4] {'seq'}, dimensions={0}, use_global_device_ids=true | all-gather | bytes 102400 | tf_op jit(solution)/shard_map/all_gather | solution.py:470
  641.2 52.3 %reduce-scatter.14.cloned.1.call-done = f32[64,640]{1,0:T(8,128)} async-done(((f32[1024,640]{1,0:T(8,128)}), f32[64,640]{1,0:T(8,128)}) %reduce-scatter.14.cloned.1.call-update) | async-done | bytes 163856 | tf_op jit(solution)/shard_map/reduce_scatter | solution.py:452
  694.5 15.0 %all_gather.97 = bf16[256,640]{1,0:T(8,128)(2,1)S(1)} all-gather(bf16[64,640]{1,0:T(8,128)(2,1)S(1)} %convert_element_type.625), channel_id=1, replica_groups=mesh['section'=2,'seq'=4,'fsdp'=4] {'seq'}, dimensions={0}, use_global_device_ids=true | all-gather | bytes 409600 | tf_op jit(solution)/shard_map/all_gather | solution.py:479
  710.3 64.9 %reduce-scatter.8.cloned.1.call-done = f32[40,1024]{1,0:T(8,128)} async-done(((f32[640,1024]{1,0:T(8,128)}), f32[40,1024]{1,0:T(8,128)}) %reduce-scatter.8.cloned.1.call-update) | async-done | bytes 163856 | tf_op jit(solution)/shard_map/reduce_scatter | solution.py:447
  776.2 14.9 %all_gather.92 = bf16[160,1024]{1,0:T(8,128)(2,1)S(1)} all-gather(bf16[40,1024]{1,0:T(8,128)(2,1)S(1)} %convert_element_type.620), channel_id=1, replica_groups=mesh['section'=2,'seq'=4,'fsdp'=4] {'seq'}, dimensions={0}, use_global_device_ids=true | all-gather | bytes 409600 | tf_op jit(solution)/shard_map/all_gather | solution.py:464
  792.0 97.8 %reduce-scatter.20.cloned.1.call-done = f32[128,640]{1,0:T(8,128)} async-done(((f32[2048,640]{1,0:T(8,128)}), f32[128,640]{1,0:T(8,128)}) %reduce-scatter.20.cloned.1.call-update) | async-done | bytes 327696 | tf_op jit(solution)/shard_map/reduce_scatter | solution.py:457
  890.7 117.8 %reduce-scatter.18.cloned.1.call-done = f32[40,2048]{1,0:T(8,128)} async-done(((f32[640,2048]{1,0:T(8,128)}), f32[40,2048]{1,0:T(8,128)}) %reduce-scatter.18.cloned.1.call-update) | async-done | bytes 327696 | tf_op jit(solution)/shard_map/reduce_scatter | solution.py:456
  1009.5 20.1 %all_gather.102 = bf16[512,640]{1,0:T(8,128)(2,1)S(1)} all-gather(bf16[128,640]{1,0:T(8,128)(2,1)S(1)} %convert_element_type.630), channel_id=1, replica_groups=mesh['section'=2,'seq'=4,'fsdp'=4] {'seq'}, dimensions={0}, use_global_device_ids=true | all-gather | bytes 819200 | tf_op jit(solution)/shard_map/all_gather | solution.py:494
  1029.6 23.1 %all_gather.101 = bf16[160,2048]{1,0:T(8,128)(2,1)S(1)} all-gather(bf16[40,2048]{1,0:T(8,128)(2,1)S(1)} %convert_element_type.629), channel_id=1, replica_groups=mesh['section'=2,'seq'=4,'fsdp'=4] {'seq'}, dimensions={0}, use_global_device_ids=true | all-gather | bytes 819200 | tf_op jit(solution)/shard_map/all_gather | solution.py:491
  1055.0 72.9 %reduce-scatter.16.cloned.1.call-done = f32[40,2048]{1,0:T(8,128)} async-done(((f32[640,2048]{1,0:T(8,128)}), f32[40,2048]{1,0:T(8,128)}) %reduce-scatter.16.cloned.1.call-update) | async-done | bytes 327696 | tf_op jit(solution)/shard_map/reduce_scatter | solution.py:455
  1129.0 16.2 %all_gather.100 = bf16[160,2048]{1,0:T(8,128)(2,1)S(1)} all-gather(bf16[40,2048]{1,0:T(8,128)(2,1)S(1)} %convert_element_type.628), channel_id=1, replica_groups=mesh['section'=2,'seq'=4,'fsdp'=4] {'seq'}, dimensions={0}, use_global_device_ids=true | all-gather | bytes 819200 | tf_op jit(solution)/shard_map/all_gather | solution.py:488
  (906 shorter events, 190.8 us)
Async XLA Ops:
  7.3 77.3 %all-gather.6.cloned.1.call-start = ((), (), s32[]{:S(2)}) async-start(), calls=%async_computation.7 | async-start | bytes 1638400 | tf_op jit(solution)/shard_map/all_gather | solution.py:343
  8.0 81.2 %all-gather.8.cloned.1.call-start = ((), (), s32[]{:S(2)}) async-start(), calls=%async_computation.8 | async-start | bytes 1638400 | tf_op jit(solution)/shard_map/all_gather | solution.py:348
  8.8 109.6 %all-gather.10.cloned.1.call-start = ((), (), s32[]{:S(2)}) async-start(), calls=%async_computation.9 | async-start | bytes 3276800 | tf_op jit(solution)/shard_map/all_gather | solution.py:351
  9.5 150.2 %all-gather.12.cloned.1.call-start = ((), (), s32[]{:S(2)}) async-start(), calls=%async_computation.10 | async-start | bytes 3276800 | tf_op jit(solution)/shard_map/all_gather | solution.py:352
  10.1 191.0 %all-gather.14.cloned.1.call-start = ((), (), s32[]{:S(2)}) async-start(), calls=%async_computation.11 | async-start | bytes 3276800 | tf_op jit(solution)/shard_map/all_gather | solution.py:353
  47.2 37.3 %collective-permute-start.7 = (bf16[64,512]{1,0:T(8,128)(2,1)S(1)}, bf16[64,512]{1,0:T(8,128)(2,1)S(1)}, u32[]{:S(2)}, u32[]{:S(2)}) collective-permute-start(bf16[64,512]{1,0:T(8,128)(2,1)S(1)} %pad_maximum_fusion.11), channel_id=1, source_target_pairs={{0,1},{1,2},{2,3},{3,4},{4,5},{5,6},{6,7},{7,8},{8,9},{9,10},{10,1... | collective-permute-start | bytes 196616 | tf_op jit(solution)/shard_map/ppermute | solution.py:19
  49.2 35.3 %collective-permute-start.6 = (bf16[64,512]{1,0:T(8,128)(2,1)S(1)}, bf16[64,512]{1,0:T(8,128)(2,1)S(1)}, u32[]{:S(2)}, u32[]{:S(2)}) collective-permute-start(bf16[64,512]{1,0:T(8,128)(2,1)S(1)} %pad_maximum_fusion.11), channel_id=1, source_target_pairs={{0,2},{1,3},{2,4},{3,5},{4,6},{5,7},{6,8},{7,9},{8,10},{9,11},{10,... | collective-permute-start | bytes 196616 | tf_op jit(solution)/shard_map/ppermute | solution.py:19
  53.0 31.4 %collective-permute-start.5 = (bf16[64,512]{1,0:T(8,128)(2,1)S(1)}, bf16[64,512]{1,0:T(8,128)(2,1)S(1)}, u32[]{:S(2)}, u32[]{:S(2)}) collective-permute-start(bf16[64,512]{1,0:T(8,128)(2,1)S(1)} %pad_maximum_fusion.11), channel_id=1, source_target_pairs={{0,3},{1,4},{2,5},{3,6},{4,7},{5,8},{6,9},{7,10},{8,11},{9,12},{10... | collective-permute-start | bytes 196616 | tf_op jit(solution)/shard_map/ppermute | solution.py:19
  56.6 27.8 %collective-permute-start.4 = (bf16[64,512]{1,0:T(8,128)(2,1)S(1)}, bf16[64,512]{1,0:T(8,128)(2,1)S(1)}, u32[]{:S(2)}, u32[]{:S(2)}) collective-permute-start(bf16[64,512]{1,0:T(8,128)(2,1)S(1)} %pad_maximum_fusion.11), channel_id=1, source_target_pairs={{0,4},{1,5},{2,6},{3,7},{4,8},{5,9},{6,10},{7,11},{8,12},{9,13},{1... | collective-permute-start | bytes 196616 | tf_op jit(solution)/shard_map/ppermute | solution.py:19
  60.3 4.9 collective-permute-start
  63.4 515.1 %reduce-scatter.10.cloned.1.call-start = ((), (), s32[]{:S(2)}) async-start(), calls=%async_computation.13 | async-start | bytes 696320 | tf_op jit(solution)/shard_map/reduce_scatter | solution.py:448
  65.2 3.2 collective-permute-start.1
  68.4 9.1 collective-permute-start.2
  77.5 6.9 collective-permute-start.3
  203.7 2.8 collective-permute-start.8
  208.8 50.8 %collective-permute-start.16 = (bf16[64,512]{1,0:T(8,128)(2,1)}, bf16[64,512]{1,0:T(8,128)(2,1)}, u32[]{:S(2)}, u32[]{:S(2)}) collective-permute-start(bf16[64,512]{1,0:T(8,128)(2,1)} %pad_maximum_fusion.12), channel_id=1, source_target_pairs={{0,1},{1,2},{2,3},{3,4},{4,5},{5,6},{6,7},{7,8},{8,9},{9,10},{10,1... | collective-permute-start | bytes 196616 | tf_op jit(solution)/shard_map/ppermute | solution.py:19
  212.8 46.0 %collective-permute-start.15 = (bf16[64,512]{1,0:T(8,128)(2,1)}, bf16[64,512]{1,0:T(8,128)(2,1)}, u32[]{:S(2)}, u32[]{:S(2)}) collective-permute-start(bf16[64,512]{1,0:T(8,128)(2,1)} %pad_maximum_fusion.12), channel_id=1, source_target_pairs={{0,2},{1,3},{2,4},{3,5},{4,6},{5,7},{6,8},{7,9},{8,10},{9,11},{10,... | collective-permute-start | bytes 196616 | tf_op jit(solution)/shard_map/ppermute | solution.py:19
  215.3 42.7 %collective-permute-start.14 = (bf16[64,512]{1,0:T(8,128)(2,1)}, bf16[64,512]{1,0:T(8,128)(2,1)}, u32[]{:S(2)}, u32[]{:S(2)}) collective-permute-start(bf16[64,512]{1,0:T(8,128)(2,1)} %pad_maximum_fusion.12), channel_id=1, source_target_pairs={{0,3},{1,4},{2,5},{3,6},{4,7},{5,8},{6,9},{7,10},{8,11},{9,12},{10... | collective-permute-start | bytes 196616 | tf_op jit(solution)/shard_map/ppermute | solution.py:19
  220.4 36.6 %collective-permute-start.13 = (bf16[64,512]{1,0:T(8,128)(2,1)}, bf16[64,512]{1,0:T(8,128)(2,1)}, u32[]{:S(2)}, u32[]{:S(2)}) collective-permute-start(bf16[64,512]{1,0:T(8,128)(2,1)} %pad_maximum_fusion.12), channel_id=1, source_target_pairs={{0,4},{1,5},{2,6},{3,7},{4,8},{5,9},{6,10},{7,11},{8,12},{9,13},{1... | collective-permute-start | bytes 196616 | tf_op jit(solution)/shard_map/ppermute | solution.py:19
  223.9 4.8 collective-permute-start.9
  228.7 3.5 collective-permute-start.10
  232.2 8.2 collective-permute-start.11
  240.4 16.6 %collective-permute-start.12 = (bf16[64,512]{1,0:T(8,128)(2,1)}, bf16[64,512]{1,0:T(8,128)(2,1)S(1)}, u32[]{:S(2)}, u32[]{:S(2)}) collective-permute-start(bf16[64,512]{1,0:T(8,128)(2,1)} %pad_maximum_fusion.12), channel_id=1, source_target_pairs={{0,5},{1,6},{2,7},{3,8},{4,9},{5,10},{6,11},{7,12},{8,13},{9,14},{... | collective-permute-start | bytes 196616 | tf_op jit(solution)/shard_map/ppermute | solution.py:19
  269.4 2.2 collective-permute-start.17
  274.5 54.2 %collective-permute-start.25 = (bf16[64,512]{1,0:T(8,128)(2,1)}, bf16[64,512]{1,0:T(8,128)(2,1)}, u32[]{:S(2)}, u32[]{:S(2)}) collective-permute-start(bf16[64,512]{1,0:T(8,128)(2,1)} %pad_maximum_fusion.13), channel_id=1, source_target_pairs={{0,1},{1,2},{2,3},{3,4},{4,5},{5,6},{6,7},{7,8},{8,9},{9,10},{10,1... | collective-permute-start | bytes 196616 | tf_op jit(solution)/shard_map/ppermute | solution.py:19
  279.4 48.4 %collective-permute-start.24 = (bf16[64,512]{1,0:T(8,128)(2,1)}, bf16[64,512]{1,0:T(8,128)(2,1)}, u32[]{:S(2)}, u32[]{:S(2)}) collective-permute-start(bf16[64,512]{1,0:T(8,128)(2,1)} %pad_maximum_fusion.13), channel_id=1, source_target_pairs={{0,2},{1,3},{2,4},{3,5},{4,6},{5,7},{6,8},{7,9},{8,10},{9,11},{10,... | collective-permute-start | bytes 196616 | tf_op jit(solution)/shard_map/ppermute | solution.py:19
  286.2 40.9 %collective-permute-start.23 = (bf16[64,512]{1,0:T(8,128)(2,1)}, bf16[64,512]{1,0:T(8,128)(2,1)}, u32[]{:S(2)}, u32[]{:S(2)}) collective-permute-start(bf16[64,512]{1,0:T(8,128)(2,1)} %pad_maximum_fusion.13), channel_id=1, source_target_pairs={{0,3},{1,4},{2,5},{3,6},{4,7},{5,8},{6,9},{7,10},{8,11},{9,12},{10... | collective-permute-start | bytes 196616 | tf_op jit(solution)/shard_map/ppermute | solution.py:19
  288.1 38.1 %collective-permute-start.22 = (bf16[64,512]{1,0:T(8,128)(2,1)}, bf16[64,512]{1,0:T(8,128)(2,1)}, u32[]{:S(2)}, u32[]{:S(2)}) collective-permute-start(bf16[64,512]{1,0:T(8,128)(2,1)} %pad_maximum_fusion.13), channel_id=1, source_target_pairs={{0,4},{1,5},{2,6},{3,7},{4,8},{5,9},{6,10},{7,11},{8,12},{9,13},{1... | collective-permute-start | bytes 196616 | tf_op jit(solution)/shard_map/ppermute | solution.py:19
  290.0 21.0 %collective-permute-start.18 = (bf16[64,512]{1,0:T(8,128)(2,1)}, bf16[64,512]{1,0:T(8,128)(2,1)}, u32[]{:S(2)}, u32[]{:S(2)}) collective-permute-start(bf16[64,512]{1,0:T(8,128)(2,1)} %pad_maximum_fusion.13), channel_id=1, source_target_pairs={{0,8},{1,9},{2,10},{3,11},{4,12},{5,13},{6,14},{7,15},{16,24},{17,... | collective-permute-start | bytes 196616 | tf_op jit(solution)/shard_map/ppermute | solution.py:19
  311.0 3.5 collective-permute-start.19
  314.5 3.6 collective-permute-start.20
  318.1 8.0 collective-permute-start.21
  347.9 6.6 collective-permute-start.26
  349.3 18.7 %collective-permute-start.33 = (bf16[64,512]{1,0:T(8,128)(2,1)S(1)}, bf16[64,512]{1,0:T(8,128)(2,1)S(1)}, u32[]{:S(2)}, u32[]{:S(2)}) collective-permute-start(bf16[64,512]{1,0:T(8,128)(2,1)S(1)} %get-tuple-element.130), channel_id=1, source_target_pairs={{8,0},{9,1},{10,2},{11,3},{12,4},{13,5},{14,6},{15,7},{24,16},{25,... | collective-permute-start | bytes 196616 | tf_op jit(solution)/shard_map/ppermute | solution.py:19
  350.6 18.6 %collective-permute-start.32 = (bf16[64,512]{1,0:T(8,128)(2,1)S(1)}, bf16[64,512]{1,0:T(8,128)(2,1)S(1)}, u32[]{:S(2)}, u32[]{:S(2)}) collective-permute-start(bf16[64,512]{1,0:T(8,128)(2,1)S(1)} %get-tuple-element.131), channel_id=1, source_target_pairs={{7,0},{8,1},{9,2},{10,3},{11,4},{12,5},{13,6},{14,7},{15,8},{23,16... | collective-permute-start | bytes 196616 | tf_op jit(solution)/shard_map/ppermute | solution.py:19
  351.9 18.7 %collective-permute-start.31 = (bf16[64,512]{1,0:T(8,128)(2,1)S(1)}, bf16[64,512]{1,0:T(8,128)(2,1)S(1)}, u32[]{:S(2)}, u32[]{:S(2)}) collective-permute-start(bf16[64,512]{1,0:T(8,128)(2,1)S(1)} %get-tuple-element.132), channel_id=1, source_target_pairs={{6,0},{7,1},{8,2},{9,3},{10,4},{11,5},{12,6},{13,7},{14,8},{15,9},... | collective-permute-start | bytes 196616 | tf_op jit(solution)/shard_map/ppermute | solution.py:19
  353.2 17.4 %collective-permute-start.30 = (bf16[64,512]{1,0:T(8,128)(2,1)S(1)}, bf16[64,512]{1,0:T(8,128)(2,1)S(1)}, u32[]{:S(2)}, u32[]{:S(2)}) collective-permute-start(bf16[64,512]{1,0:T(8,128)(2,1)S(1)} %get-tuple-element.133), channel_id=1, source_target_pairs={{5,0},{6,1},{7,2},{8,3},{9,4},{10,5},{11,6},{12,7},{13,8},{14,9},{... | collective-permute-start | bytes 196616 | tf_op jit(solution)/shard_map/ppermute | solution.py:19
  354.5 16.1 %collective-permute-start.29 = (bf16[64,512]{1,0:T(8,128)(2,1)S(1)}, bf16[64,512]{1,0:T(8,128)(2,1)S(1)}, u32[]{:S(2)}, u32[]{:S(2)}) collective-permute-start(bf16[64,512]{1,0:T(8,128)(2,1)S(1)} %get-tuple-element.134), channel_id=1, source_target_pairs={{4,0},{5,1},{6,2},{7,3},{8,4},{9,5},{10,6},{11,7},{12,8},{13,9},{1... | collective-permute-start | bytes 196616 | tf_op jit(solution)/shard_map/ppermute | solution.py:19
  368.0 7.1 collective-permute-start.28
  369.3 6.5 collective-permute-start.27
  381.0 3.2 collective-permute-start.34
  392.2 6.5 collective-permute-start.35
  393.5 8.4 collective-permute-start.42
  394.8 8.4 collective-permute-start.41
  396.1 8.8 collective-permute-start.40
  397.4 8.7 collective-permute-start.39
  398.7 10.4 collective-permute-start.38
  401.9 10.4 collective-permute-start.37
  403.2 11.4 collective-permute-start.36
  418.7 3.2 collective-permute-start.43
  430.6 7.1 collective-permute-start.44
  431.9 13.3 %collective-permute-start.51 = (bf16[64,512]{1,0:T(8,128)(2,1)S(1)}, bf16[64,512]{1,0:T(8,128)(2,1)S(1)}, u32[]{:S(2)}, u32[]{:S(2)}) collective-permute-start(bf16[64,512]{1,0:T(8,128)(2,1)S(1)} %get-tuple-element.114), channel_id=1, source_target_pairs={{8,0},{9,1},{10,2},{11,3},{12,4},{13,5},{14,6},{15,7},{24,16},{25,... | collective-permute-start | bytes 196616 | tf_op jit(solution)/shard_map/ppermute | solution.py:19
  433.2 13.3 %collective-permute-start.50 = (bf16[64,512]{1,0:T(8,128)(2,1)S(1)}, bf16[64,512]{1,0:T(8,128)(2,1)S(1)}, u32[]{:S(2)}, u32[]{:S(2)}) collective-permute-start(bf16[64,512]{1,0:T(8,128)(2,1)S(1)} %get-tuple-element.115), channel_id=1, source_target_pairs={{7,0},{8,1},{9,2},{10,3},{11,4},{12,5},{13,6},{14,7},{15,8},{23,16... | collective-permute-start | bytes 196616 | tf_op jit(solution)/shard_map/ppermute | solution.py:19
  435.1 14.2 %collective-permute-start.49 = (bf16[64,512]{1,0:T(8,128)(2,1)}, bf16[64,512]{1,0:T(8,128)(2,1)}, u32[]{:S(2)}, u32[]{:S(2)}) collective-permute-start(bf16[64,512]{1,0:T(8,128)(2,1)} %get-tuple-element.116), channel_id=1, source_target_pairs={{6,0},{7,1},{8,2},{9,3},{10,4},{11,5},{12,6},{13,7},{14,8},{15,9},... | collective-permute-start | bytes 196616 | tf_op jit(solution)/shard_map/ppermute | solution.py:19
  436.4 12.9 %collective-permute-start.48 = (bf16[64,512]{1,0:T(8,128)(2,1)}, bf16[64,512]{1,0:T(8,128)(2,1)}, u32[]{:S(2)}, u32[]{:S(2)}) collective-permute-start(bf16[64,512]{1,0:T(8,128)(2,1)} %get-tuple-element.117), channel_id=1, source_target_pairs={{5,0},{6,1},{7,2},{8,3},{9,4},{10,5},{11,6},{12,7},{13,8},{14,9},{... | collective-permute-start | bytes 196616 | tf_op jit(solution)/shard_map/ppermute | solution.py:19
  437.7 11.6 %collective-permute-start.47 = (bf16[64,512]{1,0:T(8,128)(2,1)}, bf16[64,512]{1,0:T(8,128)(2,1)}, u32[]{:S(2)}, u32[]{:S(2)}) collective-permute-start(bf16[64,512]{1,0:T(8,128)(2,1)} %get-tuple-element.118), channel_id=1, source_target_pairs={{4,0},{5,1},{6,2},{7,3},{8,4},{9,5},{10,6},{11,7},{12,8},{13,9},{1... | collective-permute-start | bytes 196616 | tf_op jit(solution)/shard_map/ppermute | solution.py:19
  445.3 7.4 collective-permute-start.46
  446.6 6.8 collective-permute-start.45
  456.2 156.0 %reduce-scatter.12.cloned.1.call-start = ((), (), s32[]{:S(2)}) async-start(), calls=%async_computation.14 | async-start | bytes 696320 | tf_op jit(solution)/shard_map/reduce_scatter | solution.py:449
  457.4 236.2 %reduce-scatter.14.cloned.1.call-start = ((), (), s32[]{:S(2)}) async-start(), calls=%async_computation.15 | async-start | bytes 2785280 | tf_op jit(solution)/shard_map/reduce_scatter | solution.py:452
  461.5 313.7 %reduce-scatter.8.cloned.1.call-start = ((), (), s32[]{:S(2)}) async-start(), calls=%async_computation.12 | async-start | bytes 2785280 | tf_op jit(solution)/shard_map/reduce_scatter | solution.py:447
  466.1 423.7 %reduce-scatter.20.cloned.1.call-start = ((), (), s32[]{:S(2)}) async-start(), calls=%async_computation.18 | async-start | bytes 5570560 | tf_op jit(solution)/shard_map/reduce_scatter | solution.py:457
  471.5 537.0 %reduce-scatter.18.cloned.1.call-start = ((), (), s32[]{:S(2)}) async-start(), calls=%async_computation.17 | async-start | bytes 5570560 | tf_op jit(solution)/shard_map/reduce_scatter | solution.py:456
  476.6 651.4 %reduce-scatter.16.cloned.1.call-start = ((), (), s32[]{:S(2)}) async-start(), calls=%async_computation.16 | async-start | bytes 5570560 | tf_op jit(solution)/shard_map/reduce_scatter | solution.py:455
  (212 other events, 3493.6 us)
Sparse Core Ops, SparseCore 0:
  10.0 33.3 all-gather.5
  45.2 30.1 all-gather.7
  77.3 41.0 all-gather.9
  120.0 39.6 all-gather.11
  161.4 39.6 all-gather.13
  456.3 79.6 reduce-scatter.9
  538.9 73.2 reduce-scatter.11
  614.5 78.9 reduce-scatter.13
  695.9 79.3 reduce-scatter.7
  777.4 112.2 reduce-scatter.19
  892.0 116.4 reduce-scatter.17
  1010.7 117.2 reduce-scatter.15
where the time goes:
time: 1160 us; the launch traced here: 1150 us
  waiting for transfers between devices  604 us (52%)
  blocking collectives  234 us (20%)
  starting transfers between devices  135 us (12%)
  matrix products  59.4 us (5%)
  other arithmetic  53.6 us (5%)
  local copies, waits for them, and re-layouts  44.8 us (4%)
  between operations  22.6 us (2%)
    ppermute x52, starting transfers between devices, shifted(): return lax.ppermute(shard, axis, pairs)  135 us
    reduce_scatter x1, waiting for transfers between devices, body(): lax.psum_scatter(local_grads[10], ('seq', 'fsdp'), scatter_dimension=0, t...  118 us
    unnamed x3, blocking collectives  97.8 us
    reduce_scatter x1, waiting for transfers between devices, body(): lax.psum_scatter(local_grads[11], ('seq', 'fsdp'), scatter_dimension=0, t...  97.8 us
    reduce_scatter x1, waiting for transfers between devices, body(): lax.psum_scatter(local_grads[9], ('seq', 'fsdp'), scatter_dimension=0, ti...  72.9 us
    reduce_scatter x1, waiting for transfers between devices, body(): lax.psum_scatter(local_grads[1], ('seq', 'fsdp'), scatter_dimension=0, ti...  64.9 us
    ppermute x52, waiting for transfers between devices, shifted(): return lax.ppermute(shard, axis, pairs)  59.1 us
    reduce_scatter x1, waiting for transfers between devices, body(): lax.psum_scatter(local_grads[6], ('seq', 'fsdp'), scatter_dimension=0, ti...  52.3 us
  transfers between devices with their start and end apart: 64, of which 34 were waited for; matrix products, arithmetic and copies ran while one was open for 7% of the time, Pallas kernels for 0%

commit v1 on v0

v1 whole, which is shorter than its diff:
```python
from functools import partial

import jax
import jax.numpy as jnp
import numpy as np
from jax import lax
from jax.sharding import PartitionSpec as P

WIN = 512
EPSILON = 1e-06
ROPE_BASE = 10000.0
NEG_LARGE = -1e30
AXES = ("section", "seq", "fsdp")
BF = jnp.bfloat16
F32 = jnp.float32


def dot(left, right, spec):
    return jnp.einsum(spec, left, right, preferred_element_type=F32)


def inverse_rms(values):
    return lax.rsqrt(jnp.mean(values * values, axis=-1, keepdims=True) + EPSILON)


def norm_back(values, scale, gain, grad):
    weighted = grad * gain
    inner = jnp.mean(values * weighted, axis=-1, keepdims=True)
    return scale * weighted - values * (scale * scale * scale * inner)


def gain_back(values, scale, grad):
    return jnp.sum((values * scale * grad).reshape(-1, values.shape[-1]), axis=0)


def rope_tables(token_pos, head_dim):
    half = head_dim // 2
    frequency = ROPE_BASE ** (-2.0 * jnp.arange(half, dtype=F32) / head_dim)
    angles = token_pos.astype(F32)[:, None] * frequency[None, :]
    return jnp.cos(angles), jnp.sin(angles)


def rotate(values, cosine, sine):
    half = values.shape[-1] // 2
    first, second = values[..., :half], values[..., half:]
    return jnp.concatenate((first * cosine - second * sine, second * cosine + first * sine), axis=-1)


class Halo:
    def __init__(self, sizes, section, seq, fsdp, rows):
        self.sizes, self.seq, self.fsdp, self.rows = sizes, seq, fsdp, rows
        self.section = section
        self.planes = WIN // (sizes["fsdp"] * rows)
        assert self.planes == 2 and self.planes * sizes["fsdp"] * rows == WIN

    def index(self, section, seq, fsdp):
        return (section * self.sizes["seq"] + seq) * self.sizes["fsdp"] + fsdp

    def along(self, array, section, by):
        pairs = [
            (self.index(section, z, f), self.index(section, z + by, f))
            for z in range(self.sizes["seq"])
            for f in range(self.sizes["fsdp"])
            if 0 <= z + by < self.sizes["seq"]
        ]
        return lax.ppermute(array, AXES, pairs)

    def across(self, array, section, flip):
        pairs = [
            (self.index(section, z, f), self.index(section, z, f ^ flip))
            for z in range(self.sizes["seq"])
            for f in range(self.sizes["fsdp"])
        ]
        return lax.ppermute(array, AXES, pairs)

    def starts(self):
        count = self.sizes["fsdp"]
        places = [(self.seq - back) * count + self.fsdp for back in range(3)]
        for flip in range(1, count):
            other = self.fsdp ^ flip
            places.append((self.seq - 1) * count + other)
            places.append(jnp.where(other < self.fsdp, self.seq, self.seq - 2) * count + other)
        return jnp.stack(places) * self.rows

    def fetch(self, own, section):
        one = self.along(own, section, 1)
        two = self.along(own, section, 2)
        blocks = [own, one, two]
        for flip in range(1, self.sizes["fsdp"]):
            chosen = jnp.where(self.fsdp < (self.fsdp ^ flip), own, two)
            got = self.across(jnp.stack((one, chosen)), section, flip)
            blocks += [got[0], got[1]]
        return jnp.concatenate(blocks, axis=1)

    def give_back(self, grads, section):
        rows = self.rows
        blocks = [grads[:, i * rows : (i + 1) * rows] for i in range(grads.shape[1] // rows)]
        own, one, two = blocks[0], blocks[1], blocks[2]
        for flip in range(1, self.sizes["fsdp"]):
            sent = jnp.stack((blocks[1 + 2 * flip], blocks[2 + 2 * flip])).astype(BF)
            got = self.across(sent, section, flip).astype(F32)
            lower = self.fsdp < (self.fsdp ^ flip)
            one = one + got[0]
            own = own + jnp.where(lower, got[1], 0.0)
            two = two + jnp.where(lower, 0.0, got[1])
        one = self.along(one.astype(BF), section, -1).astype(F32)
        two = self.along(two.astype(BF), section, -2).astype(F32)
        return own + one + two


def attend(query, keys, values, allowed):
    scores = dot(query, keys, "mthd,mkd->mhtk") * query.shape[-1] ** (-0.5)
    masked = jnp.where(allowed, scores, NEG_LARGE)
    exponent = jnp.exp(masked - jnp.max(masked, axis=-1, keepdims=True))
    probs = exponent / jnp.sum(exponent, axis=-1, keepdims=True)
    return dot(probs.astype(BF), values, "mhtk,mkd->mthd"), probs


def attend_back(grad, query, keys, values, probs):
    scale = query.shape[-1] ** (-0.5)
    grad_values = dot(probs.astype(BF), grad, "mhtk,mthd->mkd")
    grad_probs = dot(grad, values, "mthd,mkd->mhtk")
    inner = jnp.sum(probs * grad_probs, axis=-1, keepdims=True)
    grad_scores = (probs * (grad_probs - inner)).astype(BF)
    grad_query = dot(grad_scores, keys, "mhtk,mkd->mthd") * scale
    grad_keys = dot(grad_scores, query, "mhtk,mthd->mkd") * scale
    return grad_query, jnp.concatenate((grad_keys, grad_values), axis=-1)


def gated(gate, up):
    return jax.nn.gelu(gate, approximate=True) * up


def forward(layer_in, weights, tables, allowed, halo, section):
    micro, rows, width = layer_in.shape
    tokens = micro * rows
    cosine, sine = tables
    head_dim = weights["query_gain"].shape[0]
    heads_width = weights["out"].shape[0]
    heads = heads_width // head_dim
    residual = layer_in.astype(F32).reshape(tokens, width)
    scale_in = inverse_rms(residual)
    normed = (residual * scale_in * weights["attn_gain"]).astype(BF)
    qkv = dot(normed, weights["qkv"], "td,dn->tn")
    q = qkv[:, :heads_width].reshape(tokens, heads, head_dim)
    k = qkv[:, heads_width : heads_width + head_dim]
    v = qkv[:, heads_width + head_dim :]
    scale_q, scale_k = inverse_rms(q), inverse_rms(k)
    query = rotate(q * scale_q * weights["query_gain"], cosine[:, None], sine[:, None]).astype(BF)
    key = rotate(k * scale_k * weights["key_gain"], cosine, sine).astype(BF)
    own = jnp.concatenate((key, v.astype(BF)), axis=1).reshape(micro, rows, 2 * head_dim)
    window = halo.fetch(own, section)
    query = query.reshape(micro, rows, heads, head_dim)
    keys, values = window[..., :head_dim], window[..., head_dim:]
    attended, probs = attend(query, keys, values, allowed)
    attended = attended.astype(BF).reshape(tokens, heads_width)
    branch = dot(attended, weights["out"], "tn,nd->td")
    scale_branch = inverse_rms(branch)
    mixed = residual + branch * scale_branch * weights["post_attn_gain"]
    scale_mixed = inverse_rms(mixed)
    ffn_in = (mixed * scale_mixed * weights["ffn_gain"]).astype(BF)
    gate_up = dot(ffn_in, weights["gate_up"], "td,dn->tn")
    hidden = gate_up.shape[1] // 2
    gate, up = gate_up[:, :hidden], gate_up[:, hidden:]
    activated = gated(gate, up).astype(BF)
    down = dot(activated, weights["down"], "tf,fd->td")
    scale_down = inverse_rms(down)
    result = (mixed + down * scale_down * weights["post_ffn_gain"]).astype(BF)
    saved = dict(
        residual=residual, scale_in=scale_in, normed=normed, q=q, k=k, scale_q=scale_q,
        scale_k=scale_k, query=query, keys=keys, values=values, probs=probs, attended=attended,
        branch=branch, scale_branch=scale_branch, mixed=mixed, scale_mixed=scale_mixed,
        ffn_in=ffn_in, gate=gate, up=up, activated=activated, down=down, scale_down=scale_down,
    )
    return result.reshape(micro, rows, width), saved


def back_ffn(upstream, saved, weights):
    top = upstream.astype(F32).reshape(saved["mixed"].shape)
    grad_down = norm_back(saved["down"], saved["scale_down"], weights["post_ffn_gain"], top)
    grad_post_ffn = gain_back(saved["down"], saved["scale_down"], top)
    grad_down = grad_down.astype(BF)
    grad_act = dot(grad_down, weights["down"], "td,fd->tf")
    _, pull = jax.vjp(gated, saved["gate"], saved["up"])
    grad_gate, grad_up = pull(grad_act)
    grad_gate_up = jnp.concatenate((grad_gate.astype(BF), grad_up.astype(BF)), axis=1)
    grad_ffn_in = dot(grad_gate_up, weights["gate_up"], "tn,dn->td")
    grad_mixed = top + norm_back(
        saved["mixed"], saved["scale_mixed"], weights["ffn_gain"], grad_ffn_in
    )
    grad_ffn_gain = gain_back(saved["mixed"], saved["scale_mixed"], grad_ffn_in)
    return dict(
        ffn_in=saved["ffn_in"], gate_up=grad_gate_up, activated=saved["activated"],
        down=grad_down, mixed=grad_mixed, post_ffn_gain=grad_post_ffn, ffn_gain=grad_ffn_gain,
    )


def back_attention(grad_mixed, saved, weights):
    grad_branch = norm_back(
        saved["branch"], saved["scale_branch"], weights["post_attn_gain"], grad_mixed
    ).astype(BF)
    grad_post_attn = gain_back(saved["branch"], saved["scale_branch"], grad_mixed)
    grad_attended = dot(grad_branch, weights["out"], "td,nd->tn").astype(BF)
    grad_attended = grad_attended.reshape(saved["query"].shape)
    grad_query, grad_window = attend_back(
        grad_attended, saved["query"], saved["keys"], saved["values"], saved["probs"]
    )
    return dict(
        branch=grad_branch, post_attn_gain=grad_post_attn, query=grad_query, window=grad_window
    )


def back_project(grad_mixed, grad_query, grad_own, saved, weights, tables):
    cosine, sine = tables
    tokens, heads, head_dim = saved["q"].shape
    grad_own = grad_own.reshape(tokens, 2 * head_dim)
    grad_key = rotate(grad_own[:, :head_dim], cosine, -sine)
    grad_query = rotate(
        grad_query.reshape(tokens, heads, head_dim), cosine[:, None], -sine[:, None]
    )
    grad_query_gain = gain_back(saved["q"], saved["scale_q"], grad_query)
    grad_key_gain = gain_back(saved["k"], saved["scale_k"], grad_key)
    grad_q = norm_back(saved["q"], saved["scale_q"], weights["query_gain"], grad_query)
    grad_k = norm_back(saved["k"], saved["scale_k"], weights["key_gain"], grad_key)
    grad_qkv = jnp.concatenate(
        (
            grad_q.astype(BF).reshape(tokens, heads * head_dim),
            grad_k.astype(BF),
            grad_own[:, head_dim:].astype(BF),
        ),
        axis=1,
    )
    grad_normed = dot(grad_qkv, weights["qkv"], "tn,dn->td")
    grad_attn_gain = gain_back(saved["residual"], saved["scale_in"], grad_normed)
    grad_in = grad_mixed + norm_back(
        saved["residual"], saved["scale_in"], weights["attn_gain"], grad_normed
    )
    return dict(
        qkv=grad_qkv, grad_in=grad_in.astype(BF), attn_gain=grad_attn_gain,
        query_gain=grad_query_gain, key_gain=grad_key_gain,
    )


def body(sizes, hidden_in, cotangent, positions, attn_gain, w_query, w_key, w_value, query_gain,
         key_gain, w_output, post_attn_gain, ffn_gain, w_gate, w_up, w_down, post_ffn_gain):
    section = lax.axis_index("section")
    seq = lax.axis_index("seq")
    fsdp = lax.axis_index("fsdp")
    micro, rows, width = hidden_in.shape
    shard = w_query.shape[1]
    shards = sizes["fsdp"]
    heads_width, head_dim = w_query.shape[2], w_key.shape[2]

    def column(values):
        return jnp.pad(values[0], (0, shard - values.shape[1]))[:, None]

    gains = (attn_gain, post_attn_gain, ffn_gain, post_ffn_gain, query_gain, key_gain)
    columns = jnp.concatenate([column(g) for g in gains], axis=1)
    columns = jnp.pad(columns, ((0, 0), (0, 128 - len(gains))))
    first = jnp.concatenate((w_query[0], w_key[0], w_value[0], columns), axis=1)
    gather = partial(lax.all_gather, axis_name="fsdp", axis=0, tiled=True)
    first = gather(first)
    qkv_width = heads_width + 2 * head_dim
    gain_rows = first[:, qkv_width : qkv_width + len(gains)].astype(F32).T
    part = query_gain.shape[1]
    head_gains = gain_rows[4:].reshape(2, shards, shard)[:, :, :part].reshape(2, shards * part)
    weights = dict(
        qkv=first[:, :qkv_width],
        out=gather(w_output[0]),
        gate_up=gather(jnp.concatenate((w_gate[0], w_up[0]), axis=1)),
        down=gather(w_down[0]),
        attn_gain=gain_rows[0], post_attn_gain=gain_rows[1], ffn_gain=gain_rows[2],
        post_ffn_gain=gain_rows[3], query_gain=head_gains[0], key_gain=head_gains[1],
    )

    halo = Halo(sizes, section, seq, fsdp, rows)
    tables = rope_tables(positions.reshape(micro * rows), head_dim)
    query_place = (seq * shards + fsdp) * rows + jnp.arange(rows)
    key_place = (halo.starts()[:, None] + jnp.arange(rows)[None, :]).reshape(-1)
    distance = (query_place[:, None] - key_place[None, :])[None]
    allowed = (distance >= 0) & (distance < WIN) & (distance <= positions[:, :, None])
    allowed = allowed[:, None]

    def to_section(array, target):
        pairs = [
            (halo.index(1 - target, z, f), halo.index(target, z, f))
            for z in range(sizes["seq"])
            for f in range(shards)
        ]
        return lax.ppermute(array, AXES, pairs)

    result_a, saved_a = forward(hidden_in, weights, tables, allowed, halo, 0)
    middle = to_section(result_a, 1)
    result_b, saved_b = forward(middle, weights, tables, allowed, halo, 1)
    ffn_b = back_ffn(cotangent, saved_b, weights)
    attn_b = back_attention(ffn_b["mixed"], saved_b, weights)
    own_b = halo.give_back(attn_b["window"], 1)
    proj_b = back_project(ffn_b["mixed"], attn_b["query"], own_b, saved_b, weights, tables)
    grad_b = proj_b["grad_in"].reshape(micro, rows, width)
    upstream = to_section(grad_b, 0)

    is_first = section == 0

    def scatter(array):
        summed = lax.psum_scatter(array.astype(BF), "fsdp", scatter_dimension=0, tiled=True)
        return lax.psum(summed, "seq").astype(F32)

    ffn = lax.cond(is_first, lambda: back_ffn(upstream, saved_a, weights), lambda: ffn_b)
    grad_gate_up = scatter(dot(ffn["ffn_in"], ffn["gate_up"], "td,tn->dn"))
    grad_down = scatter(dot(ffn["activated"], ffn["down"], "tf,td->fd"))
    attn = lax.cond(
        is_first, lambda: back_attention(ffn["mixed"], saved_a, weights), lambda: attn_b
    )
    own = halo.give_back(attn["window"], 0)
    proj = lax.cond(
        is_first,
        lambda: back_project(ffn["mixed"], attn["query"], own, saved_a, weights, tables),
        lambda: proj_b,
    )
    attended = jnp.where(is_first, saved_a["attended"], saved_b["attended"])
    normed = jnp.where(is_first, saved_a["normed"], saved_b["normed"])
    grad_out = scatter(dot(attended, attn["branch"], "tn,td->nd"))

    def spread(values):
        return jnp.pad(values.reshape(shards, part), ((0, 0), (0, shard - part))).reshape(-1)

    gain_grads = jnp.stack(
        (
            proj["attn_gain"], attn["post_attn_gain"], ffn["ffn_gain"], ffn["post_ffn_gain"],
            spread(proj["query_gain"]), spread(proj["key_gain"]),
        ),
        axis=1,
    )
    gain_grads = jnp.pad(gain_grads, ((0, 0), (0, 128 - len(gains))))
    grad_first = scatter(
        jnp.concatenate((dot(normed, proj["qkv"], "td,tn->dn"), gain_grads), axis=1)
    )
    gain_out = grad_first[:, qkv_width : qkv_width + len(gains)].T

    section_outputs = jnp.where(is_first, result_a, result_b)[None]
    input_grads = proj["grad_in"].reshape(micro, rows, width)[None]
    hidden = w_gate.shape[2]
    return (
        section_outputs,
        input_grads,
        gain_out[0:1],
        grad_first[None, :, :heads_width],
        grad_first[None, :, heads_width : heads_width + head_dim],
        grad_first[None, :, heads_width + head_dim : qkv_width],
        gain_out[4:5, :part],
        gain_out[5:6, :part],
        grad_out[None],
        gain_out[1:2],
        gain_out[2:3],
        grad_gate_up[None, :, :hidden],
        grad_gate_up[None, :, hidden:],
        grad_down[None],
        gain_out[3:4],
    )


def solution(mesh):
    rows = P(None, ("seq", "fsdp"), None)
    vector, matrix = P("section", "fsdp"), P("section", "fsdp", None)
    weights = (vector, matrix, matrix, matrix, vector, vector, matrix, vector, vector, matrix,
               matrix, matrix, vector)
    out_rows = P("section", None, ("seq", "fsdp"), None)
    return jax.shard_map(
        partial(body, dict(mesh.shape)),
        mesh=mesh,
        in_specs=(rows, rows, P(None, ("seq", "fsdp"))) + weights,
        out_specs=(out_rows, out_rows) + weights,
        check_vma=False,
    )
```

time: 1160 us -> 654 us (0.56)
  blocking collectives: 234 us -> 0 us
  waiting for transfers between devices: 604 us -> 400 us
  starting transfers between devices: 135 us -> 41.2 us
  local copies, waits for them, and re-layouts: 44.8 us -> 68.6 us
  other arithmetic: 53.6 us -> 65.3 us
    reduce_scatter x7 -> x4, waiting for transfers between devices: 439 us -> 133 us  [scatter(): lax.psum_scatter(array.astype(BF), 'fsdp', scatter_dimension=0, tiled=True)]
    all_gather x9 -> x0, blocking collectives: 136 us -> none  [the longest x1 23.1 us: body(): lax.all_gather(pieces[10].astype(jnp.bfloat16), 'seq', axis=0, tiled=True)]
    psum x0 -> x1, waiting for transfers between devices: none -> 115 us  [scatter(): return lax.psum(summed, 'seq').astype(F32)]
    unnamed x3 -> x0, blocking collectives: 97.8 us -> none
    ppermute x52 -> x22, starting transfers between devices: 135 us -> 40.9 us  [the longest x12 23.7 us: across(): return lax.ppermute(array, AXES, pairs)]
    ppermute x52 -> x22, waiting for transfers between devices: 59.1 us -> 38.7 us  [the longest x2 26.8 us: to_section(): return lax.ppermute(array, AXES, pairs)]
    concatenate x6 -> x14, other arithmetic: 1.3 us -> 15.2 us  [the longest x2 3.51 us: attend_back(): return (grad_query, jnp.concatenate((grad_keys, grad_values), axis=-1))]
    dot_general x70 -> x30, matrix products: 59.4 us -> 48.3 us  [dot(): return jnp.einsum(spec, left, right, preferred_element_type=F32)]
  transfers between devices with their start and end apart: 64 -> 31, of which waited for: 34 -> 14; matrix products, arithmetic and copies ran while one was open for 7% -> 14% of each run, Pallas kernels for 0% -> 0%
where the time goes in v1:
time: 654 us; the launch traced here: 645 us
  waiting for transfers between devices  400 us (61%)
  local copies, waits for them, and re-layouts  68.6 us (10%)
  other arithmetic  65.3 us (10%)
  matrix products  52.9 us (8%)
  starting transfers between devices  41.2 us (6%)
  between operations  16.4 us (3%)
    reduce_scatter x4, waiting for transfers between devices, scatter(): lax.psum_scatter(array.astype(BF), 'fsdp', scatter_dimension=0, tiled=True)  133 us
    psum x1, waiting for transfers between devices, scatter(): return lax.psum(summed, 'seq').astype(F32)  115 us
    dot_general x30, matrix products, dot(): return jnp.einsum(spec, left, right, preferred_element_type=F32)  48.3 us
    all_gather x1, waiting for transfers between devices, body(): gather(jnp.concatenate((w_gate[0], w_up[0]), axis=1))  42.7 us
    all_gather x1, waiting for transfers between devices, body(): gather(w_down[0])  36.1 us
    unnamed x278, local copies, waits for them, and re-layouts  33.9 us
    all_gather x1, waiting for transfers between devices, body(): first = gather(first)  32.7 us
    ppermute x2, waiting for transfers between devices, to_section(): return lax.ppermute(array, AXES, pairs)  26.8 us
  transfers between devices with their start and end apart: 31, of which 14 were waited for; matrix products, arithmetic and copies ran while one was open for 14% of the time, Pallas kernels for 0%

profile of v1, /device:TPU:0, one launch (start us, length us, event | category | flops | bytes accessed | tf_op | source)
XLA Modules:
  0.0 644.6 jit_solution(17103842296685269140)
XLA Ops:
  9.6 1.9 fusion.79
  17.2 32.7 %all-gather.7.cloned.1.call-done = bf16[640,1664]{1,0:T(8,128)(2,1)} async-done(((bf16[160,1664]{1,0:T(8,128)(2,1)}), bf16[640,1664]{1,0:T(8,128)(2,1)}) %all-gather.7.cloned.1.call-update) | async-done | bytes 2129936 | tf_op jit(solution)/shard_map/all_gather | solution.py:262
  50.9 1.5 slice_reduce_fusion
  58.9 4.0 collective-permute-start
  62.9 4.3 collective-permute-start.1
  71.4 1.6 constant_dynamic-update-slice_fusion.1
  73.0 1.6 select_bitcast_fusion.3
  75.6 3.4 collective-permute-start.2
  79.9 2.6 collective-permute-start.3
  82.5 3.4 collective-permute-start.4
  89.6 2.0 collective-permute-done.4
  93.0 2.8 fusion.205
  95.8 1.5 broadcast_divide_fusion.1
  97.3 1.4 fusion.57
  99.7 1.9 multiply_reduce_fusion.27
  104.1 42.7 %all-gather.9.cloned.1.call-done = bf16[640,4096]{1,0:T(8,128)(2,1)} async-done(((bf16[160,4096]{1,0:T(8,128)(2,1)}), bf16[640,4096]{1,0:T(8,128)(2,1)}) %all-gather.9.cloned.1.call-update) | async-done | bytes 5242896 | tf_op jit(solution)/shard_map/all_gather | solution.py:270
  146.8 3.6 fusion.213
  150.4 1.6 fusion.199
  152.1 36.1 %all-gather.13.cloned.1.call-done = bf16[1,2048,640]{2,1,0:T(8,128)(2,1)} async-done(((bf16[1,512,640]{2,1,0:T(8,128)(2,1)}), bf16[1,2048,640]{2,1,0:T(8,128)(2,1)}) %all-gather.13.cloned.1.call-update) | async-done | bytes 2621456 | tf_op jit(solution)/shard_map/all_gather | solution.py:271
  188.2 2.6 multiply_reduce_fusion.25
  191.5 1.7 collective-permute-start.5
  193.3 2.3 fusion.200
  205.2 1.4 collective-permute-start.8
  209.6 1.6 fusion.125
  211.1 1.6 fusion.124
  215.4 1.8 fusion.210
  217.2 2.0 fusion.58
  224.0 1.3 copy-done.6
  226.3 1.4 fusion.66
  227.7 1.9 multiply_reduce_fusion.20
  230.8 2.1 multiply_reduce_fusion.13
  232.9 1.5 convolution_bitcast_fusion.4
  251.7 1.4 collective-permute-start.16
  253.1 1.8 pad_maximum_fusion.5
  256.1 26.8 %collective-permute-done.16 = bf16[2,64,640]{2,1,0:T(8,128)(2,1)} collective-permute-done((bf16[2,64,640]{2,1,0:T(8,128)(2,1)S(1)}, bf16[2,64,640]{2,1,0:T(8,128)(2,1)}, u32[]{:S(2)}, u32[]{:S(2)}) %collective-permute-start.16) | collective-permute-done | bytes 163872 | tf_op jit(solution)/shard_map/ppermute | solution.py:290
  283.0 18.3 %conditional.3 = (bf16[128,2048]{1,0:T(8,128)(2,1)}, bf16[128,640]{1,0:T(8,128)(2,1)}, bf16[128,640]{1,0:T(8,128)(2,1)}, bf16[128,4096]{1,0:T(8,128)(2,1)}, f32[...) conditional(s32[]{:T(128)} %convert_element_type.241, ...), branch_computations={%region_23.24_spmd, %region_24.27_spmd} | conditional | flops 1016579328 | bytes 32832860 | solution.py:308
  286.2 1.9 broadcast_multiply_fusion.1
  288.1 3.4 fusion.8
  293.7 4.7 multiply_reduce_fusion.3
  301.3 14.8 %conditional.4 = (bf16[128,640]{1,0:T(8,128)(2,1)}, f32[2,64,4,256]{3,1,2,0:T(8,128)}, f32[2,576,512]{2,1,0:T(8,128)}, f32[128,640]{1,0:T(8,128)}, f32[128,640]{1,0:T(8,128)}) conditional(s32[]{:T(128)} %convert_element_type.241, (f32[128,640]{1,0:T(8,128)}, f32[128,640]{1,0:T(8,128)}, bf16[128,640]{1,0:T(8,128)(2,1)}, ...), branch_computations={%region_27.29_spmd, %region_29.33_spmd} | conditional | flops 775405696 | bytes 26036864 | solution.py:311
  304.2 1.8 broadcast_multiply_fusion.2
  309.1 1.5 multiply_reduce_fusion.5
  312.4 1.8 pad_maximum_fusion.1
  316.1 2.7 convolution_convert_fusion.4
  318.9 1.6 pad_maximum_fusion.10
  320.9 3.5 collective-permute-start.19
  324.4 3.4 collective-permute-start.18
  327.9 2.5 collective-permute-start.17
  332.3 3.2 collective-permute-done.19
  335.5 1.9 collective-permute-done.18
  339.1 1.4 collective-permute-start.21
  342.7 1.9 collective-permute-done.20
  345.4 1.7 collective-permute-done.21
  349.8 16.0 %conditional.5 = (bf16[128,1536]{1,0:T(8,128)(2,1)}, bf16[1,2,64,640]{3,2,1,0:T(8,128)(2,1)}, bf16[640,1]{0,1:T(2,128)(2,1)S(1)}, bf16[640,1]{0,1:T(2,128)(2,1)S(1)}, bf16[640,1]{0,1:T(2,128)(2,1)S(1)}) conditional(s32[]{:T(128)} %convert_element_type.241, (f32[128,640]{1,0:T(8,128)}, f32[128,640]{1,0:T(8,128)}, bf16[128,640]{1,0:T(8,128)(2,1)}, ...), branch_computations={%region_33.37_spmd, %region_37.44_spmd} | conditional | flops 256987264 | bytes 20435236 | solution.py:315
  350.8 1.7 add_add_fusion
  366.8 1.9 convolution_convert_fusion.2
  368.7 1.5 fusion.46
  371.2 2.4 convolution_convert_fusion.3
  374.9 3.9 convolution_convert_fusion.1
  378.9 26.2 %reduce-scatter.5.cloned.1.call-done = bf16[160,1664]{1,0:T(8,128)(2,1)} async-done(((bf16[640,1664]{1,0:T(8,128)(2,1)}), bf16[160,1664]{1,0:T(8,128)(2,1)}) %reduce-scatter.5.cloned.1.call-update) | async-done | bytes 532496 | tf_op jit(solution)/shard_map/reduce_scatter | solution.py:305
  405.2 42.6 %reduce-scatter.11.cloned.1.call-done = bf16[512,640]{1,0:T(8,128)(2,1)} async-done(((bf16[2048,640]{1,0:T(8,128)(2,1)}), bf16[512,640]{1,0:T(8,128)(2,1)}) %reduce-scatter.11.cloned.1.call-update) | async-done | bytes 655376 | tf_op jit(solution)/shard_map/reduce_scatter | solution.py:305
  447.7 64.5 %reduce-scatter.9.cloned.1.call-done = bf16[160,4096]{1,0:T(8,128)(2,1)} async-done(((bf16[640,4096]{1,0:T(8,128)(2,1)}), bf16[160,4096]{1,0:T(8,128)(2,1)}) %reduce-scatter.9.cloned.1.call-update) | async-done | bytes 1310736 | tf_op jit(solution)/shard_map/reduce_scatter | solution.py:305
  512.2 114.7 %all-reduce.11.cloned.1.call-done = (bf16[160,1664]{1,0:T(8,128)(2,1)}, bf16[1,256,640]{2,1,0:T(8,128)(2,1)}, bf16[160,4096]{1,0:T(8,128)(2,1)}, bf16[1,512,640]{2,1,0:T(8,128)(2,1)}) async-done(((bf16[160,1664]{1,0:T(8,128)(2,1)}, bf16[1,256,640]{2,1,0:T(8,128)(2,1)}, bf16[160,4096]{1,0:T(8,128)(2,1)}, bf16[1,512,640]{2,1,0:T(8,128)(2,1)}), (bf16[160,1664]{1,0:T(8,128)(2,1)}, ...) | async-done | bytes 2826256 | tf_op jit(solution)/shard_map/psum | solution.py:306
  630.2 1.7 slice_bitcast_fusion
  (593 shorter events, 123.7 us)
Async XLA Ops:
  7.2 42.7 %all-gather.7.cloned.1.call-start = ((), (), s32[]{:S(2)}) async-start(), calls=%async_computation.4 | async-start | bytes 2662400 | tf_op jit(solution)/shard_map/all_gather | solution.py:262
  11.5 88.2 %all-gather.11.cloned.1.call-start = ((), (), s32[]{:S(2)}) async-start(), calls=%async_computation.10 | async-start | bytes 1638400 | tf_op jit(solution)/shard_map/all_gather | solution.py:269
  12.2 134.6 %all-gather.9.cloned.1.call-start = ((), (), s32[]{:S(2)}) async-start(), calls=%async_computation.5 | async-start | bytes 6553600 | tf_op jit(solution)/shard_map/all_gather | solution.py:270
  13.5 174.7 %all-gather.13.cloned.1.call-start = ((), (), s32[]{:S(2)}) async-start(), calls=%async_computation.11 | async-start | bytes 3276800 | tf_op jit(solution)/shard_map/all_gather | solution.py:271
  14.1 364.8 %reduce-scatter.7.cloned.1.call-start = ((), (), s32[]{:S(2)}) async-start(), calls=%async_computation.7 | async-start | bytes 1638400 | tf_op jit(solution)/shard_map/reduce_scatter | solution.py:305
  14.1 42.9 %copy-start.132 = (f32[128]{0:T(128)}, f32[128]{0:T(128)S(1)}, u32[]{:S(2)}) copy-start(f32[128]{0:T(128)S(1)} %multiply_power_fusion) | copy-start | bytes 1540
  14.7 37.6 %copy-start.143 = (f32[2,64]{1,0:T(2,128)}, f32[2,64]{1,0:T(2,128)S(1)}, u32[]{:S(2)}) copy-start(f32[2,64]{1,0:T(2,128)S(1)} %multiply_reduce_fusion.28) | copy-start | bytes 1540
  15.7 41.3 %copy-start.135 = (f32[128]{0:T(128)}, f32[128]{0:T(128)S(1)}, u32[]{:S(2)}) copy-start(f32[128]{0:T(128)S(1)} %convert_element_type.226) | copy-start | bytes 1540
  53.6 9.3 %copy-start.37 = (f32[128,1536]{1,0:T(8,128)}, f32[128,1536]{1,0:T(8,128)S(1)}, u32[]{:S(2)}) copy-start(f32[128,1536]{1,0:T(8,128)S(1)} %fusion.197) | copy-start | bytes 2359300
  54.3 14.0 %copy-start.148 = (f32[128]{0:T(128)}, f32[128]{0:T(128)S(1)}, u32[]{:S(2)}) copy-start(f32[128]{0:T(128)S(1)} %get-tuple-element.1099) | copy-start | bytes 1540
  58.0 21.0 %copy-start.76 = (f32[128,128]{1,0:T(8,128)}, f32[128,128]{1,0:T(8,128)S(1)}, u32[]{:S(2)}) copy-start(f32[128,128]{1,0:T(8,128)S(1)} %get-tuple-element.1143) | copy-start | bytes 196612
  58.9 12.6 %collective-permute-start = (bf16[2,64,512]{2,1,0:T(8,128)(2,1)S(1)}, bf16[2,64,512]{2,1,0:T(8,128)(2,1)}, u32[]{:S(2)}, u32[]{:S(2)}) collective-permute-start(bf16[2,64,512]{2,1,0:T(8,128)(2,1)S(1)} %bitcast.541), channel_id=1, source_target_pairs={{0,4},{1,5},{2,6},{3,7},{4,8},{5,9},{6,10},{7,11},{8,12},{9,13},{1... | collective-permute-start | bytes 393224 | tf_op jit(solution)/shard_map/ppermute | solution.py:66
  62.9 10.1 %collective-permute-start.1 = (bf16[2,64,512]{2,1,0:T(8,128)(2,1)S(1)}, bf16[2,64,512]{2,1,0:T(8,128)(2,1)}, u32[]{:S(2)}, u32[]{:S(2)}) collective-permute-start(bf16[2,64,512]{2,1,0:T(8,128)(2,1)S(1)} %bitcast.542), channel_id=1, source_target_pairs={{0,8},{1,9},{2,10},{3,11},{4,12},{5,13},{6,14},{7,15}} | collective-permute-start | bytes 393224 | tf_op jit(solution)/shard_map/ppermute | solution.py:66
  68.6 6.0 copy-start.8
  68.8 6.8 %copy-start.81 = (f32[128,4]{1,0:T(8,128)}, f32[128,4]{1,0:T(8,128)S(1)}, u32[]{:S(2)}) copy-start(f32[128,4]{1,0:T(8,128)S(1)} %multiply_reduce_fusion.15) | copy-start | bytes 6148
  69.9 5.7 copy-start.124
  70.0 5.6 copy-start.119
  75.6 10.2 %collective-permute-start.2 = (bf16[2,2,64,512]{3,2,1,0:T(8,128)(2,1)S(1)}, bf16[2,2,64,512]{3,2,1,0:T(8,128)(2,1)S(1)}, u32[]{:S(2)}, u32[]{:S(2)}) collective-permute-start(bf16[2,2,64,512]{3,2,1,0:T(8,128)(2,1)S(1)} %get-tuple-element.1134), channel_id=1, source_target_pairs={{0,1},{1,0},{2,3},{3,2},{4,5},{5,4},{6,7},{7,6},{8,9},{9,8},{10,11... | collective-permute-start | bytes 786440 | tf_op jit(solution)/shard_map/ppermute | solution.py:74
  79.9 13.1 %copy-start.115 = (pred[2,64,576]{2,1,0:T(8,128)(4,1)S(1)}, pred[2,64,576]{2,1,0:T(8,128)(4,1)}, u32[]{:S(2)}) copy-start(pred[2,64,576]{2,1,0:T(8,128)(4,1)} %compare_and_fusion) | copy-start | bytes 221188
  79.9 8.4 %collective-permute-start.3 = (bf16[2,2,64,512]{3,2,1,0:T(8,128)(2,1)S(1)}, bf16[2,2,64,512]{3,2,1,0:T(8,128)(2,1)S(1)}, u32[]{:S(2)}, u32[]{:S(2)}) collective-permute-start(bf16[2,2,64,512]{3,2,1,0:T(8,128)(2,1)S(1)} %get-tuple-element.1133), channel_id=1, source_target_pairs={{0,2},{1,3},{2,0},{3,1},{4,6},{5,7},{6,4},{7,5},{8,10},{9,11},{10,... | collective-permute-start | bytes 786440 | tf_op jit(solution)/shard_map/ppermute | solution.py:74
  82.5 9.2 %collective-permute-start.4 = (bf16[2,2,64,512]{3,2,1,0:T(8,128)(2,1)S(1)}, bf16[2,2,64,512]{3,2,1,0:T(8,128)(2,1)S(1)}, u32[]{:S(2)}, u32[]{:S(2)}) collective-permute-start(bf16[2,2,64,512]{3,2,1,0:T(8,128)(2,1)S(1)} %get-tuple-element.1132), channel_id=1, source_target_pairs={{0,3},{1,2},{2,1},{3,0},{4,7},{5,6},{6,5},{7,4},{8,11},{9,10},{10,... | collective-permute-start | bytes 786440 | tf_op jit(solution)/shard_map/ppermute | solution.py:74
  101.6 48.8 %copy-start.150 = (f32[128]{0:T(128)}, f32[128]{0:T(128)S(1)}, u32[]{:S(2)}) copy-start(f32[128]{0:T(128)S(1)} %get-tuple-element.1151) | copy-start | bytes 1540
  102.6 47.8 %copy-start.151 = (f32[128]{0:T(128)}, f32[128]{0:T(128)S(1)}, u32[]{:S(2)}) copy-start(f32[128]{0:T(128)S(1)} %get-tuple-element.1043) | copy-start | bytes 1540
  191.5 4.1 collective-permute-start.5
  200.2 2.6 collective-permute-start.6
  200.9 2.6 collective-permute-start.7
  205.2 4.4 collective-permute-start.8
  208.0 9.2 %copy-start.101 = (bf16[128,4,128]{2,0,1:T(8,128)(2,1)}, bf16[128,4,128]{2,0,1:T(8,128)(2,1)S(1)}, u32[]{:S(2)}) copy-start(bf16[128,4,128]{2,0,1:T(8,128)(2,1)S(1)} %get-tuple-element.1102) | copy-start | bytes 393220
  208.0 9.2 %copy-start.103 = (bf16[128,4,128]{2,0,1:T(8,128)(2,1)}, bf16[128,4,128]{2,0,1:T(8,128)(2,1)S(1)}, u32[]{:S(2)}) copy-start(bf16[128,4,128]{2,0,1:T(8,128)(2,1)S(1)} %get-tuple-element.1103) | copy-start | bytes 393220
  208.0 4.7 collective-permute-start.9
  208.7 5.3 collective-permute-start.10
  221.7 8.0 %copy-start.16 = (f32[128,640]{1,0:T(8,128)}, f32[128,640]{1,0:T(8,128)S(1)}, u32[]{:S(2)}) copy-start(f32[128,640]{1,0:T(8,128)S(1)} %get-tuple-element.1039) | copy-start | bytes 983044
  229.9 21.1 %copy-start.13 = (f32[128,640]{1,0:T(8,128)}, f32[128,640]{1,0:T(8,128)S(1)}, u32[]{:S(2)}) copy-start(f32[128,640]{1,0:T(8,128)S(1)} %get-tuple-element.1033) | copy-start | bytes 983044
  242.8 2.5 collective-permute-start.11
  243.6 1.7 collective-permute-start.12
  244.3 1.1 collective-permute-start.13
  245.8 2.6 collective-permute-start.14
  246.4 1.9 collective-permute-start.15
  251.7 31.2 %collective-permute-start.16 = (bf16[2,64,640]{2,1,0:T(8,128)(2,1)S(1)}, bf16[2,64,640]{2,1,0:T(8,128)(2,1)}, u32[]{:S(2)}, u32[]{:S(2)}) collective-permute-start(bf16[2,64,640]{2,1,0:T(8,128)(2,1)S(1)} %bitcast.576), channel_id=1, source_target_pairs={{16,0},{17,1},{18,2},{19,3},{20,4},{21,5},{22,6},{23,7},{24,8},{25... | collective-permute-start | bytes 491528 | tf_op jit(solution)/shard_map/ppermute | solution.py:290
  254.9 28.0 %copy-start.12 = (f32[128,640]{1,0:T(8,128)S(1)}, f32[128,640]{1,0:T(8,128)}, u32[]{:S(2)}) copy-start(f32[128,640]{1,0:T(8,128)} %copy-done.10) | copy-start | bytes 983044
  254.9 28.0 %copy-start.14 = (f32[128,640]{1,0:T(8,128)S(1)}, f32[128,640]{1,0:T(8,128)}, u32[]{:S(2)}) copy-start(f32[128,640]{1,0:T(8,128)} %copy-done.13) | copy-start | bytes 983044
  282.9 18.3 %copy-start.129 = (f32[128,1]{0,1:T(1,128)}, f32[128,1]{0,1:T(1,128)S(1)}, u32[]{:S(2)}) copy-start(f32[128,1]{0,1:T(1,128)S(1)} %broadcast.599) | copy-start | bytes 1540
  283.0 18.3 %copy-start.1 = (bf16[1,1024,640]{2,1,0:T(8,128)(2,1)S(1)}, bf16[1,1024,640]{2,1,0:T(8,128)(2,1)}, u32[]{:S(2)}) copy-start(bf16[1,1024,640]{2,1,0:T(8,128)(2,1)} %all-gather.11.cloned.1.call-done) | copy-start | bytes 3932164
  318.8 86.3 %reduce-scatter.5.cloned.1.call-start = ((), (), s32[]{:S(2)}) async-start(), calls=%async_computation.6 | async-start | bytes 2662400 | tf_op jit(solution)/shard_map/reduce_scatter | solution.py:305
  320.7 9.6 %copy-start.25 = (f32[128,640]{1,0:T(8,128)S(1)}, f32[128,640]{1,0:T(8,128)}, u32[]{:S(2)}) copy-start(f32[128,640]{1,0:T(8,128)} %get-tuple-element.568) | copy-start | bytes 983044
  320.7 9.6 %copy-start.30 = (f32[128,640]{1,0:T(8,128)S(1)}, f32[128,640]{1,0:T(8,128)}, u32[]{:S(2)}) copy-start(f32[128,640]{1,0:T(8,128)} %get-tuple-element.571) | copy-start | bytes 983044
  320.7 9.6 %copy-start.72 = (f32[128,640]{1,0:T(8,128)S(1)}, f32[128,640]{1,0:T(8,128)}, u32[]{:S(2)}) copy-start(f32[128,640]{1,0:T(8,128)} %get-tuple-element.567) | copy-start | bytes 983044
  320.8 9.6 %copy-start.74 = (f32[128,640]{1,0:T(8,128)S(1)}, f32[128,640]{1,0:T(8,128)}, u32[]{:S(2)}) copy-start(f32[128,640]{1,0:T(8,128)} %get-tuple-element.570) | copy-start | bytes 983044
  320.9 10.8 %copy-start.15 = (f32[128,640]{1,0:T(8,128)S(1)}, f32[128,640]{1,0:T(8,128)}, u32[]{:S(2)}) copy-start(f32[128,640]{1,0:T(8,128)} %get-tuple-element.583) | copy-start | bytes 983044
  320.9 10.8 %copy-start.71 = (f32[128,640]{1,0:T(8,128)S(1)}, f32[128,640]{1,0:T(8,128)}, u32[]{:S(2)}) copy-start(f32[128,640]{1,0:T(8,128)} %get-tuple-element.582) | copy-start | bytes 983044
  320.9 14.6 %collective-permute-start.19 = (bf16[2,2,64,512]{3,2,1,0:T(8,128)(2,1)S(1)}, bf16[2,2,64,512]{3,2,1,0:T(8,128)(2,1)S(1)}, u32[]{:S(2)}, u32[]{:S(2)}) collective-permute-start(bf16[2,2,64,512]{3,2,1,0:T(8,128)(2,1)S(1)} %pad_maximum_fusion.24), channel_id=1, source_target_pairs={{0,3},{1,2},{2,1},{3,0},{4,7},{5,6},{6,5},{7,4},{8,11},{9,10},{10,... | collective-permute-start | bytes 786440 | tf_op jit(solution)/shard_map/ppermute | solution.py:74
  324.4 13.0 %collective-permute-start.18 = (bf16[2,2,64,512]{3,2,1,0:T(8,128)(2,1)S(1)}, bf16[2,2,64,512]{3,2,1,0:T(8,128)(2,1)S(1)}, u32[]{:S(2)}, u32[]{:S(2)}) collective-permute-start(bf16[2,2,64,512]{3,2,1,0:T(8,128)(2,1)S(1)} %pad_maximum_fusion.23), channel_id=1, source_target_pairs={{0,2},{1,3},{2,0},{3,1},{4,6},{5,7},{6,4},{7,5},{8,10},{9,11},{10,... | collective-permute-start | bytes 786440 | tf_op jit(solution)/shard_map/ppermute | solution.py:74
  327.9 9.6 %collective-permute-start.17 = (bf16[2,2,64,512]{3,2,1,0:T(8,128)(2,1)S(1)}, bf16[2,2,64,512]{3,2,1,0:T(8,128)(2,1)S(1)}, u32[]{:S(2)}, u32[]{:S(2)}) collective-permute-start(bf16[2,2,64,512]{3,2,1,0:T(8,128)(2,1)S(1)} %pad_maximum_fusion.22), channel_id=1, source_target_pairs={{0,1},{1,0},{2,3},{3,2},{4,5},{5,4},{6,7},{7,6},{8,9},{9,8},{10,11... | collective-permute-start | bytes 786440 | tf_op jit(solution)/shard_map/ppermute | solution.py:74
  337.8 6.9 %collective-permute-start.20 = (bf16[2,64,512]{2,1,0:T(8,128)(2,1)S(1)}, bf16[2,64,512]{2,1,0:T(8,128)(2,1)S(1)}, u32[]{:S(2)}, u32[]{:S(2)}) collective-permute-start(bf16[2,64,512]{2,1,0:T(8,128)(2,1)S(1)} %get-tuple-element.1072), channel_id=1, source_target_pairs={{4,0},{5,1},{6,2},{7,3},{8,4},{9,5},{10,6},{11,7},{12,8},{13,9},{1... | collective-permute-start | bytes 393224 | tf_op jit(solution)/shard_map/ppermute | solution.py:66
  339.1 10.7 %slice-start.2 = ((bf16[640,1664]{1,0:T(8,128)(2,1)}), bf16[640,1536]{1,0:T(8,128)(2,1)S(1)}, s32[]{:S(2)}) async-start(bf16[640,1664]{1,0:T(8,128)(2,1)} %all-gather.7.cloned.1.call-done), calls=%async_computation.15 | async-start | bytes 3932160 | tf_op jit(solution)/shard_map/slice | solution.py:268
  339.1 10.7 %copy-start.9 = (f32[128,4,256]{2,1,0:T(4,128)S(1)}, f32[128,4,256]{2,1,0:T(4,128)}, u32[]{:S(2)}) copy-start(f32[128,4,256]{2,1,0:T(4,128)} %copy-done.8) | copy-start | bytes 1572868
  339.1 10.7 %copy-start.123 = (f32[1,4,64]{2,1,0:T(4,128)S(1)}, f32[1,4,64]{2,1,0:T(4,128)}, u32[]{:S(2)}) copy-start(f32[1,4,64]{2,1,0:T(4,128)} %copy-done.122) | copy-start | bytes 3076
  339.1 10.7 %copy-start.125 = (f32[1,4,64]{2,1,0:T(4,128)S(1)}, f32[1,4,64]{2,1,0:T(4,128)}, u32[]{:S(2)}) copy-start(f32[1,4,64]{2,1,0:T(4,128)} %copy-done.124) | copy-start | bytes 3076
  339.1 7.9 %collective-permute-start.21 = (bf16[2,64,512]{2,1,0:T(8,128)(2,1)S(1)}, bf16[2,64,512]{2,1,0:T(8,128)(2,1)S(1)}, u32[]{:S(2)}, u32[]{:S(2)}) collective-permute-start(bf16[2,64,512]{2,1,0:T(8,128)(2,1)S(1)} %get-tuple-element.1071), channel_id=1, source_target_pairs={{8,0},{9,1},{10,2},{11,3},{12,4},{13,5},{14,6},{15,7}} | collective-permute-start | bytes 393224 | tf_op jit(solution)/shard_map/ppermute | solution.py:66
  357.5 6.2 copy-start.68
  357.5 6.4 copy-start.40
  370.2 77.5 %reduce-scatter.11.cloned.1.call-start = ((), (), s32[]{:S(2)}) async-start(), calls=%async_computation.9 | async-start | bytes 3276800 | tf_op jit(solution)/shard_map/reduce_scatter | solution.py:305
  373.7 138.5 %reduce-scatter.9.cloned.1.call-start = ((), (), s32[]{:S(2)}) async-start(), calls=%async_computation.8 | async-start | bytes 6553600 | tf_op jit(solution)/shard_map/reduce_scatter | solution.py:305
  378.8 248.0 %all-reduce.11.cloned.1.call-start = ((), (), s32[]{:S(2)}) async-start(), calls=%async_computation.12 | async-start | bytes 5652480 | tf_op jit(solution)/shard_map/psum | solution.py:306
  (122 other events, 235.2 us)
Sparse Core Ops, SparseCore 0:
  11.6 38.2 all-gather.6
  51.8 28.8 all-gather.10
  83.1 63.6 all-gather.8
  148.5 39.6 all-gather.12
  319.0 30.4 reduce-scatter.6
  370.3 34.7 reduce-scatter.4
  408.1 39.5 reduce-scatter.10
  450.7 61.4 reduce-scatter.8
  514.8 111.9 all-reduce.10

commit v2 on v1

--- a/solution.py
+++ b/solution.py
@@ -68,6 +68,14 @@
     def across(self, array, section, flip):
         pairs = [
             (self.index(section, z, f), self.index(section, z, f ^ flip))
+            for z in range(self.sizes["seq"])
+            for f in range(self.sizes["fsdp"])
+        ]
+        return lax.ppermute(array, AXES, pairs)
+
+    def exchange(self, array, section, span):
+        pairs = [
+            (self.index(section, z, f), self.index(section, z ^ span, f))
             for z in range(self.sizes["seq"])
             for f in range(self.sizes["fsdp"])
         ]
@@ -250,6 +258,10 @@
     shard = w_query.shape[1]
     shards = sizes["fsdp"]
     heads_width, head_dim = w_query.shape[2], w_key.shape[2]
+    qkv_width = heads_width + 2 * head_dim
+    hidden = w_gate.shape[2]
+    part = query_gain.shape[1]
+    halo = Halo(sizes, section, seq, fsdp, rows)
 
     def column(values):
         return jnp.pad(values[0], (0, shard - values.shape[1]))[:, None]
@@ -257,23 +269,32 @@
     gains = (attn_gain, post_attn_gain, ffn_gain, post_ffn_gain, query_gain, key_gain)
     columns = jnp.concatenate([column(g) for g in gains], axis=1)
     columns = jnp.pad(columns, ((0, 0), (0, 128 - len(gains))))
-    first = jnp.concatenate((w_query[0], w_key[0], w_value[0], columns), axis=1)
-    gather = partial(lax.all_gather, axis_name="fsdp", axis=0, tiled=True)
-    first = gather(first)
-    qkv_width = heads_width + 2 * head_dim
-    gain_rows = first[:, qkv_width : qkv_width + len(gains)].astype(F32).T
-    part = query_gain.shape[1]
-    head_gains = gain_rows[4:].reshape(2, shards, shard)[:, :, :part].reshape(2, shards * part)
-    weights = dict(
-        qkv=first[:, :qkv_width],
-        out=gather(w_output[0]),
-        gate_up=gather(jnp.concatenate((w_gate[0], w_up[0]), axis=1)),
-        down=gather(w_down[0]),
-        attn_gain=gain_rows[0], post_attn_gain=gain_rows[1], ffn_gain=gain_rows[2],
-        post_ffn_gain=gain_rows[3], query_gain=head_gains[0], key_gain=head_gains[1],
-    )
-
-    halo = Halo(sizes, section, seq, fsdp, rows)
+    own_shards = (
+        jnp.concatenate((w_query[0], w_key[0], w_value[0], columns), axis=1),
+        w_output[0],
+        jnp.concatenate((w_gate[0], w_up[0]), axis=1),
+        w_down[0],
+    )
+
+    def gather(array, target):
+        count = array.shape[0]
+        full = jnp.zeros((count * shards, array.shape[1]), array.dtype)
+        for flip in range(shards):
+            piece = halo.across(array, target, flip) if flip else array
+            full = lax.dynamic_update_slice_in_dim(full, piece, (fsdp ^ flip) * count, 0)
+        return full
+
+    def gather_weights(arrays, target):
+        first, out, gate_up, down = [gather(array, target) for array in arrays]
+        gain_rows = first[:, qkv_width : qkv_width + len(gains)].astype(F32).T
+        head_gains = gain_rows[4:].reshape(2, shards, shard)[:, :, :part]
+        head_gains = head_gains.reshape(2, shards * part)
+        return dict(
+            qkv=first[:, :qkv_width], out=out, gate_up=gate_up, down=down,
+            attn_gain=gain_rows[0], post_attn_gain=gain_rows[1], ffn_gain=gain_rows[2],
+            post_ffn_gain=gain_rows[3], query_gain=head_gains[0], key_gain=head_gains[1],
+        )
+
     tables = rope_tables(positions.reshape(micro * rows), head_dim)
     query_place = (seq * shards + fsdp) * rows + jnp.arange(rows)
     key_place = (halo.starts()[:, None] + jnp.arange(rows)[None, :]).reshape(-1)
@@ -289,71 +310,142 @@
         ]
         return lax.ppermute(array, AXES, pairs)
 
-    result_a, saved_a = forward(hidden_in, weights, tables, allowed, halo, 0)
-    middle = to_section(result_a, 1)
-    result_b, saved_b = forward(middle, weights, tables, allowed, halo, 1)
-    ffn_b = back_ffn(cotangent, saved_b, weights)
-    attn_b = back_attention(ffn_b["mixed"], saved_b, weights)
-    own_b = halo.give_back(attn_b["window"], 1)
-    proj_b = back_project(ffn_b["mixed"], attn_b["query"], own_b, saved_b, weights, tables)
-    grad_b = proj_b["grad_in"].reshape(micro, rows, width)
-    upstream = to_section(grad_b, 0)
-
-    is_first = section == 0
-
-    def scatter(array):
-        summed = lax.psum_scatter(array.astype(BF), "fsdp", scatter_dimension=0, tiled=True)
-        return lax.psum(summed, "seq").astype(F32)
-
-    ffn = lax.cond(is_first, lambda: back_ffn(upstream, saved_a, weights), lambda: ffn_b)
-    grad_gate_up = scatter(dot(ffn["ffn_in"], ffn["gate_up"], "td,tn->dn"))
-    grad_down = scatter(dot(ffn["activated"], ffn["down"], "tf,td->fd"))
-    attn = lax.cond(
-        is_first, lambda: back_attention(ffn["mixed"], saved_a, weights), lambda: attn_b
-    )
-    own = halo.give_back(attn["window"], 0)
-    proj = lax.cond(
-        is_first,
-        lambda: back_project(ffn["mixed"], attn["query"], own, saved_a, weights, tables),
-        lambda: proj_b,
-    )
-    attended = jnp.where(is_first, saved_a["attended"], saved_b["attended"])
-    normed = jnp.where(is_first, saved_a["normed"], saved_b["normed"])
-    grad_out = scatter(dot(attended, attn["branch"], "tn,td->nd"))
+    def columns_of(array, flip):
+        count = array.shape[1] // shards
+        return lax.dynamic_slice_in_dim(array, (fsdp ^ flip) * count, count, 1)
+
+    def fold(array):
+        return jnp.concatenate([array[i * shard : (i + 1) * shard] for i in range(shards)], axis=1)
+
+    def unfold(array):
+        count = array.shape[1] // shards
+        return jnp.concatenate(
+            [array[:, i * count : (i + 1) * count] for i in range(shards)], axis=0
+        ).T
+
+    def ffn_block(ffn, saved, flip):
+        return jnp.concatenate(
+            (
+                dot(columns_of(saved["ffn_in"], flip), ffn["gate_up"], "td,tn->dn"),
+                fold(dot(ffn["down"], columns_of(saved["activated"], flip), "td,tf->df")),
+            ),
+            axis=1,
+        )
+
+    def attention_block(attn, proj, gain_grads, saved, flip):
+        return jnp.concatenate(
+            (
+                dot(columns_of(saved["normed"], flip), proj["qkv"], "td,tn->dn"),
+                lax.dynamic_slice_in_dim(gain_grads, (fsdp ^ flip) * shard, shard, 0),
+                fold(dot(attn["branch"], columns_of(saved["attended"], flip), "td,tn->dn")),
+            ),
+            axis=1,
+        )
 
     def spread(values):
         return jnp.pad(values.reshape(shards, part), ((0, 0), (0, shard - part))).reshape(-1)
 
-    gain_grads = jnp.stack(
-        (
-            proj["attn_gain"], attn["post_attn_gain"], ffn["ffn_gain"], ffn["post_ffn_gain"],
-            spread(proj["query_gain"]), spread(proj["key_gain"]),
-        ),
-        axis=1,
-    )
-    gain_grads = jnp.pad(gain_grads, ((0, 0), (0, 128 - len(gains))))
-    grad_first = scatter(
-        jnp.concatenate((dot(normed, proj["qkv"], "td,tn->dn"), gain_grads), axis=1)
-    )
-    gain_out = grad_first[:, qkv_width : qkv_width + len(gains)].T
-
+    def gain_columns(ffn, attn, proj):
+        stacked = jnp.stack(
+            (
+                proj["attn_gain"], attn["post_attn_gain"], ffn["ffn_gain"], ffn["post_ffn_gain"],
+                spread(proj["query_gain"]), spread(proj["key_gain"]),
+            ),
+            axis=1,
+        )
+        return jnp.pad(stacked, ((0, 0), (0, 128 - len(gains))))
+
+    def blocks_of(block):
+        return [block(flip).astype(BF) for flip in range(1, shards)], block(0)
+
+    def sum_plane(blocks, target):
+        sent, own = blocks
+        got = [halo.across(piece, target, 1 + i).astype(F32) for i, piece in enumerate(sent)]
+        return sum(got, own).astype(BF)
+
+    def sum_seq(array, target):
+        steps = []
+        span = 1
+        while span < sizes["seq"]:
+            bit = (seq // span) % 2
+            half = array.shape[1] // 2
+            keep = lax.dynamic_slice_in_dim(array, bit * half, half, 1)
+            send = lax.dynamic_slice_in_dim(array, (1 - bit) * half, half, 1)
+            got = halo.exchange(send, target, span)
+            array = (keep.astype(F32) + got.astype(F32)).astype(BF)
+            steps.append((span, bit))
+            span *= 2
+        for span, bit in reversed(steps):
+            got = halo.exchange(array, target, span)
+            array = jnp.concatenate(
+                (jnp.where(bit == 0, array, got), jnp.where(bit == 0, got, array)), axis=1
+            )
+        return array
+
+    first = gather_weights(own_shards, 0)
+    result_a, saved_a = forward(hidden_in, first, tables, allowed, halo, 0)
+    token = to_section(saved_a["keys"][:1, -16:, :64], 1)
+    later, token = lax.optimization_barrier((own_shards, token))
+    tied = lax.dynamic_update_slice(later[0], token[0], (0, later[0].shape[1] - token.shape[2]))
+    second = gather_weights((tied,) + later[1:], 1)
+    middle = to_section(result_a, 1)
+    result_b, saved_b = forward(middle, second, tables, allowed, halo, 1)
+
+    ffn_b = back_ffn(cotangent, saved_b, second)
+    attn_b = back_attention(ffn_b["mixed"], saved_b, second)
+    own_b = halo.give_back(attn_b["window"], 1)
+    proj_b = back_project(ffn_b["mixed"], attn_b["query"], own_b, saved_b, second, tables)
+    upstream = to_section(proj_b["grad_in"].reshape(micro, rows, width), 0)
+    gains_b = gain_columns(ffn_b, attn_b, proj_b)
+    ffn_blocks = blocks_of(partial(ffn_block, ffn_b, saved_b))
+    attn_blocks = blocks_of(partial(attention_block, attn_b, proj_b, gains_b, saved_b))
+    upstream, ffn_blocks, attn_blocks = lax.optimization_barrier(
+        (upstream, ffn_blocks, attn_blocks)
+    )
+    ffn_sum_b = sum_plane(ffn_blocks, 1)
+    attn_sum_b = sum_plane(attn_blocks, 1)
+
+    ffn_a = back_ffn(upstream, saved_a, first)
+    ffn_sum_a = sum_plane(blocks_of(partial(ffn_block, ffn_a, saved_a)), 0)
+    attn_a = back_attention(ffn_a["mixed"], saved_a, first)
+    own_a = halo.give_back(attn_a["window"], 0)
+    proj_a = back_project(ffn_a["mixed"], attn_a["query"], own_a, saved_a, first, tables)
+    gains_a = gain_columns(ffn_a, attn_a, proj_a)
+    attn_sum_a = sum_plane(
+        blocks_of(partial(attention_block, attn_a, proj_a, gains_a, saved_a)), 0
+    )
+
+    is_first = section == 0
+    attn_cols = attn_sum_a.shape[1]
+    padded = -(-attn_cols // (128 * sizes["seq"])) * 128 * sizes["seq"]
+
+    def total(ours, theirs, target_a=0, target_b=1):
+        return jnp.where(is_first, sum_seq(ours, target_a), sum_seq(theirs, target_b)).astype(F32)
+
+    def widen(array):
+        return jnp.pad(array, ((0, 0), (0, padded - attn_cols)))
+
+    ffn_total = total(ffn_sum_a, ffn_sum_b)
+    attn_total = total(widen(attn_sum_a), widen(attn_sum_b))
+    gain_out = attn_total[:, qkv_width : qkv_width + len(gains)].T
+    grad_down = unfold(ffn_total[:, 2 * hidden :])
+    grad_out = unfold(attn_total[:, qkv_width + 128 : qkv_width + 128 + heads_width])
     section_outputs = jnp.where(is_first, result_a, result_b)[None]
-    input_grads = proj["grad_in"].reshape(micro, rows, width)[None]
-    hidden = w_gate.shape[2]
+    input_grads = jnp.where(is_first, proj_a["grad_in"], proj_b["grad_in"])
     return (
         section_outputs,
-        input_grads,
+        input_grads.reshape(micro, rows, width)[None],
         gain_out[0:1],
-        grad_first[None, :, :heads_width],
-        grad_first[None, :, heads_width : heads_width + head_dim],
-        grad_first[None, :, heads_width + head_dim : qkv_width],
+        attn_total[None, :, :heads_width],
+        attn_total[None, :, heads_width : heads_width + head_dim],
+        attn_total[None, :, heads_width + head_dim : qkv_width],
         gain_out[4:5, :part],
         gain_out[5:6, :part],
         grad_out[None],
         gain_out[1:2],
         gain_out[2:3],
-        grad_gate_up[None, :, :hidden],
-        grad_gate_up[None, :, hidden:],
+        ffn_total[None, :, :hidden],
+        ffn_total[None, :, hidden : 2 * hidden],
         grad_down[None],
         gain_out[3:4],
     )

time: 654 us -> 761 us (1.16)
  waiting for transfers between devices: 400 us -> 169 us
  local copies, waits for them, and re-layouts: 68.6 us -> 255 us
  starting transfers between devices: 41.2 us -> 160 us
  matrix products: 52.9 us -> 98.3 us
  between operations: 16.4 us -> 5.1 us
    reduce_scatter x4 -> x0, waiting for transfers between devices: 133 us -> none  [scatter(): lax.psum_scatter(array.astype(BF), 'fsdp', scatter_dimension=0, tiled=True)]
    dynamic_update_slice x0 -> x33, local copies, waits for them, and re-layouts: none -> 117 us  [the longest x31 116 us: gather(): lax.dynamic_update_slice_in_dim(full, piece, (fsdp ^ flip) * count, 0)]
    psum x1 -> x0, waiting for transfers between devices: 115 us -> none  [scatter(): return lax.psum(summed, 'seq').astype(F32)]
    all_gather x4 -> x0, waiting for transfers between devices: 112 us -> none  [the longest x1 42.7 us: body(): gather(jnp.concatenate((w_gate[0], w_up[0]), axis=1))]
    ppermute x12 -> x48, starting transfers between devices: 23.7 us -> 112 us  [across(): return lax.ppermute(array, AXES, pairs)]
    ppermute x12 -> x48, waiting for transfers between devices: 8.23 us -> 86.8 us  [across(): return lax.ppermute(array, AXES, pairs)]
    ppermute x0 -> x16, waiting for transfers between devices: none -> 49 us  [exchange(): return lax.ppermute(array, AXES, pairs)]
    dot_general x30 -> x58, matrix products: 48.3 us -> 92.8 us  [dot(): return jnp.einsum(spec, left, right, preferred_element_type=F32)]
  transfers between devices with their start and end apart: 31 -> 75, of which waited for: 14 -> 16; matrix products, arithmetic and copies ran while one was open for 14% -> 40% of each run, Pallas kernels for 0% -> 0%
where the time goes in v2:
time: 761 us; the launch traced here: 746 us
  local copies, waits for them, and re-layouts  255 us (34%)
  waiting for transfers between devices  169 us (22%)
  starting transfers between devices  160 us (21%)
  matrix products  98.3 us (13%)
  other arithmetic  57.7 us (8%)
    dynamic_update_slice x31, local copies, waits for them, and re-layouts, gather(): lax.dynamic_update_slice_in_dim(full, piece, (fsdp ^ flip) * count, 0)  116 us
    ppermute x48, starting transfers between devices, across(): return lax.ppermute(array, AXES, pairs)  112 us
    dot_general x58, matrix products, dot(): return jnp.einsum(spec, left, right, preferred_element_type=F32)  92.8 us
    ppermute x48, waiting for transfers between devices, across(): return lax.ppermute(array, AXES, pairs)  86.8 us
    unnamed x457, local copies, waits for them, and re-layouts  73.3 us
    ppermute x16, waiting for transfers between devices, exchange(): return lax.ppermute(array, AXES, pairs)  49 us
    ppermute x16, starting transfers between devices, exchange(): return lax.ppermute(array, AXES, pairs)  29.6 us
    ppermute x3, waiting for transfers between devices, to_section(): return lax.ppermute(array, AXES, pairs)  28.7 us
  transfers between devices with their start and end apart: 75, of which 16 were waited for; matrix products, arithmetic and copies ran while one was open for 40% of the time, Pallas kernels for 0%

profile of v2, /device:TPU:0, one launch (start us, length us, event | category | flops | bytes accessed | tf_op | source)
XLA Modules:
  0.0 745.5 jit_solution(9556097087921920804)
XLA Ops:
  4.0 4.8 collective-permute-start
  8.9 3.4 collective-permute-start.1
  14.2 3.9 collective-permute-start.8
  18.1 3.4 collective-permute-start.9
  27.6 3.0 broadcast.572.clone
  34.7 8.9 %dynamic_update_slice.99 = bf16[640,1664]{0,1:T(8,128)(2,1)} dynamic-update-slice(bf16[640,1664]{0,1:T(8,128)(2,1)} %broadcast.563.clone, bf16[160,1664]{0,1:T(8,128)(2,1)S(1)} %copy.248, s32[]{:T(128)S(6)} %select_n.421, s32[]{:T(128)} %constant.141.clone.1) | dynamic-update-slice | bytes 1064964 | tf_op jit(solution)/shard_map/dynamic_update_slice | solution.py:284
  47.0 4.4 collective-permute-start.14
  53.6 3.4 collective-permute-start.15
  57.1 3.6 collective-permute-start.16
  62.1 10.0 %dynamic_update_slice.100 = bf16[640,1664]{0,1:T(8,128)(2,1)} dynamic-update-slice(bf16[640,1664]{0,1:T(8,128)(2,1)} %dynamic_update_slice.99, bf16[160,1664]{0,1:T(8,128)(2,1)S(1)} %copy.249, s32[]{:T(128)S(6)} %select_n.422, s32[]{:T(128)} %constant.141.clone.1) | dynamic-update-slice | bytes 1064964 | tf_op jit(solution)/shard_map/dynamic_update_slice | solution.py:284
  73.5 9.9 %dynamic_update_slice.101 = bf16[640,1664]{0,1:T(8,128)(2,1)} dynamic-update-slice(bf16[640,1664]{0,1:T(8,128)(2,1)} %dynamic_update_slice.100, bf16[160,1664]{0,1:T(8,128)(2,1)S(1)} %copy.250, s32[]{:T(128)S(6)} %select_n.423, s32[]{:T(128)} %constant.141.clone.1) | dynamic-update-slice | bytes 1064964 | tf_op jit(solution)/shard_map/dynamic_update_slice | solution.py:284
  84.7 9.3 %dynamic_update_slice.102 = bf16[640,1664]{0,1:T(8,128)(2,1)} dynamic-update-slice(bf16[640,1664]{0,1:T(8,128)(2,1)} %dynamic_update_slice.101, bf16[160,1664]{0,1:T(8,128)(2,1)S(1)} %copy.251, s32[]{:T(128)S(6)} %select_n.424, s32[]{:T(128)} %constant.141.clone.1) | dynamic-update-slice | bytes 1064964 | tf_op jit(solution)/shard_map/dynamic_update_slice | solution.py:284
  100.5 4.1 collective-permute-start.3
  104.6 4.5 collective-permute-start.4
  119.5 3.2 collective-permute-start.12
  125.3 4.1 collective-permute-start.7
  137.4 3.1 collective-permute-start.6
  148.3 2.7 fusion.277
  159.9 2.9 broadcast.572
  162.9 2.5 constant_dynamic-update-slice_fusion.89
  167.4 10.9 %dynamic_update_slice.116 = bf16[640,1664]{0,1:T(8,128)(2,1)S(1)} dynamic-update-slice(bf16[640,1664]{0,1:T(8,128)(2,1)S(1)} %broadcast.563, bf16[160,1664]{0,1:T(8,128)(2,1)} %copy.257, s32[]{:T(128)S(6)} %select_n.421, s32[]{:T(128)} %constant.141.clone.1) | dynamic-update-slice | bytes 1064964 | tf_op jit(solution)/shard_map/dynamic_update_slice | solution.py:284
  183.6 4.3 collective-permute-start.13
  194.9 2.6 constant_dynamic-update-slice_fusion.100
  199.0 2.5 constant_dynamic-update-slice_fusion.99
  201.5 16.8 %collective-permute-done.13 = bf16[160,4096]{1,0:T(8,128)(2,1)S(1)} collective-permute-done((bf16[160,4096]{1,0:T(8,128)(2,1)}, bf16[160,4096]{1,0:T(8,128)(2,1)S(1)}, u32[]{:S(2)}, u32[]{:S(2)}) %collective-permute-start.13) | collective-permute-done | bytes 1310752 | tf_op jit(solution)/shard_map/ppermute | solution.py:74
  221.0 3.5 fusion.283
  224.8 2.9 multiply_reduce_fusion.15
  233.0 10.0 %dynamic_update_slice.117 = bf16[640,1664]{0,1:T(8,128)(2,1)} dynamic-update-slice(bf16[640,1664]{0,1:T(8,128)(2,1)} %copy-done.6, bf16[160,1664]{0,1:T(8,128)(2,1)S(1)} %copy.258, s32[]{:T(128)S(6)} %select_n.422, s32[]{:T(128)} %constant.141.clone.1) | dynamic-update-slice | bytes 1064964 | tf_op jit(solution)/shard_map/dynamic_update_slice | solution.py:284
  245.7 9.9 %dynamic_update_slice.118 = bf16[640,1664]{0,1:T(8,128)(2,1)} dynamic-update-slice(bf16[640,1664]{0,1:T(8,128)(2,1)} %dynamic_update_slice.117, bf16[160,1664]{0,1:T(8,128)(2,1)S(1)} %copy.259, s32[]{:T(128)S(6)} %select_n.423, s32[]{:T(128)} %constant.141.clone.1) | dynamic-update-slice | bytes 1064964 | tf_op jit(solution)/shard_map/dynamic_update_slice | solution.py:284
  256.9 9.3 %dynamic_update_slice.119 = bf16[640,1664]{0,1:T(8,128)(2,1)} dynamic-update-slice(bf16[640,1664]{0,1:T(8,128)(2,1)} %dynamic_update_slice.118, bf16[160,1664]{0,1:T(8,128)(2,1)S(1)} %copy.260, s32[]{:T(128)S(6)} %select_n.424, s32[]{:T(128)} %constant.141.clone.1) | dynamic-update-slice | bytes 1064964 | tf_op jit(solution)/shard_map/dynamic_update_slice | solution.py:284
  296.6 2.7 fusion.280
  302.4 2.6 constant_dynamic-update-slice_fusion.88
  304.9 2.5 constant_dynamic-update-slice_fusion.87
  307.5 2.5 constant_dynamic-update-slice_fusion.86
  310.0 3.5 fusion.284
  313.9 2.6 multiply_reduce_fusion.12
  317.5 3.2 fusion.53
  320.7 5.4 multiply_reduce_fusion.8
  403.7 28.7 %collective-permute-done.41 = bf16[2,64,640]{2,1,0:T(8,128)(2,1)S(1)} collective-permute-done((bf16[2,64,640]{2,1,0:T(8,128)(2,1)S(1)}, bf16[2,64,640]{2,1,0:T(8,128)(2,1)S(1)}, u32[]{:S(2)}, u32[]{:S(2)}) %collective-permute-start.41) | collective-permute-done | bytes 163872 | tf_op jit(solution)/shard_map/ppermute | solution.py:311
  433.3 3.2 fusion.46
  448.8 5.0 multiply_reduce_fusion.4
  487.3 2.9 collective-permute-start.43
  491.0 4.1 collective-permute-start.44
  508.2 3.0 collective-permute-done.45
  544.7 2.5 collective-permute-start.47
  547.2 3.0 collective-permute-start.48
  550.2 4.0 collective-permute-start.49
  556.4 12.5 %collective-permute-done.47 = bf16[160,2688]{1,0:T(8,128)(2,1)S(1)} collective-permute-done((bf16[160,2688]{1,0:T(8,128)(2,1)S(1)}, bf16[160,2688]{1,0:T(8,128)(2,1)S(1)}, u32[]{:S(2)}, u32[]{:S(2)}) %collective-permute-start.47) | collective-permute-done | bytes 860192 | tf_op jit(solution)/shard_map/ppermute | solution.py:74
  569.7 19.0 %collective-permute-done.48 = bf16[160,2688]{1,0:T(8,128)(2,1)S(1)} collective-permute-done((bf16[160,2688]{1,0:T(8,128)(2,1)S(1)}, bf16[160,2688]{1,0:T(8,128)(2,1)S(1)}, u32[]{:S(2)}, u32[]{:S(2)}) %collective-permute-start.48) | collective-permute-done | bytes 860192 | tf_op jit(solution)/shard_map/ppermute | solution.py:74
  591.6 4.4 collective-permute-start.50
  598.0 3.3 collective-permute-start.61
  601.4 6.1 collective-permute-done.50
  608.3 2.8 collective-permute-start.62
  611.3 4.0 collective-permute-start.63
  617.9 3.4 add_convert_fusion
  621.3 3.2 collective-permute-done.61
  625.2 30.7 %collective-permute-done.62 = bf16[160,6144]{1,0:T(8,128)(2,1)S(1)} collective-permute-done((bf16[160,6144]{1,0:T(8,128)(2,1)S(1)}, bf16[160,6144]{1,0:T(8,128)(2,1)S(1)}, u32[]{:S(2)}, u32[]{:S(2)}) %collective-permute-start.62) | collective-permute-done | bytes 1966112 | tf_op jit(solution)/shard_map/ppermute | solution.py:74
  655.9 3.3 add_convert_fusion.1
  661.3 4.4 collective-permute-start.64
  665.7 5.4 collective-permute-done.52
  673.4 11.1 %collective-permute-done.53 = bf16[160,1536]{1,0:T(8,128)(2,1)S(1)} collective-permute-done((bf16[160,1536]{1,0:T(8,128)(2,1)S(1)}, bf16[160,1536]{1,0:T(8,128)(2,1)S(1)}, u32[]{:S(2)}, u32[]{:S(2)}) %collective-permute-start.53) | collective-permute-done | bytes 491552 | tf_op jit(solution)/shard_map/ppermute | solution.py:82
  689.4 4.4 collective-permute-start.65
  711.6 13.0 %collective-permute-done.66 = bf16[160,1536]{1,0:T(8,128)(2,1)S(1)} collective-permute-done((bf16[160,1536]{1,0:T(8,128)(2,1)S(1)}, bf16[160,1536]{1,0:T(8,128)(2,1)S(1)}, u32[]{:S(2)}, u32[]{:S(2)}) %collective-permute-start.66) | collective-permute-done | bytes 491552 | tf_op jit(solution)/shard_map/ppermute | solution.py:82
  728.1 12.7 %collective-permute-done.67 = bf16[160,3072]{1,0:T(8,128)(2,1)S(1)} collective-permute-done((bf16[160,3072]{1,0:T(8,128)(2,1)S(1)}, bf16[160,3072]{1,0:T(8,128)(2,1)S(1)}, u32[]{:S(2)}, u32[]{:S(2)}) %collective-permute-start.67) | collective-permute-done | bytes 983072 | tf_op jit(solution)/shard_map/ppermute | solution.py:82
  (903 shorter events, 347.5 us)
Async XLA Ops:
  4.0 53.1 %collective-permute-start = (bf16[160,1664]{1,0:T(8,128)(2,1)S(1)}, bf16[160,1664]{1,0:T(8,128)(2,1)}, u32[]{:S(2)}, u32[]{:S(2)}) collective-permute-start(bf16[160,1664]{1,0:T(8,128)(2,1)S(1)} %fusion.55), channel_id=1, source_target_pairs={{0,1},{1,0},{2,3},{3,2},{4,5},{5,4},{6,7},{7,6},{8,9},{9,8},{10,11... | collective-permute-start | bytes 1597448 | tf_op jit(solution)/shard_map/ppermute | solution.py:74
  8.9 63.3 %collective-permute-start.1 = (bf16[160,1664]{1,0:T(8,128)(2,1)S(1)}, bf16[160,1664]{1,0:T(8,128)(2,1)}, u32[]{:S(2)}, u32[]{:S(2)}) collective-permute-start(bf16[160,1664]{1,0:T(8,128)(2,1)S(1)} %fusion.55), channel_id=1, source_target_pairs={{0,2},{1,3},{2,0},{3,1},{4,6},{5,7},{6,4},{7,5},{8,10},{9,11},{10,... | collective-permute-start | bytes 1597448 | tf_op jit(solution)/shard_map/ppermute | solution.py:74
  12.3 71.1 %collective-permute-start.2 = (bf16[160,1664]{1,0:T(8,128)(2,1)S(1)}, bf16[160,1664]{1,0:T(8,128)(2,1)}, u32[]{:S(2)}, u32[]{:S(2)}) collective-permute-start(bf16[160,1664]{1,0:T(8,128)(2,1)S(1)} %fusion.55), channel_id=1, source_target_pairs={{0,3},{1,2},{2,1},{3,0},{4,7},{5,6},{6,5},{7,4},{8,11},{9,10},{10,... | collective-permute-start | bytes 1597448 | tf_op jit(solution)/shard_map/ppermute | solution.py:74
  14.2 29.4 %collective-permute-start.8 = (bf16[256,640]{1,0:T(8,128)(2,1)}, bf16[256,640]{1,0:T(8,128)(2,1)}, u32[]{:S(2)}, u32[]{:S(2)}) collective-permute-start(bf16[256,640]{1,0:T(8,128)(2,1)} %bitcast.39), channel_id=1, source_target_pairs={{0,1},{1,0},{2,3},{3,2},{4,5},{5,4},{6,7},{7,6},{8,9},{9,8},{10,11... | collective-permute-start | bytes 983048 | tf_op jit(solution)/shard_map/ppermute | solution.py:74
  18.1 28.9 %collective-permute-start.9 = (bf16[256,640]{1,0:T(8,128)(2,1)}, bf16[256,640]{1,0:T(8,128)(2,1)S(1)}, u32[]{:S(2)}, u32[]{:S(2)}) collective-permute-start(bf16[256,640]{1,0:T(8,128)(2,1)} %bitcast.39), channel_id=1, source_target_pairs={{0,2},{1,3},{2,0},{3,1},{4,6},{5,7},{6,4},{7,5},{8,10},{9,11},{10,... | collective-permute-start | bytes 983048 | tf_op jit(solution)/shard_map/ppermute | solution.py:74
  43.6 10.1 %collective-permute-start.10 = (bf16[256,640]{1,0:T(8,128)(2,1)}, bf16[256,640]{1,0:T(8,128)(2,1)S(1)}, u32[]{:S(2)}, u32[]{:S(2)}) collective-permute-start(bf16[256,640]{1,0:T(8,128)(2,1)} %bitcast.39), channel_id=1, source_target_pairs={{0,3},{1,2},{2,1},{3,0},{4,7},{5,6},{6,5},{7,4},{8,11},{9,10},{10,... | collective-permute-start | bytes 983048 | tf_op jit(solution)/shard_map/ppermute | solution.py:74
  47.0 78.3 %collective-permute-start.14 = (bf16[512,640]{1,0:T(8,128)(2,1)}, bf16[512,640]{1,0:T(8,128)(2,1)}, u32[]{:S(2)}, u32[]{:S(2)}) collective-permute-start(bf16[512,640]{1,0:T(8,128)(2,1)} %bitcast.42), channel_id=1, source_target_pairs={{0,1},{1,0},{2,3},{3,2},{4,5},{5,4},{6,7},{7,6},{8,9},{9,8},{10,11... | collective-permute-start | bytes 1966088 | tf_op jit(solution)/shard_map/ppermute | solution.py:74
  53.6 77.8 %collective-permute-start.15 = (bf16[512,640]{1,0:T(8,128)(2,1)}, bf16[512,640]{1,0:T(8,128)(2,1)}, u32[]{:S(2)}, u32[]{:S(2)}) collective-permute-start(bf16[512,640]{1,0:T(8,128)(2,1)} %bitcast.42), channel_id=1, source_target_pairs={{0,2},{1,3},{2,0},{3,1},{4,6},{5,7},{6,4},{7,5},{8,10},{9,11},{10,... | collective-permute-start | bytes 1966088 | tf_op jit(solution)/shard_map/ppermute | solution.py:74
  57.1 78.3 %collective-permute-start.16 = (bf16[512,640]{1,0:T(8,128)(2,1)}, bf16[512,640]{1,0:T(8,128)(2,1)}, u32[]{:S(2)}, u32[]{:S(2)}) collective-permute-start(bf16[512,640]{1,0:T(8,128)(2,1)} %bitcast.42), channel_id=1, source_target_pairs={{0,3},{1,2},{2,1},{3,0},{4,7},{5,6},{6,5},{7,4},{8,11},{9,10},{10,... | collective-permute-start | bytes 1966088 | tf_op jit(solution)/shard_map/ppermute | solution.py:74
  100.5 15.6 %collective-permute-start.3 = (bf16[2,64,512]{2,1,0:T(8,128)(2,1)S(1)}, bf16[2,64,512]{2,1,0:T(8,128)(2,1)}, u32[]{:S(2)}, u32[]{:S(2)}) collective-permute-start(bf16[2,64,512]{2,1,0:T(8,128)(2,1)S(1)} %bitcast.485), channel_id=1, source_target_pairs={{0,4},{1,5},{2,6},{3,7},{4,8},{5,9},{6,10},{7,11},{8,12},{9,13},{1... | collective-permute-start | bytes 393224 | tf_op jit(solution)/shard_map/ppermute | solution.py:66
  104.6 14.9 %collective-permute-start.4 = (bf16[2,64,512]{2,1,0:T(8,128)(2,1)S(1)}, bf16[2,64,512]{2,1,0:T(8,128)(2,1)}, u32[]{:S(2)}, u32[]{:S(2)}) collective-permute-start(bf16[2,64,512]{2,1,0:T(8,128)(2,1)S(1)} %bitcast.486), channel_id=1, source_target_pairs={{0,8},{1,9},{2,10},{3,11},{4,12},{5,13},{6,14},{7,15}} | collective-permute-start | bytes 393224 | tf_op jit(solution)/shard_map/ppermute | solution.py:66
  116.1 77.4 %collective-permute-start.11 = (bf16[160,4096]{1,0:T(8,128)(2,1)}, bf16[160,4096]{1,0:T(8,128)(2,1)}, u32[]{:S(2)}, u32[]{:S(2)}) collective-permute-start(bf16[160,4096]{1,0:T(8,128)(2,1)} %get-tuple-element.32), channel_id=1, source_target_pairs={{0,1},{1,0},{2,3},{3,2},{4,5},{5,4},{6,7},{7,6},{8,9},{9,8},{10,11... | collective-permute-start | bytes 3932168 | tf_op jit(solution)/shard_map/ppermute | solution.py:74
  119.5 78.0 %collective-permute-start.12 = (bf16[160,4096]{1,0:T(8,128)(2,1)}, bf16[160,4096]{1,0:T(8,128)(2,1)}, u32[]{:S(2)}, u32[]{:S(2)}) collective-permute-start(bf16[160,4096]{1,0:T(8,128)(2,1)} %get-tuple-element.32), channel_id=1, source_target_pairs={{0,2},{1,3},{2,0},{3,1},{4,6},{5,7},{6,4},{7,5},{8,10},{9,11},{10,... | collective-permute-start | bytes 3932168 | tf_op jit(solution)/shard_map/ppermute | solution.py:74
  125.3 15.2 %collective-permute-start.7 = (bf16[2,2,64,512]{3,2,1,0:T(8,128)(2,1)S(1)}, bf16[2,2,64,512]{3,2,1,0:T(8,128)(2,1)S(1)}, u32[]{:S(2)}, u32[]{:S(2)}) collective-permute-start(bf16[2,2,64,512]{3,2,1,0:T(8,128)(2,1)S(1)} %get-tuple-element.253), channel_id=1, source_target_pairs={{0,3},{1,2},{2,1},{3,0},{4,7},{5,6},{6,5},{7,4},{8,11},{9,10},{10,... | collective-permute-start | bytes 786440 | tf_op jit(solution)/shard_map/ppermute | solution.py:74
  133.5 8.4 %collective-permute-start.5 = (bf16[2,2,64,512]{3,2,1,0:T(8,128)(2,1)S(1)}, bf16[2,2,64,512]{3,2,1,0:T(8,128)(2,1)S(1)}, u32[]{:S(2)}, u32[]{:S(2)}) collective-permute-start(bf16[2,2,64,512]{3,2,1,0:T(8,128)(2,1)S(1)} %get-tuple-element.255), channel_id=1, source_target_pairs={{0,1},{1,0},{2,3},{3,2},{4,5},{5,4},{6,7},{7,6},{8,9},{9,8},{10,11... | collective-permute-start | bytes 786440 | tf_op jit(solution)/shard_map/ppermute | solution.py:74
  137.4 8.3 %collective-permute-start.6 = (bf16[2,2,64,512]{3,2,1,0:T(8,128)(2,1)S(1)}, bf16[2,2,64,512]{3,2,1,0:T(8,128)(2,1)S(1)}, u32[]{:S(2)}, u32[]{:S(2)}) collective-permute-start(bf16[2,2,64,512]{3,2,1,0:T(8,128)(2,1)S(1)} %get-tuple-element.254), channel_id=1, source_target_pairs={{0,2},{1,3},{2,0},{3,1},{4,6},{5,7},{6,4},{7,5},{8,10},{9,11},{10,... | collective-permute-start | bytes 786440 | tf_op jit(solution)/shard_map/ppermute | solution.py:74
  140.6 14.9 %collective-permute-start.18 = (bf16[1,16,64]{2,1,0:T(8,128)(2,1)S(1)}, bf16[1,16,64]{2,1,0:T(8,128)(2,1)S(1)}, u32[]{:S(2)}, u32[]{:S(2)}) collective-permute-start(bf16[1,16,64]{2,1,0:T(8,128)(2,1)S(1)} %slice.832), channel_id=1, source_target_pairs={{0,16},{1,17},{2,18},{3,19},{4,20},{5,21},{6,22},{7,23},{8,24},{9,... | collective-permute-start | bytes 6152 | tf_op jit(solution)/shard_map/ppermute | solution.py:311
  155.5 28.0 %collective-permute-start.27 = (bf16[256,640]{1,0:T(8,128)(2,1)}, bf16[256,640]{1,0:T(8,128)(2,1)}, u32[]{:S(2)}, u32[]{:S(2)}) collective-permute-start(bf16[256,640]{1,0:T(8,128)(2,1)} %bitcast.39), channel_id=1, source_target_pairs={{16,17},{17,16},{18,19},{19,18},{20,21},{21,20},{22,23},{23,22},{2... | collective-permute-start | bytes 983048 | tf_op jit(solution)/shard_map/ppermute | solution.py:74
  156.9 32.0 %collective-permute-start.28 = (bf16[256,640]{1,0:T(8,128)(2,1)}, bf16[256,640]{1,0:T(8,128)(2,1)}, u32[]{:S(2)}, u32[]{:S(2)}) collective-permute-start(bf16[256,640]{1,0:T(8,128)(2,1)} %bitcast.39), channel_id=1, source_target_pairs={{16,18},{17,19},{18,16},{19,17},{20,22},{21,23},{22,20},{23,21},{2... | collective-permute-start | bytes 983048 | tf_op jit(solution)/shard_map/ppermute | solution.py:74
  158.3 33.4 %collective-permute-start.29 = (bf16[256,640]{1,0:T(8,128)(2,1)}, bf16[256,640]{1,0:T(8,128)(2,1)}, u32[]{:S(2)}, u32[]{:S(2)}) collective-permute-start(bf16[256,640]{1,0:T(8,128)(2,1)} %bitcast.39), channel_id=1, source_target_pairs={{16,19},{17,18},{18,17},{19,16},{20,23},{21,22},{22,21},{23,20},{2... | collective-permute-start | bytes 983048 | tf_op jit(solution)/shard_map/ppermute | solution.py:74
  183.6 34.7 %collective-permute-start.13 = (bf16[160,4096]{1,0:T(8,128)(2,1)}, bf16[160,4096]{1,0:T(8,128)(2,1)S(1)}, u32[]{:S(2)}, u32[]{:S(2)}) collective-permute-start(bf16[160,4096]{1,0:T(8,128)(2,1)} %get-tuple-element.32), channel_id=1, source_target_pairs={{0,3},{1,2},{2,1},{3,0},{4,7},{5,6},{6,5},{7,4},{8,11},{9,10},{10,... | collective-permute-start | bytes 3932168 | tf_op jit(solution)/shard_map/ppermute | solution.py:74
  188.9 113.4 %collective-permute-start.30 = (bf16[160,4096]{1,0:T(8,128)(2,1)}, bf16[160,4096]{1,0:T(8,128)(2,1)}, u32[]{:S(2)}, u32[]{:S(2)}) collective-permute-start(bf16[160,4096]{1,0:T(8,128)(2,1)} %get-tuple-element.32), channel_id=1, source_target_pairs={{16,17},{17,16},{18,19},{19,18},{20,21},{21,20},{22,23},{23,22},{2... | collective-permute-start | bytes 3932168 | tf_op jit(solution)/shard_map/ppermute | solution.py:74
  191.7 37.6 %collective-permute-start.19 = (bf16[160,1664]{1,0:T(8,128)(2,1)S(1)}, bf16[160,1664]{1,0:T(8,128)(2,1)S(1)}, u32[]{:S(2)}, u32[]{:S(2)}) collective-permute-start(bf16[160,1664]{1,0:T(8,128)(2,1)S(1)} %dynamic_update_slice.115), channel_id=1, source_target_pairs={{16,17},{17,16},{18,19},{19,18},{20,21},{21,20},{22,23},{23,22},{2... | collective-permute-start | bytes 1597448 | tf_op jit(solution)/shard_map/ppermute | solution.py:74
  193.4 49.6 %collective-permute-start.20 = (bf16[160,1664]{1,0:T(8,128)(2,1)S(1)}, bf16[160,1664]{1,0:T(8,128)(2,1)}, u32[]{:S(2)}, u32[]{:S(2)}) collective-permute-start(bf16[160,1664]{1,0:T(8,128)(2,1)S(1)} %dynamic_update_slice.115), channel_id=1, source_target_pairs={{16,18},{17,19},{18,16},{19,17},{20,22},{21,23},{22,20},{23,21},{2... | collective-permute-start | bytes 1597448 | tf_op jit(solution)/shard_map/ppermute | solution.py:74
  197.5 58.1 %collective-permute-start.21 = (bf16[160,1664]{1,0:T(8,128)(2,1)S(1)}, bf16[160,1664]{1,0:T(8,128)(2,1)}, u32[]{:S(2)}, u32[]{:S(2)}) collective-permute-start(bf16[160,1664]{1,0:T(8,128)(2,1)S(1)} %dynamic_update_slice.115), channel_id=1, source_target_pairs={{16,19},{17,18},{18,17},{19,16},{20,23},{21,22},{22,21},{23,20},{2... | collective-permute-start | bytes 1597448 | tf_op jit(solution)/shard_map/ppermute | solution.py:74
  218.3 64.9 %collective-permute-start.33 = (bf16[512,640]{1,0:T(8,128)(2,1)}, bf16[512,640]{1,0:T(8,128)(2,1)}, u32[]{:S(2)}, u32[]{:S(2)}) collective-permute-start(bf16[512,640]{1,0:T(8,128)(2,1)} %bitcast.42), channel_id=1, source_target_pairs={{16,17},{17,16},{18,19},{19,18},{20,21},{21,20},{22,23},{23,22},{2... | collective-permute-start | bytes 1966088 | tf_op jit(solution)/shard_map/ppermute | solution.py:74
  230.1 55.9 %collective-permute-start.34 = (bf16[512,640]{1,0:T(8,128)(2,1)}, bf16[512,640]{1,0:T(8,128)(2,1)}, u32[]{:S(2)}, u32[]{:S(2)}) collective-permute-start(bf16[512,640]{1,0:T(8,128)(2,1)} %bitcast.42), channel_id=1, source_target_pairs={{16,18},{17,19},{18,16},{19,17},{20,22},{21,23},{22,20},{23,21},{2... | collective-permute-start | bytes 1966088 | tf_op jit(solution)/shard_map/ppermute | solution.py:74
  243.0 24.3 %collective-permute-start.17 = (bf16[2,64,640]{2,1,0:T(8,128)(2,1)}, bf16[2,64,640]{2,1,0:T(8,128)(2,1)S(1)}, u32[]{:S(2)}, u32[]{:S(2)}) collective-permute-start(bf16[2,64,640]{2,1,0:T(8,128)(2,1)} %bitcast.503), channel_id=1, source_target_pairs={{0,16},{1,17},{2,18},{3,19},{4,20},{5,21},{6,22},{7,23},{8,24},{9,... | collective-permute-start | bytes 491528 | tf_op jit(solution)/shard_map/ppermute | solution.py:311
  278.5 11.4 %collective-permute-start.35 = (bf16[512,640]{1,0:T(8,128)(2,1)}, bf16[512,640]{1,0:T(8,128)(2,1)S(1)}, u32[]{:S(2)}, u32[]{:S(2)}) collective-permute-start(bf16[512,640]{1,0:T(8,128)(2,1)} %bitcast.42), channel_id=1, source_target_pairs={{16,19},{17,18},{18,17},{19,16},{20,23},{21,22},{22,21},{23,20},{2... | collective-permute-start | bytes 1966088 | tf_op jit(solution)/shard_map/ppermute | solution.py:74
  279.8 25.1 %collective-permute-start.31 = (bf16[160,4096]{1,0:T(8,128)(2,1)}, bf16[160,4096]{1,0:T(8,128)(2,1)}, u32[]{:S(2)}, u32[]{:S(2)}) collective-permute-start(bf16[160,4096]{1,0:T(8,128)(2,1)} %get-tuple-element.32), channel_id=1, source_target_pairs={{16,18},{17,19},{18,16},{19,17},{20,22},{21,23},{22,20},{23,21},{2... | collective-permute-start | bytes 3932168 | tf_op jit(solution)/shard_map/ppermute | solution.py:74
  283.3 8.1 %collective-permute-start.24 = (bf16[2,2,64,512]{3,2,1,0:T(8,128)(2,1)S(1)}, bf16[2,2,64,512]{3,2,1,0:T(8,128)(2,1)S(1)}, u32[]{:S(2)}, u32[]{:S(2)}) collective-permute-start(bf16[2,2,64,512]{3,2,1,0:T(8,128)(2,1)S(1)} %get-tuple-element.251), channel_id=1, source_target_pairs={{16,17},{17,16},{18,19},{19,18},{20,21},{21,20},{22,23},{23,22},{2... | collective-permute-start | bytes 786440 | tf_op jit(solution)/shard_map/ppermute | solution.py:74
  286.0 21.5 %collective-permute-start.32 = (bf16[160,4096]{1,0:T(8,128)(2,1)}, bf16[160,4096]{1,0:T(8,128)(2,1)}, u32[]{:S(2)}, u32[]{:S(2)}) collective-permute-start(bf16[160,4096]{1,0:T(8,128)(2,1)} %get-tuple-element.32), channel_id=1, source_target_pairs={{16,19},{17,18},{18,17},{19,16},{20,23},{21,22},{22,21},{23,20},{2... | collective-permute-start | bytes 3932168 | tf_op jit(solution)/shard_map/ppermute | solution.py:74
  355.9 22.7 %collective-permute-start.36 = (bf16[2,2,64,512]{3,2,1,0:T(8,128)(2,1)}, bf16[2,2,64,512]{3,2,1,0:T(8,128)(2,1)}, u32[]{:S(2)}, u32[]{:S(2)}) collective-permute-start(bf16[2,2,64,512]{3,2,1,0:T(8,128)(2,1)} %pad_maximum_fusion.21), channel_id=1, source_target_pairs={{16,17},{17,16},{18,19},{19,18},{20,21},{21,20},{22,23},{23,22},{2... | collective-permute-start | bytes 786440 | tf_op jit(solution)/shard_map/ppermute | solution.py:74
  358.1 21.4 %collective-permute-start.37 = (bf16[2,2,64,512]{3,2,1,0:T(8,128)(2,1)}, bf16[2,2,64,512]{3,2,1,0:T(8,128)(2,1)}, u32[]{:S(2)}, u32[]{:S(2)}) collective-permute-start(bf16[2,2,64,512]{3,2,1,0:T(8,128)(2,1)} %pad_maximum_fusion.22), channel_id=1, source_target_pairs={{16,18},{17,19},{18,16},{19,17},{20,22},{21,23},{22,20},{23,21},{2... | collective-permute-start | bytes 786440 | tf_op jit(solution)/shard_map/ppermute | solution.py:74
  360.2 20.4 %collective-permute-start.38 = (bf16[2,2,64,512]{3,2,1,0:T(8,128)(2,1)}, bf16[2,2,64,512]{3,2,1,0:T(8,128)(2,1)}, u32[]{:S(2)}, u32[]{:S(2)}) collective-permute-start(bf16[2,2,64,512]{3,2,1,0:T(8,128)(2,1)} %pad_maximum_fusion.23), channel_id=1, source_target_pairs={{16,19},{17,18},{18,17},{19,16},{20,23},{21,22},{22,21},{23,20},{2... | collective-permute-start | bytes 786440 | tf_op jit(solution)/shard_map/ppermute | solution.py:74
  401.7 30.7 %collective-permute-start.41 = (bf16[2,64,640]{2,1,0:T(8,128)(2,1)S(1)}, bf16[2,64,640]{2,1,0:T(8,128)(2,1)S(1)}, u32[]{:S(2)}, u32[]{:S(2)}) collective-permute-start(bf16[2,64,640]{2,1,0:T(8,128)(2,1)S(1)} %bitcast.504), channel_id=1, source_target_pairs={{16,0},{17,1},{18,2},{19,3},{20,4},{21,5},{22,6},{23,7},{24,8},{25... | collective-permute-start | bytes 491528 | tf_op jit(solution)/shard_map/ppermute | solution.py:311
  466.5 144.8 %collective-permute-start.68 = (bf16[160,6144]{1,0:T(8,128)(2,1)}, bf16[160,6144]{1,0:T(8,128)(2,1)}, u32[]{:S(2)}, u32[]{:S(2)}) collective-permute-start(bf16[160,6144]{1,0:T(8,128)(2,1)} %constant_dynamic-update-slice_fusion.18), channel_id=1, source_target_pairs={{16,17},{17,16},{18,19},{19,18},{20,21},{21,20},{22,23},{23,22},{2... | collective-permute-start | bytes 5898248 | tf_op jit(solution)/shard_map/ppermute | solution.py:74
  468.6 146.7 %collective-permute-start.69 = (bf16[160,6144]{1,0:T(8,128)(2,1)}, bf16[160,6144]{1,0:T(8,128)(2,1)}, u32[]{:S(2)}, u32[]{:S(2)}) collective-permute-start(bf16[160,6144]{1,0:T(8,128)(2,1)} %constant_dynamic-update-slice_fusion.22), channel_id=1, source_target_pairs={{16,18},{17,19},{18,16},{19,17},{20,22},{21,23},{22,20},{23,21},{2... | collective-permute-start | bytes 5898248 | tf_op jit(solution)/shard_map/ppermute | solution.py:74
  484.4 15.7 %collective-permute-start.42 = (bf16[2,2,64,512]{3,2,1,0:T(8,128)(2,1)}, bf16[2,2,64,512]{3,2,1,0:T(8,128)(2,1)S(1)}, u32[]{:S(2)}, u32[]{:S(2)}) collective-permute-start(bf16[2,2,64,512]{3,2,1,0:T(8,128)(2,1)} %pad_maximum_fusion.24), channel_id=1, source_target_pairs={{0,1},{1,0},{2,3},{3,2},{4,5},{5,4},{6,7},{7,6},{8,9},{9,8},{10,11... | collective-permute-start | bytes 786440 | tf_op jit(solution)/shard_map/ppermute | solution.py:74
  487.3 14.4 %collective-permute-start.43 = (bf16[2,2,64,512]{3,2,1,0:T(8,128)(2,1)}, bf16[2,2,64,512]{3,2,1,0:T(8,128)(2,1)}, u32[]{:S(2)}, u32[]{:S(2)}) collective-permute-start(bf16[2,2,64,512]{3,2,1,0:T(8,128)(2,1)} %pad_maximum_fusion.25), channel_id=1, source_target_pairs={{0,2},{1,3},{2,0},{3,1},{4,6},{5,7},{6,4},{7,5},{8,10},{9,11},{10,... | collective-permute-start | bytes 786440 | tf_op jit(solution)/shard_map/ppermute | solution.py:74
  491.0 11.8 %collective-permute-start.44 = (bf16[2,2,64,512]{3,2,1,0:T(8,128)(2,1)}, bf16[2,2,64,512]{3,2,1,0:T(8,128)(2,1)}, u32[]{:S(2)}, u32[]{:S(2)}) collective-permute-start(bf16[2,2,64,512]{3,2,1,0:T(8,128)(2,1)} %pad_maximum_fusion.26), channel_id=1, source_target_pairs={{0,3},{1,2},{2,1},{3,0},{4,7},{5,6},{6,5},{7,4},{8,11},{9,10},{10,... | collective-permute-start | bytes 786440 | tf_op jit(solution)/shard_map/ppermute | solution.py:74
  500.1 44.6 %collective-permute-start.54 = (bf16[160,2688]{1,0:T(8,128)(2,1)}, bf16[160,2688]{1,0:T(8,128)(2,1)}, u32[]{:S(2)}, u32[]{:S(2)}) collective-permute-start(bf16[160,2688]{1,0:T(8,128)(2,1)} %constant_dynamic-update-slice_fusion.30), channel_id=1, source_target_pairs={{16,17},{17,16},{18,19},{19,18},{20,21},{21,20},{22,23},{23,22},{2... | collective-permute-start | bytes 2580488 | tf_op jit(solution)/shard_map/ppermute | solution.py:74
  505.3 8.7 %collective-permute-start.46 = (bf16[2,64,512]{2,1,0:T(8,128)(2,1)S(1)}, bf16[2,64,512]{2,1,0:T(8,128)(2,1)S(1)}, u32[]{:S(2)}, u32[]{:S(2)}) collective-permute-start(bf16[2,64,512]{2,1,0:T(8,128)(2,1)S(1)} %get-tuple-element.174), channel_id=1, source_target_pairs={{8,0},{9,1},{10,2},{11,3},{12,4},{13,5},{14,6},{15,7}} | collective-permute-start | bytes 393224 | tf_op jit(solution)/shard_map/ppermute | solution.py:66
  511.2 36.0 %collective-permute-start.55 = (bf16[160,2688]{1,0:T(8,128)(2,1)}, bf16[160,2688]{1,0:T(8,128)(2,1)}, u32[]{:S(2)}, u32[]{:S(2)}) collective-permute-start(bf16[160,2688]{1,0:T(8,128)(2,1)} %constant_dynamic-update-slice_fusion.35), channel_id=1, source_target_pairs={{16,18},{17,19},{18,16},{19,17},{20,22},{21,23},{22,20},{23,21},{2... | collective-permute-start | bytes 2580488 | tf_op jit(solution)/shard_map/ppermute | solution.py:74
  514.1 36.1 %collective-permute-start.56 = (bf16[160,2688]{1,0:T(8,128)(2,1)}, bf16[160,2688]{1,0:T(8,128)(2,1)}, u32[]{:S(2)}, u32[]{:S(2)}) collective-permute-start(bf16[160,2688]{1,0:T(8,128)(2,1)} %constant_dynamic-update-slice_fusion.40), channel_id=1, source_target_pairs={{16,19},{17,18},{18,17},{19,16},{20,23},{21,22},{22,21},{23,20},{2... | collective-permute-start | bytes 2580488 | tf_op jit(solution)/shard_map/ppermute | solution.py:74
  544.7 24.2 %collective-permute-start.47 = (bf16[160,2688]{1,0:T(8,128)(2,1)S(1)}, bf16[160,2688]{1,0:T(8,128)(2,1)S(1)}, u32[]{:S(2)}, u32[]{:S(2)}) collective-permute-start(bf16[160,2688]{1,0:T(8,128)(2,1)S(1)} %copy-done.183), channel_id=1, source_target_pairs={{0,1},{1,0},{2,3},{3,2},{4,5},{5,4},{6,7},{7,6},{8,9},{9,8},{10,11... | collective-permute-start | bytes 2580488 | tf_op jit(solution)/shard_map/ppermute | solution.py:74
  547.2 41.5 %collective-permute-start.48 = (bf16[160,2688]{1,0:T(8,128)(2,1)S(1)}, bf16[160,2688]{1,0:T(8,128)(2,1)S(1)}, u32[]{:S(2)}, u32[]{:S(2)}) collective-permute-start(bf16[160,2688]{1,0:T(8,128)(2,1)S(1)} %copy-done.182), channel_id=1, source_target_pairs={{0,2},{1,3},{2,0},{3,1},{4,6},{5,7},{6,4},{7,5},{8,10},{9,11},{10,... | collective-permute-start | bytes 2580488 | tf_op jit(solution)/shard_map/ppermute | solution.py:74
  550.2 39.2 %collective-permute-start.49 = (bf16[160,2688]{1,0:T(8,128)(2,1)}, bf16[160,2688]{1,0:T(8,128)(2,1)S(1)}, u32[]{:S(2)}, u32[]{:S(2)}) collective-permute-start(bf16[160,2688]{1,0:T(8,128)(2,1)} %constant_dynamic-update-slice_fusion.65), channel_id=1, source_target_pairs={{0,3},{1,2},{2,1},{3,0},{4,7},{5,6},{6,5},{7,4},{8,11},{9,10},{10,... | collective-permute-start | bytes 2580488 | tf_op jit(solution)/shard_map/ppermute | solution.py:74
  568.9 48.3 %collective-permute-start.70 = (bf16[160,6144]{1,0:T(8,128)(2,1)S(1)}, bf16[160,6144]{1,0:T(8,128)(2,1)S(1)}, u32[]{:S(2)}, u32[]{:S(2)}) collective-permute-start(bf16[160,6144]{1,0:T(8,128)(2,1)S(1)} %copy-done.181), channel_id=1, source_target_pairs={{16,19},{17,18},{18,17},{19,16},{20,23},{21,22},{22,21},{23,20},{2... | collective-permute-start | bytes 5898248 | tf_op jit(solution)/shard_map/ppermute | solution.py:74
  591.6 15.9 %collective-permute-start.50 = (bf16[160,1536]{1,0:T(8,128)(2,1)S(1)}, bf16[160,1536]{1,0:T(8,128)(2,1)S(1)}, u32[]{:S(2)}, u32[]{:S(2)}) collective-permute-start(bf16[160,1536]{1,0:T(8,128)(2,1)S(1)} %pad_dynamic-slice_fusion.2), channel_id=1, source_target_pairs={{0,4},{1,5},{2,6},{3,7},{4,0},{5,1},{6,2},{7,3},{8,12},{9,13},{10,... | collective-permute-start | bytes 1474568 | tf_op jit(solution)/shard_map/ppermute | solution.py:82
  598.0 26.5 %collective-permute-start.61 = (bf16[160,6144]{1,0:T(8,128)(2,1)S(1)}, bf16[160,6144]{1,0:T(8,128)(2,1)S(1)}, u32[]{:S(2)}, u32[]{:S(2)}) collective-permute-start(bf16[160,6144]{1,0:T(8,128)(2,1)S(1)} %copy-done.180), channel_id=1, source_target_pairs={{0,1},{1,0},{2,3},{3,2},{4,5},{5,4},{6,7},{7,6},{8,9},{9,8},{10,11... | collective-permute-start | bytes 5898248 | tf_op jit(solution)/shard_map/ppermute | solution.py:74
  608.3 47.6 %collective-permute-start.62 = (bf16[160,6144]{1,0:T(8,128)(2,1)S(1)}, bf16[160,6144]{1,0:T(8,128)(2,1)S(1)}, u32[]{:S(2)}, u32[]{:S(2)}) collective-permute-start(bf16[160,6144]{1,0:T(8,128)(2,1)S(1)} %copy-done.179), channel_id=1, source_target_pairs={{0,2},{1,3},{2,0},{3,1},{4,6},{5,7},{6,4},{7,5},{8,10},{9,11},{10,... | collective-permute-start | bytes 5898248 | tf_op jit(solution)/shard_map/ppermute | solution.py:74
  611.3 44.7 %collective-permute-start.63 = (bf16[160,6144]{1,0:T(8,128)(2,1)S(1)}, bf16[160,6144]{1,0:T(8,128)(2,1)S(1)}, u32[]{:S(2)}, u32[]{:S(2)}) collective-permute-start(bf16[160,6144]{1,0:T(8,128)(2,1)S(1)} %copy-done.178), channel_id=1, source_target_pairs={{0,3},{1,2},{2,1},{3,0},{4,7},{5,6},{6,5},{7,4},{8,11},{9,10},{10,... | collective-permute-start | bytes 5898248 | tf_op jit(solution)/shard_map/ppermute | solution.py:74
  615.3 44.0 %collective-permute-start.51 = (bf16[160,768]{1,0:T(8,128)(2,1)S(1)}, bf16[160,768]{1,0:T(8,128)(2,1)S(1)}, u32[]{:S(2)}, u32[]{:S(2)}) collective-permute-start(bf16[160,768]{1,0:T(8,128)(2,1)S(1)} %constant_dynamic-slice_fusion.5), channel_id=1, source_target_pairs={{0,8},{1,9},{2,10},{3,11},{4,12},{5,13},{6,14},{7,15},{8,0},{9,1},... | collective-permute-start | bytes 737288 | tf_op jit(solution)/shard_map/ppermute | solution.py:82
  617.2 56.1 %collective-permute-start.60 = (bf16[160,1536]{1,0:T(8,128)(2,1)S(1)}, bf16[160,1536]{1,0:T(8,128)(2,1)S(1)}, u32[]{:S(2)}, u32[]{:S(2)}) collective-permute-start(bf16[160,1536]{1,0:T(8,128)(2,1)S(1)} %pad_maximum_fusion.10), channel_id=1, source_target_pairs={{16,20},{17,21},{18,22},{19,23},{20,16},{21,17},{22,18},{23,19},{2... | collective-permute-start | bytes 1474568 | tf_op jit(solution)/shard_map/ppermute | solution.py:82
  624.5 62.7 %collective-permute-start.71 = (bf16[160,3072]{1,0:T(8,128)(2,1)S(1)}, bf16[160,3072]{1,0:T(8,128)(2,1)S(1)}, u32[]{:S(2)}, u32[]{:S(2)}) collective-permute-start(bf16[160,3072]{1,0:T(8,128)(2,1)S(1)} %constant_dynamic-slice_fusion.1), channel_id=1, source_target_pairs={{16,20},{17,21},{18,22},{19,23},{20,16},{21,17},{22,18},{23,19},{2... | collective-permute-start | bytes 2949128 | tf_op jit(solution)/shard_map/ppermute | solution.py:82
  659.3 11.8 %collective-permute-start.52 = (bf16[160,768]{1,0:T(8,128)(2,1)S(1)}, bf16[160,768]{1,0:T(8,128)(2,1)S(1)}, u32[]{:S(2)}, u32[]{:S(2)}) collective-permute-start(bf16[160,768]{1,0:T(8,128)(2,1)S(1)} %add_convert_fusion.11), channel_id=1, source_target_pairs={{0,8},{1,9},{2,10},{3,11},{4,12},{5,13},{6,14},{7,15},{8,0},{9,1},... | collective-permute-start | bytes 737288 | tf_op jit(solution)/shard_map/ppermute | solution.py:82
  661.3 27.0 %collective-permute-start.64 = (bf16[160,3072]{1,0:T(8,128)(2,1)S(1)}, bf16[160,3072]{1,0:T(8,128)(2,1)S(1)}, u32[]{:S(2)}, u32[]{:S(2)}) collective-permute-start(bf16[160,3072]{1,0:T(8,128)(2,1)S(1)} %constant_dynamic-slice_fusion.3), channel_id=1, source_target_pairs={{0,4},{1,5},{2,6},{3,7},{4,0},{5,1},{6,2},{7,3},{8,12},{9,13},{10,... | collective-permute-start | bytes 2949128 | tf_op jit(solution)/shard_map/ppermute | solution.py:82
  671.2 13.3 %collective-permute-start.53 = (bf16[160,1536]{1,0:T(8,128)(2,1)S(1)}, bf16[160,1536]{1,0:T(8,128)(2,1)S(1)}, u32[]{:S(2)}, u32[]{:S(2)}) collective-permute-start(bf16[160,1536]{1,0:T(8,128)(2,1)S(1)} %pad_maximum_fusion.9), channel_id=1, source_target_pairs={{0,4},{1,5},{2,6},{3,7},{4,0},{5,1},{6,2},{7,3},{8,12},{9,13},{10,... | collective-permute-start | bytes 1474568 | tf_op jit(solution)/shard_map/ppermute | solution.py:82
  689.4 17.2 %collective-permute-start.65 = (bf16[160,1536]{1,0:T(8,128)(2,1)}, bf16[160,1536]{1,0:T(8,128)(2,1)}, u32[]{:S(2)}, u32[]{:S(2)}) collective-permute-start(bf16[160,1536]{1,0:T(8,128)(2,1)} %constant_dynamic-slice_fusion.2), channel_id=1, source_target_pairs={{0,8},{1,9},{2,10},{3,11},{4,12},{5,13},{6,14},{7,15},{8,0},{9,1},... | collective-permute-start | bytes 1474568 | tf_op jit(solution)/shard_map/ppermute | solution.py:82
  694.0 15.7 %collective-permute-start.73 = (bf16[160,1536]{1,0:T(8,128)(2,1)S(1)}, bf16[160,1536]{1,0:T(8,128)(2,1)}, u32[]{:S(2)}, u32[]{:S(2)}) collective-permute-start(bf16[160,1536]{1,0:T(8,128)(2,1)S(1)} %add_convert_fusion.6), channel_id=1, source_target_pairs={{16,24},{17,25},{18,26},{19,27},{20,28},{21,29},{22,30},{23,31},{2... | collective-permute-start | bytes 1474568 | tf_op jit(solution)/shard_map/ppermute | solution.py:82
  707.8 16.9 %collective-permute-start.66 = (bf16[160,1536]{1,0:T(8,128)(2,1)S(1)}, bf16[160,1536]{1,0:T(8,128)(2,1)S(1)}, u32[]{:S(2)}, u32[]{:S(2)}) collective-permute-start(bf16[160,1536]{1,0:T(8,128)(2,1)S(1)} %add_convert_fusion.7), channel_id=1, source_target_pairs={{0,8},{1,9},{2,10},{3,11},{4,12},{5,13},{6,14},{7,15},{8,0},{9,1},... | collective-permute-start | bytes 1474568 | tf_op jit(solution)/shard_map/ppermute | solution.py:82
  710.9 16.7 %collective-permute-start.74 = (bf16[160,3072]{1,0:T(8,128)(2,1)S(1)}, bf16[160,3072]{1,0:T(8,128)(2,1)S(1)}, u32[]{:S(2)}, u32[]{:S(2)}) collective-permute-start(bf16[160,3072]{1,0:T(8,128)(2,1)S(1)} %pad_maximum_fusion.6), channel_id=1, source_target_pairs={{16,20},{17,21},{18,22},{19,23},{20,16},{21,17},{22,18},{23,19},{2... | collective-permute-start | bytes 2949128 | tf_op jit(solution)/shard_map/ppermute | solution.py:82
  724.8 16.0 %collective-permute-start.67 = (bf16[160,3072]{1,0:T(8,128)(2,1)S(1)}, bf16[160,3072]{1,0:T(8,128)(2,1)S(1)}, u32[]{:S(2)}, u32[]{:S(2)}) collective-permute-start(bf16[160,3072]{1,0:T(8,128)(2,1)S(1)} %pad_maximum_fusion.5), channel_id=1, source_target_pairs={{0,4},{1,5},{2,6},{3,7},{4,0},{5,1},{6,2},{7,3},{8,12},{9,13},{10,... | collective-permute-start | bytes 2949128 | tf_op jit(solution)/shard_map/ppermute | solution.py:82
  (196 other events, 2618.8 us)

commit v3 on v1

v3 whole, which is shorter than its diff:
```python
import functools

import jax
import jax.numpy as jnp
from jax import lax
from jax.experimental import pallas as pl
from jax.experimental.pallas import tpu as pltpu
from jax.sharding import PartitionSpec as P

WIN = 512
EPSILON = 1e-06
ROPE_BASE = 10000.0
NEG_LARGE = -1e30
AXES = ("section", "seq", "fsdp")
BF = jnp.bfloat16
F32 = jnp.float32
GAIN_ROWS = 16
INTERPRET = False


def mm(left, right):
    return lax.dot_general(left, right, (((1,), (0,)), ((), ())), preferred_element_type=F32)


def mm_nt(left, right):
    return lax.dot_general(left, right, (((1,), (1,)), ((), ())), preferred_element_type=F32)


def mm_tn(left, right):
    return lax.dot_general(left, right, (((0,), (0,)), ((), ())), preferred_element_type=F32)


def inverse_rms(values):
    return lax.rsqrt(jnp.mean(values * values, axis=-1, keepdims=True) + EPSILON)


def norm_back(values, scale, gain, grad):
    weighted = grad * gain
    inner = jnp.mean(values * weighted, axis=-1, keepdims=True)
    return scale * weighted - values * (scale * scale * scale * inner)


def gain_back(values, scale, grad):
    return jnp.sum(values * scale * grad, axis=0, keepdims=True)


def call(kernel, info, arrays, outs, scratch=(), flops=0):
    smem = pl.BlockSpec(memory_space=pltpu.SMEM)
    vmem = pl.BlockSpec(memory_space=pltpu.VMEM)
    size = sum(a.size * a.dtype.itemsize for a in arrays)
    size += sum(a.size * a.dtype.itemsize for a in outs)
    return pl.pallas_call(
        kernel,
        out_shape=outs,
        in_specs=[smem] + [vmem] * len(arrays),
        out_specs=[vmem] * len(outs),
        scratch_shapes=list(scratch),
        compiler_params=pltpu.CompilerParams(vmem_limit_bytes=40 * 1024 * 1024),
        cost_estimate=pl.CostEstimate(flops=flops, bytes_accessed=size, transcendentals=0),
        interpret=INTERPRET,
    )(info, *arrays)


def shape(dims, kind):
    return jax.ShapeDtypeStruct(tuple(dims), kind)


def slot(index, width):
    return pl.ds(pl.multiple_of(index * width, width), width)


def gains_kernel(info, *refs):
    pieces, out, held = refs[:-2], refs[-2], refs[-1]
    count = len(pieces)
    shard = out.shape[1] // count
    rows = pieces[0].shape[0] - GAIN_ROWS
    part = shard * 2 // 5
    for flip, piece in enumerate(pieces):
        held[info[0] ^ flip] = piece[rows : rows + GAIN_ROWS, : held.shape[2]].astype(F32)
    out[...] = jnp.zeros_like(out)
    for place in range(count):
        for row in range(4):
            out[row : row + 1, place * shard : (place + 1) * shard] = held[
                place, 0:1, row * shard : (row + 1) * shard
            ]
        for row in range(2):
            start = 4 * shard + row * part
            out[4 + row : 5 + row, place * part : (place + 1) * part] = held[
                place, 0:1, start : start + part
            ]


def project_kernel(info, x, gains, cosine, sine, *refs):
    pieces = refs[:-4]
    blocks, qkv, query, own = refs[-4:]
    shard = blocks.shape[2]
    half = cosine.shape[1]
    head = 2 * half
    residual = x[...].astype(F32)
    normed = residual * inverse_rms(residual) * gains[0:1, :]
    for place in range(len(pieces)):
        blocks[place] = normed[:, place * shard : (place + 1) * shard].astype(BF)
    total = None
    for flip, piece in enumerate(pieces):
        term = mm(blocks[info[0] ^ flip], piece[:shard, :])
        total = term if total is None else total + term
    qkv[...] = total
    cos, sin = cosine[...], sine[...]
    heads = query.shape[1] // head
    for index in range(heads + 1):
        raw = total[:, index * head : (index + 1) * head]
        row = 4 if index < heads else 5
        normal = raw * inverse_rms(raw) * gains[row : row + 1, :head]
        one, two = normal[:, :half], normal[:, half:]
        target, start = (query, index * head) if index < heads else (own, 0)
        target[:, start : start + half] = (one * cos - two * sin).astype(BF)
        target[:, start + half : start + head] = (two * cos + one * sin).astype(BF)
    own[:, head:] = total[:, (heads + 1) * head :].astype(BF)


def select_kernel(info, own, one, two, *outs):
    for index, out in enumerate(outs):
        lower = (info[0] < (info[0] ^ (index + 1))).astype(F32)
        out[0] = one[...]
        mixed = own[...].astype(F32) * lower + two[...].astype(F32) * (1.0 - lower)
        out[1] = mixed.astype(BF)


def attend_kernel(micro, info, query, own, one, two, *refs):
    got = refs[:3]
    x, gains, limit, query_place, key_place = refs[3:8]
    pieces = refs[8:12]
    window, probs, attended, branch, mixed, blocks = refs[12:]
    rows = own.shape[0] // micro
    head = own.shape[1] // 2
    heads = query.shape[1] // head
    shard = blocks.shape[2]
    for m in range(micro):
        span = slice(m * rows, (m + 1) * rows)
        parts = [own[span], one[span], two[span]]
        for ref in got:
            parts += [ref[0, span], ref[1, span]]
        for index, part in enumerate(parts):
            window[m, index * rows : (index + 1) * rows] = part
        distance = query_place[span] - key_place[...]
        allowed = (distance >= 0) & (distance <= limit[span])
        bias = jnp.where(allowed, 0.0, NEG_LARGE)
        bias = jnp.concatenate([bias] * heads, axis=0)
        stacked = jnp.concatenate(
            [query[span, h * head : (h + 1) * head] for h in range(heads)], axis=0
        )
        scores = mm_nt(stacked, window[m, :, :head]) * head ** (-0.5) + bias
        exponent = jnp.exp(scores - jnp.max(scores, axis=-1, keepdims=True))
        chance = exponent / jnp.sum(exponent, axis=-1, keepdims=True)
        probs[m] = chance
        result = mm(chance.astype(BF), window[m, :, head:]).astype(BF)
        for h in range(heads):
            attended[span, h * head : (h + 1) * head] = result[h * rows : (h + 1) * rows]
    total = None
    for flip, piece in enumerate(pieces):
        term = mm(attended[:, slot(info[0] ^ flip, head)], piece[...])
        total = term if total is None else total + term
    branch[...] = total
    value = x[...].astype(F32) + total * inverse_rms(total) * gains[1:2, :]
    mixed[...] = value
    normed = value * inverse_rms(value) * gains[2:3, :]
    for place in range(len(pieces)):
        blocks[place] = normed[:, place * shard : (place + 1) * shard].astype(BF)


def gelu_parts(gate):
    c = 0.7978845608028654
    inner = jnp.tanh(c * (gate + 0.044715 * gate * gate * gate))
    value = 0.5 * gate * (1.0 + inner)
    slope = 0.5 * (1.0 + inner) + 0.5 * gate * (1.0 - inner * inner) * c * (
        1.0 + 3 * 0.044715 * gate * gate
    )
    return value, slope


def ffn_kernel(info, blocks, mixed, gains, *refs):
    gate_up_pieces, down_pieces = refs[:4], refs[4:8]
    gate_up, activated, down, result = refs[8:]
    hidden = activated.shape[1]
    width = 512
    for start in range(0, hidden, width):
        both = []
        for base in (start, hidden + start):
            total = None
            for flip, piece in enumerate(gate_up_pieces):
                term = mm(blocks[info[0] ^ flip], piece[:, base : base + width])
                total = term if total is None else total + term
            gate_up[:, base : base + width] = total
            both.append(total)
        value, _ = gelu_parts(both[0])
        activated[:, start : start + width] = (value * both[1]).astype(BF)
    total = None
    for flip, piece in enumerate(down_pieces):
        term = mm(activated[:, slot(info[0] ^ flip, piece.shape[0])], piece[...])
        total = term if total is None else total + term
    down[...] = total
    result[...] = (mixed[...] + total * inverse_rms(total) * gains[3:4, :]).astype(BF)


def ffn_back_kernel(info, upstream, mixed, down, gate_up, activated, blocks, gains, *refs):
    gate_up_pieces, down_pieces = refs[:4], refs[4:8]
    packs, grad_mixed, gain_rows = refs[8:12], refs[12], refs[13]
    grad_act, grad_gate_up, held, natural = refs[14:]
    hidden = activated.shape[1]
    model = mixed.shape[1]
    shard = blocks.shape[2]
    top = upstream[...].astype(F32)
    raw = down[...]
    scale = inverse_rms(raw)
    grad_down = norm_back(raw, scale, gains[3:4, :], top).astype(BF)
    gain_rows[...] = jnp.zeros_like(gain_rows)
    gain_rows[3:4, :] = gain_back(raw, scale, top)
    act_at = 2 * hidden + model
    block_at = act_at + hidden // 4
    for flip, piece in enumerate(down_pieces):
        grad_act[:, slot(info[0] ^ flip, piece.shape[0])] = mm_nt(grad_down, piece[...])
    for flip, pack in enumerate(packs):
        pack[:, 2 * hidden : act_at] = grad_down
        pack[:, act_at:block_at] = activated[:, slot(info[0] ^ flip, hidden // 4)]
        pack[:, block_at:] = jnp.zeros_like(pack[:, block_at:])
        pack[:, block_at : block_at + shard] = blocks[info[0] ^ flip]
    width = 512
    for start in range(0, hidden, width):
        value, slope = gelu_parts(gate_up[:, start : start + width])
        up = gate_up[:, hidden + start : hidden + start + width]
        grad = grad_act[:, start : start + width]
        grad_gate_up[:, start : start + width] = (grad * up * slope).astype(BF)
        grad_gate_up[:, hidden + start : hidden + start + width] = (grad * value).astype(BF)
    for pack in packs:
        pack[:, : 2 * hidden] = grad_gate_up[...]
    for flip, piece in enumerate(gate_up_pieces):
        held[info[0] ^ flip] = mm_nt(grad_gate_up[...], piece[...])
    for place in range(4):
        natural[:, place * shard : (place + 1) * shard] = held[place]
    grad_in = natural[...]
    raw = mixed[...]
    scale = inverse_rms(raw)
    gain_rows[2:3, :] = gain_back(raw, scale, grad_in)
    grad_mixed[...] = top + norm_back(raw, scale, gains[2:3, :], grad_in)


def attend_back_kernel(micro, info, grad_mixed, branch, window, probs, query, gains, *refs):
    pieces = refs[:4]
    grad_branch, grad_query, own, one, two = refs[4:9]
    gives, gain_rows, grad_attended = refs[9:12], refs[12], refs[13]
    rows = own.shape[0] // micro
    head = own.shape[1] // 2
    heads = query.shape[1] // head
    factor = head ** (-0.5)
    raw = branch[...]
    scale = inverse_rms(raw)
    grad = grad_mixed[...]
    gain_rows[...] = jnp.zeros_like(gain_rows)
    gain_rows[1:2, :] = gain_back(raw, scale, grad)
    low = norm_back(raw, scale, gains[1:2, :], grad).astype(BF)
    grad_branch[...] = low
    for flip, piece in enumerate(pieces):
        grad_attended[:, slot(info[0] ^ flip, head)] = mm_nt(low, piece[...]).astype(BF)
    for m in range(micro):
        span = slice(m * rows, (m + 1) * rows)
        chance = probs[m]
        keys, values = window[m, :, :head], window[m, :, head:]
        stacked = jnp.concatenate(
            [query[span, h * head : (h + 1) * head] for h in range(heads)], axis=0
        )
        upstream = jnp.concatenate(
            [grad_attended[span, h * head : (h + 1) * head] for h in range(heads)], axis=0
        )
        grad_values = mm_tn(chance.astype(BF), upstream)
        grad_chance = mm_nt(upstream, values)
        inner = jnp.sum(chance * grad_chance, axis=-1, keepdims=True)
        grad_scores = (chance * (grad_chance - inner)).astype(BF)
        grad_stacked = mm(grad_scores, keys) * factor
        grad_keys = mm_tn(grad_scores, stacked) * factor
        for h in range(heads):
            grad_query[span, h * head : (h + 1) * head] = grad_stacked[h * rows : (h + 1) * rows]
        for index, target in enumerate((own, one, two)):
            part = slice(index * rows, (index + 1) * rows)
            target[span, :head] = grad_keys[part]
            target[span, head:] = grad_values[part]
        for index, target in enumerate(gives):
            for side in range(2):
                start = (3 + 2 * index + side) * rows
                target[side, span, :head] = grad_keys[start : start + rows].astype(BF)
                target[side, span, head:] = grad_values[start : start + rows].astype(BF)


def combine_kernel(info, own, one, two, first, second, third, own_out, one_out, two_out):
    total_own, total_one, total_two = own[...], one[...], two[...]
    for index, got in enumerate((first, second, third)):
        lower = (info[0] < (info[0] ^ (index + 1))).astype(F32)
        total_one = total_one + got[0].astype(F32)
        side = got[1].astype(F32)
        total_own = total_own + side * lower
        total_two = total_two + side * (1.0 - lower)
    own_out[...] = total_own
    one_out[...] = total_one.astype(BF)
    two_out[...] = total_two.astype(BF)


def project_back_kernel(info, own, back_one, back_two, grad_query, qkv, cosine, sine, x, grad_mixed,
                        grad_branch, attended, blocks, gains, rows_ffn, rows_attn, *refs):
    pieces = refs[:4]
    packs, grad_in = refs[4:8], refs[8]
    grad_qkv, held, natural, gain_held = refs[9:]
    tokens, model = natural.shape
    shard = blocks.shape[2]
    half = cosine.shape[1]
    head = 2 * half
    heads = grad_query.shape[1] // head
    cos, sin = cosine[...], sine[...]
    grad_own = own[...] + back_one[...].astype(F32) + back_two[...].astype(F32)
    head_gains = [None, None]
    for index in range(heads + 1):
        if index < heads:
            grad = grad_query[:, index * head : (index + 1) * head]
        else:
            grad = grad_own[:, :head]
        one, two = grad[:, :half], grad[:, half:]
        grad = jnp.concatenate((one * cos + two * sin, two * cos - one * sin), axis=1)
        raw = qkv[:, index * head : (index + 1) * head]
        scale = inverse_rms(raw)
        kind = 0 if index < heads else 1
        term = gain_back(raw, scale, grad)
        head_gains[kind] = term if head_gains[kind] is None else head_gains[kind] + term
        back = norm_back(raw, scale, gains[4 + kind : 5 + kind, :head], grad)
        grad_qkv[:, index * head : (index + 1) * head] = back.astype(BF)
    grad_qkv[:, (heads + 1) * head :] = grad_own[:, head:].astype(BF)
    for flip, piece in enumerate(pieces):
        held[info[0] ^ flip] = mm_nt(grad_qkv[...], piece[:shard, :])
    for place in range(4):
        natural[:, place * shard : (place + 1) * shard] = held[place]
    grad_normed = natural[...]
    residual = x[...].astype(F32)
    scale = inverse_rms(residual)
    first_gain = gain_back(residual, scale, grad_normed)
    total = grad_mixed[...] + norm_back(residual, scale, gains[0:1, :], grad_normed)
    grad_in[...] = total.astype(BF)
    gain_held[...] = jnp.zeros_like(gain_held)
    part = head // 4
    four = (first_gain, rows_attn[1:2, :], rows_ffn[2:3, :], rows_ffn[3:4, :])
    for place in range(4):
        for row, values in enumerate(four):
            gain_held[place, row : row + 1, :shard] = values[
                :, place * shard : (place + 1) * shard
            ]
        for row, values in enumerate(head_gains):
            gain_held[place, 4 + row : 5 + row, :part] = values[
                :, place * part : (place + 1) * part
            ]
    wide = grad_qkv.shape[1]
    att_at = wide + model
    block_at = att_at + head
    for flip, pack in enumerate(packs):
        other = info[0] ^ flip
        pack[tokens:, :] = jnp.zeros_like(pack[tokens:, :])
        pack[tokens:, : gain_held.shape[2]] = gain_held[other].astype(BF)
        pack[:tokens, :wide] = grad_qkv[...]
        pack[:tokens, wide:att_at] = grad_branch[...]
        pack[:tokens, att_at:block_at] = attended[:, slot(other, head)]
        pack[:tokens, block_at:] = jnp.zeros_like(pack[:tokens, block_at:])
        pack[:tokens, block_at : block_at + shard] = blocks[other]


def over(packs, tokens, left, right, left_width, right_width):
    total = None
    for pack in packs:
        term = mm_tn(
            pack[:tokens, left : left + left_width], pack[:tokens, right : right + right_width]
        )
        total = term if total is None else total + term
    return total.astype(BF)


def ffn_weights_kernel(shard, model, info, *refs):
    packs, first, second = refs[:4], refs[4], refs[5]
    tokens = packs[0].shape[0]
    wide = first.shape[1]
    quarter = second.shape[1] // 4
    act_at = wide + model
    for start in range(0, wide, 1024):
        first[:, start : start + 1024] = over(
            packs, tokens, act_at + quarter, start, shard, 1024
        )
    for place in range(4):
        second[:, place * quarter : (place + 1) * quarter] = over(
            packs, tokens, wide + place * shard, act_at, shard, quarter
        )


def weights_kernel(shard, model, info, *refs):
    packs, gate_up, down, first, second = refs[:4], refs[4], refs[5], refs[6], refs[7]
    tokens = packs[0].shape[0] - GAIN_ROWS
    head = model // 5 * 2
    wide = packs[0].shape[1] - model - 2 * head
    hidden = gate_up.shape[1]
    first[:, :hidden] = gate_up[...]
    first[:, hidden:] = jnp.zeros_like(first[:, hidden:])
    gains = sum(pack[tokens:, :head].astype(F32) for pack in packs)
    first[:GAIN_ROWS, hidden : hidden + head] = gains.astype(BF)
    att_at = wide + model
    second[:, :wide] = over(packs, tokens, att_at + head, 0, shard, wide)
    for place in range(4):
        start = wide + place * head
        second[:, start : start + head] = over(
            packs, tokens, wide + place * shard, att_at, shard, head
        )
    second[:, wide + 4 * head :] = down[...]


class Links:
    def __init__(self, sizes):
        self.sizes = sizes

    def index(self, section, seq, fsdp):
        return (section * self.sizes["seq"] + seq) * self.sizes["fsdp"] + fsdp

    def send(self, array, section, place):
        pairs = []
        for z in range(self.sizes["seq"]):
            for f in range(self.sizes["fsdp"]):
                to_section, to_z, to_f = place(z, f)
                if 0 <= to_z < self.sizes["seq"]:
                    pairs.append((self.index(section, z, f), self.index(to_section, to_z, to_f)))
        return lax.ppermute(array, AXES, pairs)

    def along(self, array, section, by):
        return self.send(array, section, lambda z, f: (section, z + by, f))

    def across(self, array, section, flip):
        return self.send(array, section, lambda z, f: (section, z, f ^ flip))

    def cross(self, array, section):
        return self.send(array, section, lambda z, f: (1 - section, z, f))

    def swap(self, array):
        pairs = []
        for section in range(2):
            for z in range(self.sizes["seq"]):
                for f in range(self.sizes["fsdp"]):
                    pairs.append((self.index(section, z, f), self.index(1 - section, z, f)))
        return lax.ppermute(array, AXES, pairs)


def body(sizes, hidden_in, cotangent, positions, attn_gain, w_query, w_key, w_value, query_gain,
         key_gain, w_output, post_attn_gain, ffn_gain, w_gate, w_up, w_down, post_ffn_gain):
    section = lax.axis_index("section")
    seq = lax.axis_index("seq")
    fsdp = lax.axis_index("fsdp")
    is_first = section == 0
    micro, rows, model = hidden_in.shape
    tokens = micro * rows
    shard = w_query.shape[1]
    shards = sizes["fsdp"]
    heads_width, head = w_query.shape[2], w_key.shape[2]
    wide = heads_width + 2 * head
    hidden = w_gate.shape[2]
    quarter = hidden // shards
    assert shards == 4 and 2 * shards * rows == WIN and heads_width == shards * head
    links = Links(sizes)
    info = jnp.stack([fsdp, seq, section]).astype(jnp.int32)

    row = jnp.concatenate(
        (attn_gain[0], post_attn_gain[0], ffn_gain[0], post_ffn_gain[0], query_gain[0], key_gain[0])
    )
    row = jnp.pad(row[None], ((0, GAIN_ROWS - 1), (0, wide - row.shape[0])))
    own_shards = (
        jnp.concatenate(
            (jnp.concatenate((w_query[0], w_key[0], w_value[0]), axis=1), row), axis=0
        ),
        w_output[0],
        jnp.concatenate((w_gate[0], w_up[0]), axis=1),
        w_down[0],
    )

    def gather(arrays, target):
        return [
            [array] + [links.across(array, target, flip) for flip in range(1, shards)]
            for array in arrays
        ]

    half = head // 2
    place = positions.reshape(tokens, 1)
    frequency = ROPE_BASE ** (-2.0 * jnp.arange(half, dtype=F32) / head)
    angles = place.astype(F32) * frequency[None, :]
    cosine, sine = jnp.cos(angles), jnp.sin(angles)
    limit = jnp.minimum(place, WIN - 1)
    query_place = jnp.tile((seq * shards + fsdp) * rows + jnp.arange(rows), micro)[:, None]
    starts = [(seq - back) * shards + fsdp for back in range(3)]
    for flip in range(1, shards):
        other = fsdp ^ flip
        starts.append((seq - 1) * shards + other)
        starts.append(jnp.where(other < fsdp, seq, seq - 2) * shards + other)
    key_place = (jnp.stack(starts)[:, None] * rows + jnp.arange(rows)[None, :]).reshape(1, -1)
    query_place, key_place = query_place.astype(jnp.int32), key_place.astype(jnp.int32)
    span = key_place.shape[1]

    def gain_table(pieces):
        return call(
            gains_kernel, info, pieces, [shape((8, model), F32)],
            [pltpu.VMEM((shards, GAIN_ROWS, 768), F32)],
        )[0]

    def forward(x, weights, target):
        first, out, gate_up_w, down_w = weights
        gains = gain_table(first)
        blocks, qkv, query, own = call(
            project_kernel, info, [x, gains, cosine, sine] + first,
            [shape((shards, tokens, shard), BF), shape((tokens, wide), F32),
             shape((tokens, heads_width), BF), shape((tokens, 2 * head), BF)],
            flops=2 * tokens * model * wide,
        )
        one, two = links.along(own, target, 1), links.along(own, target, 2)
        sent = call(
            select_kernel, info, [own, one, two], [shape((2, tokens, 2 * head), BF)] * (shards - 1)
        )
        got = [links.across(array, target, 1 + i) for i, array in enumerate(sent)]
        window, probs, attended, branch, mixed, ffn_blocks = call(
            functools.partial(attend_kernel, micro), info,
            [query, own, one, two] + got + [x, gains, limit, query_place, key_place] + out,
            [shape((micro, span, 2 * head), BF), shape((micro, shards * rows, span), F32),
             shape((tokens, heads_width), BF), shape((tokens, model), F32),
             shape((tokens, model), F32), shape((shards, tokens, shard), BF)],
            flops=2 * tokens * heads_width * (2 * span + model),
        )
        gate_up, activated, down, result = call(
            ffn_kernel, info, [ffn_blocks, mixed, gains] + gate_up_w + down_w,
            [shape((tokens, 2 * hidden), F32), shape((tokens, hidden), BF),
             shape((tokens, model), F32), shape((tokens, model), BF)],
            flops=6 * tokens * hidden * model,
        )
        saved = dict(
            x=x, gains=gains, blocks=blocks, qkv=qkv, query=query, window=window, probs=probs,
            attended=attended, branch=branch, mixed=mixed, ffn_blocks=ffn_blocks, gate_up=gate_up,
            activated=activated, down=down,
        )
        return result, saved

    def back_ffn(upstream, s, weights):
        _, _, gate_up_w, down_w = weights
        outs = call(
            ffn_back_kernel, info,
            [upstream, s["mixed"], s["down"], s["gate_up"], s["activated"], s["ffn_blocks"],
             s["gains"]] + gate_up_w + down_w,
            [shape((tokens, 2 * hidden + model + quarter + 256), BF)] * shards
            + [shape((tokens, model), F32), shape((8, model), F32)],
            [pltpu.VMEM((tokens, hidden), F32), pltpu.VMEM((tokens, 2 * hidden), BF),
             pltpu.VMEM((shards, tokens, shard), F32), pltpu.VMEM((tokens, model), F32)],
            flops=6 * tokens * hidden * model,
        )
        return outs[:shards], outs[shards], outs[shards + 1]

    def back_attend(grad_mixed, s, weights):
        pair = [shape((tokens, 2 * head), F32)] * 3
        outs = call(
            functools.partial(attend_back_kernel, micro), info,
            [grad_mixed, s["branch"], s["window"], s["probs"], s["query"], s["gains"]] + weights[1],
            [shape((tokens, model), BF), shape((tokens, heads_width), F32)] + pair
            + [shape((2, tokens, 2 * head), BF)] * (shards - 1) + [shape((8, model), F32)],
            [pltpu.VMEM((tokens, heads_width), BF)],
            flops=2 * tokens * heads_width * (4 * span + model),
        )
        return outs[0], outs[1], outs[2:5], outs[5:8], outs[8]

    def back_window(kept, gives, target):
        got = [links.across(array, target, 1 + i) for i, array in enumerate(gives)]
        own, one, two = call(
            combine_kernel, info, list(kept) + got,
            [shape((tokens, 2 * head), F32)] + [shape((tokens, 2 * head), BF)] * 2,
        )
        return own, links.along(one, target, -1), links.along(two, target, -2)

    def back_project(window_grads, grad_query, grad_mixed, grad_branch, rows_ffn, rows_attn, s,
                     weights):
        outs = call(
            project_back_kernel, info,
            list(window_grads) + [grad_query, s["qkv"], cosine, sine, s["x"], grad_mixed,
            grad_branch, s["attended"], s["blocks"], s["gains"], rows_ffn, rows_attn] + weights[0],
            [shape((tokens + GAIN_ROWS, wide + model + head + 256), BF)] * shards
            + [shape((tokens, model), BF)],
            [pltpu.VMEM((tokens, wide), BF), pltpu.VMEM((shards, tokens, shard), F32),
             pltpu.VMEM((tokens, model), F32), pltpu.VMEM((shards, GAIN_ROWS, 256), F32)],
            flops=2 * tokens * wide * model,
        )
        return outs[:shards], outs[shards]

    def exchange(packs, target):
        return [packs[0]] + [links.across(packs[i], target, i) for i in range(1, shards)]

    total_width = 2 * hidden + 512

    def ffn_weights(packs):
        return call(
            functools.partial(ffn_weights_kernel, shard, model), info, list(packs),
            [shape((shard, 2 * hidden), BF), shape((shard, hidden), BF)],
            flops=2 * shards * tokens * shard * 3 * hidden,
        )

    def attn_weights(packs, ffn):
        return call(
            functools.partial(weights_kernel, shard, model), info, list(packs) + list(ffn),
            [shape((shard, total_width), BF)] * 2,
            flops=2 * shards * tokens * shard * (total_width - hidden),
        )

    tie = lax.optimization_barrier

    def backward(upstream, s, weights, target, other=None):
        ffn_packs, grad_mixed, rows_ffn = back_ffn(upstream, s, weights)
        ffn_packs = exchange(ffn_packs, target)
        grad_branch, grad_query, kept, gives, rows_attn = back_attend(grad_mixed, s, weights)
        window_grads = back_window(kept, gives, target)
        if other is not None:
            ffn = ffn_weights(ffn_packs)
            window_grads, ffn, other = tie((window_grads, ffn, other))
        attn_packs, grad_in = back_project(
            window_grads, grad_query, grad_mixed, grad_branch, rows_ffn, rows_attn, s, weights
        )
        if other is None:
            ffn = ffn_weights(ffn_packs)
        return ffn, attn_packs, grad_in, other

    first = gather(own_shards, 0)
    x_first = hidden_in.reshape(tokens, model)
    result_a, saved_a = forward(x_first, first, 0)
    token = links.cross(saved_a["window"][0, -16:, :128], 0)
    later, token = lax.optimization_barrier((own_shards, token))
    tied = lax.dynamic_update_slice(later[0], token, (shard, wide - token.shape[1]))
    second = gather((tied,) + later[1:], 1)
    middle = links.cross(result_a, 0)
    result_b, saved_b = forward(middle, second, 1)

    ffn, attn_packs, grad_b, _ = backward(cotangent.reshape(tokens, model), saved_b, second, 1)
    upstream = links.cross(grad_b, 1)
    b_first, b_second = attn_weights(exchange(attn_packs, 1), ffn)
    upstream, b_first, b_second = tie((upstream, b_first, b_second))
    half_b = jnp.where(is_first, links.cross(b_first, 1), b_second)

    ffn, attn_packs, grad_a, half_b = backward(upstream, saved_a, first, 0, half_b)
    part_b = lax.psum(half_b, "seq")
    attn_packs, part_b = tie((exchange(attn_packs, 0), part_b))
    a_first, a_second = attn_weights(attn_packs, ffn)
    half_a = jnp.where(is_first, a_first, links.cross(a_second, 0))
    part_a = lax.psum(half_a, "seq")

    mine = jnp.where(is_first, part_a, part_b)
    theirs = links.swap(jnp.where(is_first, part_b, part_a))
    total_first = jnp.where(is_first, mine, theirs)
    total_second = jnp.where(is_first, theirs, mine).astype(F32)
    gain_out = total_first[:8, 2 * hidden : 2 * hidden + shard].astype(F32)

    def unfold(array):
        count = array.shape[1] // shards
        return jnp.concatenate(
            [array[:, i * count : (i + 1) * count] for i in range(shards)], axis=0
        ).T

    part = head // shards
    section_outputs = jnp.where(is_first, result_a, result_b).reshape(1, micro, rows, model)
    input_grads = jnp.where(is_first, grad_a, grad_b).reshape(1, micro, rows, model)
    return (
        section_outputs,
        input_grads,
        gain_out[0:1],
        total_second[None, :, :heads_width],
        total_second[None, :, heads_width : heads_width + head],
        total_second[None, :, heads_width + head : wide],
        gain_out[4:5, :part],
        gain_out[5:6, :part],
        unfold(total_second[:, wide : wide + heads_width])[None],
        gain_out[1:2],
        gain_out[2:3],
        total_first[None, :, :hidden].astype(F32),
        total_first[None, :, hidden : 2 * hidden].astype(F32),
        unfold(total_second[:, wide + heads_width :])[None],
        gain_out[3:4],
    )


def solution(mesh):
    rows = P(None, ("seq", "fsdp"), None)
    vector, matrix = P("section", "fsdp"), P("section", "fsdp", None)
    weights = (vector, matrix, matrix, matrix, vector, vector, matrix, vector, vector, matrix,
               matrix, matrix, vector)
    out_rows = P("section", None, ("seq", "fsdp"), None)
    return jax.shard_map(
        functools.partial(body, dict(mesh.shape)),
        mesh=mesh,
        in_specs=(rows, rows, P(None, ("seq", "fsdp"))) + weights,
        out_specs=(out_rows, out_rows) + weights,
        check_vma=False,
    )
```

time: 654 us -> 543 us (0.83)
  waiting for transfers between devices: 400 us -> 285 us
  starting transfers between devices: 41.2 us -> 114 us
  Pallas kernels: 0 us -> 60.6 us
  matrix products: 52.9 us -> 0 us
  other arithmetic: 65.3 us -> 13.2 us
  local copies, waits for them, and re-layouts: 68.6 us -> 43.7 us
    ppermute x22 -> x62, waiting for transfers between devices: 38.7 us -> 184 us  [the longest x61 182 us: send(): return lax.ppermute(array, AXES, pairs)]
    reduce_scatter x4 -> x0, waiting for transfers between devices: 133 us -> none  [scatter(): lax.psum_scatter(array.astype(BF), 'fsdp', scatter_dimension=0, tiled=True)]
    all_gather x4 -> x0, waiting for transfers between devices: 112 us -> none  [the longest x1 42.7 us: body(): gather(jnp.concatenate((w_gate[0], w_up[0]), axis=1))]
    ppermute x22 -> x62, starting transfers between devices: 40.9 us -> 114 us  [the longest x61 113 us: send(): return lax.ppermute(array, AXES, pairs)]
    pallas_call x0 -> x22, Pallas kernels: none -> 60.6 us  [call(): pl.pallas_call(kernel, out_shape=outs, in_specs=[smem] + [vmem] * len(arr...]
    dot_general x30 -> x0, matrix products: 48.3 us -> none  [dot(): return jnp.einsum(spec, left, right, preferred_element_type=F32)]
    psum x1 -> x2, waiting for transfers between devices: 115 us -> 102 us  [the longest x1 65.7 us: body(): part_a = lax.psum(half_a, 'seq')]
    concatenate x13 -> x1, other arithmetic: 14 us -> 1.09 us  [body(): jnp.concatenate((jnp.concatenate((w_query[0], w_key[0], w_value[0]), axis...]
  transfers between devices with their start and end apart: 31 -> 64, of which waited for: 14 -> 14; matrix products, arithmetic and copies ran while one was open for 14% -> 1% of each run, Pallas kernels for 0% -> 8%
where the time goes in v3:
time: 543 us; the launch traced here: 533 us
  waiting for transfers between devices  285 us (52%)
  starting transfers between devices  114 us (21%)
  Pallas kernels  60.6 us (11%)
  local copies, waits for them, and re-layouts  43.7 us (8%)
  between operations  16.3 us (3%)
  other arithmetic  13.2 us (2%)
    ppermute x61, waiting for transfers between devices, send(): return lax.ppermute(array, AXES, pairs)  182 us
    ppermute x61, starting transfers between devices, send(): return lax.ppermute(array, AXES, pairs)  113 us
    psum x1, waiting for transfers between devices, body(): part_a = lax.psum(half_a, 'seq')  65.7 us
    pallas_call x22, Pallas kernels, call(): pl.pallas_call(kernel, out_shape=outs, in_specs=[smem] + [vmem] * len(arr...  60.6 us
    unnamed x213, local copies, waits for them, and re-layouts  36.8 us
    psum x1, waiting for transfers between devices, body(): part_b = lax.psum(half_b, 'seq')  35.8 us
  transfers between devices with their start and end apart: 64, of which 14 were waited for; matrix products, arithmetic and copies ran while one was open for 1% of the time, Pallas kernels for 8%

profile of v3, /device:TPU:0, one launch (start us, length us, event | category | flops | bytes accessed | tf_op | source)
XLA Modules:
  0.0 533.1 jit_solution(1456391767766876164)
XLA Ops:
  10.0 1.4 concatenate.23
  12.6 5.0 collective-permute-start
  17.5 3.4 collective-permute-start.1
  21.0 1.9 collective-permute-start.2
  22.9 3.9 collective-permute-start.8
  26.8 3.4 collective-permute-start.9
  31.5 1.9 collective-permute-start.10
  35.4 2.1 shard_map.272
  39.8 4.3 collective-permute-start.3
  44.1 4.5 collective-permute-start.4
  48.8 2.7 collective-permute-start.14
  51.6 1.8 shard_map.273
  54.8 3.1 collective-permute-start.5
  57.9 2.7 collective-permute-start.11
  60.6 3.4 collective-permute-start.6
  64.1 3.1 collective-permute-start.7
  67.3 3.4 collective-permute-start.12
  72.3 2.6 collective-permute-start.13
  75.0 7.2 %collective-permute-done.7.refs_2_ = bf16[2,128,512]{2,1,0:T(8,128)(2,1)} collective-permute-done((bf16[2,128,512]{2,1,0:T(8,128)(2,1)}, bf16[2,128,512]{2,1,0:T(8,128)(2,1)}, u32[]{:S(2)}, u32[]{:S(2)}) %collective-permute-start.7) | collective-permute-done | bytes 262176 | tf_op jit(solution)/shard_map/ppermute | solution.py:430
  82.2 2.4 collective-permute-start.15
  88.1 3.6 shard_map.274
  97.4 3.6 collective-permute-start.16
  101.1 28.4 %collective-permute-done.15.refs_6_ = bf16[512,640]{1,0:T(8,128)(2,1)S(1)} collective-permute-done((bf16[512,640]{1,0:T(8,128)(2,1)S(1)}, bf16[512,640]{1,0:T(8,128)(2,1)S(1)}, u32[]{:S(2)}, u32[]{:S(2)}) %collective-permute-start.15) | collective-permute-done | bytes 655392 | tf_op jit(solution)/shard_map/ppermute | solution.py:430
  133.1 3.9 shard_map.275
  141.9 1.5 shard_map.277
  153.2 2.6 shard_map.279
  156.9 2.5 shard_map.280
  159.5 1.4 copy-done.15
  163.1 7.4 %shard_map.281 = (bf16[128,5504]{1,0:T(8,128)(2,1)S(1)}, bf16[128,5504]{1,0:T(8,128)(2,1)}, bf16[128,5504]{1,0:T(8,128)(2,1)}, bf16[128,5504]{1,0:T(8,128)(2,1)}...) custom-call(s32[3]{0:T(128)S(1)} %pad_add_fusion.info, bf16[128,640]{1,0:T(8,128)(2,1)S(1)} %bitcast.74, ...), custom_call_target="tpu_custom_call" | custom-call | flops 1006632960 | bytes 17473536 | tf_op jit(solution)/shard_map/pallas_call | solution.py:52
  174.1 2.5 shard_map.282
  181.1 2.0 shard_map.284
  185.3 1.5 collective-permute-start.41
  186.8 2.8 shard_map.285
  189.6 3.0 shard_map.286
  192.6 95.8 %collective-permute-done.41.upstream = bf16[128,640]{1,0:T(8,128)(2,1)S(1)} collective-permute-done((bf16[128,640]{1,0:T(8,128)(2,1)S(1)}, bf16[128,640]{1,0:T(8,128)(2,1)S(1)}, u32[]{:S(2)}, u32[]{:S(2)}) %collective-permute-start.41) | collective-permute-done | bytes 163872 | tf_op jit(solution)/shard_map/ppermute | solution.py:430
  288.4 8.3 %shard_map.287 = (bf16[128,5504]{1,0:T(8,128)(2,1)S(1)}, bf16[128,5504]{1,0:T(8,128)(2,1)}, bf16[128,5504]{1,0:T(8,128)(2,1)}, bf16[128,5504]{1,0:T(8,128)(2,1)}...) custom-call(s32[3]{0:T(128)S(1)} %pad_add_fusion.info, bf16[128,640]{1,0:T(8,128)(2,1)S(1)} %collective-permute-done.41.upstream, ...), custom_call_target="tpu_custom_call" | custom-call | flops 1006632960 | bytes 17473536 | tf_op jit(solution)/shard_map/pallas_call | solution.py:52
  296.7 3.1 collective-permute-start.53
  299.9 3.3 collective-permute-start.54
  303.2 2.8 collective-permute-start.55
  307.3 3.9 shard_map.288
  312.6 3.1 collective-permute-start.48
  315.7 19.7 %collective-permute-done.48.first = bf16[2,128,512]{2,1,0:T(8,128)(2,1)S(1)} collective-permute-done((bf16[2,128,512]{2,1,0:T(8,128)(2,1)S(1)}, bf16[2,128,512]{2,1,0:T(8,128)(2,1)S(1)}, u32[]{:S(2)}, u32[]{:S(2)}) %collective-permute-start.48) | collective-permute-done | bytes 262176 | tf_op jit(solution)/shard_map/ppermute | solution.py:430
  335.5 3.0 collective-permute-start.49
  338.5 5.2 collective-permute-done.49.second
  343.7 4.0 collective-permute-start.50
  347.7 5.4 %collective-permute-done.50.third = bf16[2,128,512]{2,1,0:T(8,128)(2,1)S(1)} collective-permute-done((bf16[2,128,512]{2,1,0:T(8,128)(2,1)}, bf16[2,128,512]{2,1,0:T(8,128)(2,1)S(1)}, u32[]{:S(2)}, u32[]{:S(2)}) %collective-permute-start.50) | collective-permute-done | bytes 262176 | tf_op jit(solution)/shard_map/ppermute | solution.py:430
  353.1 1.3 shard_map.289
  357.8 4.5 shard_map.290
  364.2 2.8 broadcast_select_fusion.4
  372.1 2.4 shard_map.291
  376.1 3.1 collective-permute-start.57
  379.2 3.3 collective-permute-start.58
  382.5 3.0 collective-permute-start.59
  385.6 4.3 collective-permute-done.57.refs_1_
  389.8 11.4 %collective-permute-done.58.refs_2_ = bf16[144,2688]{1,0:T(8,128)(2,1)S(1)} collective-permute-done((bf16[144,2688]{1,0:T(8,128)(2,1)S(1)}, bf16[144,2688]{1,0:T(8,128)(2,1)S(1)}, u32[]{:S(2)}, u32[]{:S(2)}) %collective-permute-start.58) | collective-permute-done | bytes 774176 | tf_op jit(solution)/shard_map/ppermute | solution.py:430
  401.2 35.8 %all-reduce.4.cloned.1.call-done = bf16[160,4608]{1,0:T(8,128)(2,1)} async-done(((bf16[160,4608]{1,0:T(8,128)(2,1)}), bf16[160,4608]{1,0:T(8,128)(2,1)}) %all-reduce.4.cloned.1.call-update) | async-done | bytes 1474576 | tf_op jit(solution)/shard_map/psum | solution.py:645
  440.5 1.8 shard_map.292
  442.3 1.4 collective-permute-start.60
  443.7 2.8 collective-permute-done.60
  446.5 1.3 broadcast_select_fusion.3
  447.9 65.7 %all-reduce.6.cloned.1.call-done = bf16[160,4608]{1,0:T(8,128)(2,1)} async-done(((bf16[160,4608]{1,0:T(8,128)(2,1)}), bf16[160,4608]{1,0:T(8,128)(2,1)}) %all-reduce.6.cloned.1.call-update) | async-done | bytes 1474576 | tf_op jit(solution)/shard_map/psum | solution.py:649
  515.7 1.5 collective-permute-done.61
  520.3 1.8 fusion.1
  524.3 1.5 copy.36
  (339 shorter events, 78.5 us)
Async XLA Ops:
  7.2 429.8 %all-reduce.4.cloned.1.call-start = ((), (), s32[]{:S(2)}) async-start(), calls=%async_computation | async-start | bytes 2949120 | tf_op jit(solution)/shard_map/psum | solution.py:645
  12.6 18.9 %collective-permute-start = (bf16[176,1536]{1,0:T(8,128)(2,1)S(1)}, bf16[176,1536]{1,0:T(8,128)(2,1)S(1)}, u32[]{:S(2)}, u32[]{:S(2)}) collective-permute-start(bf16[176,1536]{1,0:T(8,128)(2,1)S(1)} %fusion.3.refs_0_), channel_id=1, source_target_pairs={{0,1},{1,0},{2,3},{3,2},{4,5},{5,4},{6,7},{7,6},{8,9},{9,8},{10,11... | collective-permute-start | bytes 1622024 | tf_op jit(solution)/shard_map/ppermute | solution.py:430
  17.5 17.0 %collective-permute-start.1 = (bf16[176,1536]{1,0:T(8,128)(2,1)S(1)}, bf16[176,1536]{1,0:T(8,128)(2,1)S(1)}, u32[]{:S(2)}, u32[]{:S(2)}) collective-permute-start(bf16[176,1536]{1,0:T(8,128)(2,1)S(1)} %fusion.3.refs_0_), channel_id=1, source_target_pairs={{0,2},{1,3},{2,0},{3,1},{4,6},{5,7},{6,4},{7,5},{8,10},{9,11},{10,... | collective-permute-start | bytes 1622024 | tf_op jit(solution)/shard_map/ppermute | solution.py:430
  21.0 13.6 %collective-permute-start.2 = (bf16[176,1536]{1,0:T(8,128)(2,1)S(1)}, bf16[176,1536]{1,0:T(8,128)(2,1)S(1)}, u32[]{:S(2)}, u32[]{:S(2)}) collective-permute-start(bf16[176,1536]{1,0:T(8,128)(2,1)S(1)} %fusion.3.refs_0_), channel_id=1, source_target_pairs={{0,3},{1,2},{2,1},{3,0},{4,7},{5,6},{6,5},{7,4},{8,11},{9,10},{10,... | collective-permute-start | bytes 1622024 | tf_op jit(solution)/shard_map/ppermute | solution.py:430
  22.9 35.0 %collective-permute-start.8 = (bf16[256,640]{1,0:T(8,128)(2,1)}, bf16[256,640]{1,0:T(8,128)(2,1)}, u32[]{:S(2)}, u32[]{:S(2)}) collective-permute-start(bf16[256,640]{1,0:T(8,128)(2,1)} %bitcast.61), channel_id=1, source_target_pairs={{0,1},{1,0},{2,3},{3,2},{4,5},{5,4},{6,7},{7,6},{8,9},{9,8},{10,11... | collective-permute-start | bytes 983048 | tf_op jit(solution)/shard_map/ppermute | solution.py:430
  26.8 33.9 %collective-permute-start.9 = (bf16[256,640]{1,0:T(8,128)(2,1)}, bf16[256,640]{1,0:T(8,128)(2,1)}, u32[]{:S(2)}, u32[]{:S(2)}) collective-permute-start(bf16[256,640]{1,0:T(8,128)(2,1)} %bitcast.62), channel_id=1, source_target_pairs={{0,2},{1,3},{2,0},{3,1},{4,6},{5,7},{6,4},{7,5},{8,10},{9,11},{10,... | collective-permute-start | bytes 983048 | tf_op jit(solution)/shard_map/ppermute | solution.py:430
  31.5 32.6 %collective-permute-start.10 = (bf16[256,640]{1,0:T(8,128)(2,1)}, bf16[256,640]{1,0:T(8,128)(2,1)}, u32[]{:S(2)}, u32[]{:S(2)}) collective-permute-start(bf16[256,640]{1,0:T(8,128)(2,1)} %bitcast.63), channel_id=1, source_target_pairs={{0,3},{1,2},{2,1},{3,0},{4,7},{5,6},{6,5},{7,4},{8,11},{9,10},{10,... | collective-permute-start | bytes 983048 | tf_op jit(solution)/shard_map/ppermute | solution.py:430
  39.8 9.0 %collective-permute-start.3 = (bf16[128,512]{1,0:T(8,128)(2,1)}, bf16[128,512]{1,0:T(8,128)(2,1)}, u32[]{:S(2)}, u32[]{:S(2)}) collective-permute-start(bf16[128,512]{1,0:T(8,128)(2,1)} %get-tuple-element.123.own), channel_id=1, source_target_pairs={{0,4},{1,5},{2,6},{3,7},{4,8},{5,9},{6,10},{7,11},{8,12},{9,13},{1... | collective-permute-start | bytes 393224 | tf_op jit(solution)/shard_map/ppermute | solution.py:430
  44.1 7.5 %collective-permute-start.4 = (bf16[128,512]{1,0:T(8,128)(2,1)}, bf16[128,512]{1,0:T(8,128)(2,1)}, u32[]{:S(2)}, u32[]{:S(2)}) collective-permute-start(bf16[128,512]{1,0:T(8,128)(2,1)} %get-tuple-element.123.own), channel_id=1, source_target_pairs={{0,8},{1,9},{2,10},{3,11},{4,12},{5,13},{6,14},{7,15}} | collective-permute-start | bytes 393224 | tf_op jit(solution)/shard_map/ppermute | solution.py:430
  48.8 46.5 %collective-permute-start.14 = (bf16[512,640]{1,0:T(8,128)(2,1)S(1)}, bf16[512,640]{1,0:T(8,128)(2,1)}, u32[]{:S(2)}, u32[]{:S(2)}) collective-permute-start(bf16[512,640]{1,0:T(8,128)(2,1)S(1)} %bitcast.51), channel_id=1, source_target_pairs={{0,1},{1,0},{2,3},{3,2},{4,5},{5,4},{6,7},{7,6},{8,9},{9,8},{10,11... | collective-permute-start | bytes 1966088 | tf_op jit(solution)/shard_map/ppermute | solution.py:430
  54.8 12.5 %collective-permute-start.5 = (bf16[2,128,512]{2,1,0:T(8,128)(2,1)}, bf16[2,128,512]{2,1,0:T(8,128)(2,1)}, u32[]{:S(2)}, u32[]{:S(2)}) collective-permute-start(bf16[2,128,512]{2,1,0:T(8,128)(2,1)} %get-tuple-element.124), channel_id=1, source_target_pairs={{0,1},{1,0},{2,3},{3,2},{4,5},{5,4},{6,7},{7,6},{8,9},{9,8},{10,11... | collective-permute-start | bytes 786440 | tf_op jit(solution)/shard_map/ppermute | solution.py:430
  57.9 73.0 %collective-permute-start.11 = (bf16[160,4096]{1,0:T(8,128)(2,1)S(1)}, bf16[160,4096]{1,0:T(8,128)(2,1)}, u32[]{:S(2)}, u32[]{:S(2)}) collective-permute-start(bf16[160,4096]{1,0:T(8,128)(2,1)S(1)} %pad_maximum_fusion.refs_0_), channel_id=1, source_target_pairs={{0,1},{1,0},{2,3},{3,2},{4,5},{5,4},{6,7},{7,6},{8,9},{9,8},{10,11... | collective-permute-start | bytes 3932168 | tf_op jit(solution)/shard_map/ppermute | solution.py:430
  60.6 11.7 %collective-permute-start.6 = (bf16[2,128,512]{2,1,0:T(8,128)(2,1)}, bf16[2,128,512]{2,1,0:T(8,128)(2,1)}, u32[]{:S(2)}, u32[]{:S(2)}) collective-permute-start(bf16[2,128,512]{2,1,0:T(8,128)(2,1)} %copy-done.96), channel_id=1, source_target_pairs={{0,2},{1,3},{2,0},{3,1},{4,6},{5,7},{6,4},{7,5},{8,10},{9,11},{10,... | collective-permute-start | bytes 786440 | tf_op jit(solution)/shard_map/ppermute | solution.py:430
  64.1 18.1 %collective-permute-start.7 = (bf16[2,128,512]{2,1,0:T(8,128)(2,1)}, bf16[2,128,512]{2,1,0:T(8,128)(2,1)}, u32[]{:S(2)}, u32[]{:S(2)}) collective-permute-start(bf16[2,128,512]{2,1,0:T(8,128)(2,1)} %copy-done.95), channel_id=1, source_target_pairs={{0,3},{1,2},{2,1},{3,0},{4,7},{5,6},{6,5},{7,4},{8,11},{9,10},{10,... | collective-permute-start | bytes 786440 | tf_op jit(solution)/shard_map/ppermute | solution.py:430
  67.3 64.4 %collective-permute-start.12 = (bf16[160,4096]{1,0:T(8,128)(2,1)S(1)}, bf16[160,4096]{1,0:T(8,128)(2,1)}, u32[]{:S(2)}, u32[]{:S(2)}) collective-permute-start(bf16[160,4096]{1,0:T(8,128)(2,1)S(1)} %pad_maximum_fusion.refs_0_), channel_id=1, source_target_pairs={{0,2},{1,3},{2,0},{3,1},{4,6},{5,7},{6,4},{7,5},{8,10},{9,11},{10,... | collective-permute-start | bytes 3932168 | tf_op jit(solution)/shard_map/ppermute | solution.py:430
  72.3 60.0 %collective-permute-start.13 = (bf16[160,4096]{1,0:T(8,128)(2,1)S(1)}, bf16[160,4096]{1,0:T(8,128)(2,1)S(1)}, u32[]{:S(2)}, u32[]{:S(2)}) collective-permute-start(bf16[160,4096]{1,0:T(8,128)(2,1)S(1)} %pad_maximum_fusion.refs_0_), channel_id=1, source_target_pairs={{0,3},{1,2},{2,1},{3,0},{4,7},{5,6},{6,5},{7,4},{8,11},{9,10},{10,... | collective-permute-start | bytes 3932168 | tf_op jit(solution)/shard_map/ppermute | solution.py:430
  82.2 47.4 %collective-permute-start.15 = (bf16[512,640]{1,0:T(8,128)(2,1)S(1)}, bf16[512,640]{1,0:T(8,128)(2,1)S(1)}, u32[]{:S(2)}, u32[]{:S(2)}) collective-permute-start(bf16[512,640]{1,0:T(8,128)(2,1)S(1)} %bitcast.52), channel_id=1, source_target_pairs={{0,2},{1,3},{2,0},{3,1},{4,6},{5,7},{6,4},{7,5},{8,10},{9,11},{10,... | collective-permute-start | bytes 1966088 | tf_op jit(solution)/shard_map/ppermute | solution.py:430
  95.3 2.1 collective-permute-start.18
  97.4 32.8 %collective-permute-start.16 = (bf16[512,640]{1,0:T(8,128)(2,1)S(1)}, bf16[512,640]{1,0:T(8,128)(2,1)S(1)}, u32[]{:S(2)}, u32[]{:S(2)}) collective-permute-start(bf16[512,640]{1,0:T(8,128)(2,1)S(1)} %bitcast.53), channel_id=1, source_target_pairs={{0,3},{1,2},{2,1},{3,0},{4,7},{5,6},{6,5},{7,4},{8,11},{9,10},{10,... | collective-permute-start | bytes 1966088 | tf_op jit(solution)/shard_map/ppermute | solution.py:430
  129.5 9.0 %collective-permute-start.19 = (bf16[176,1536]{1,0:T(8,128)(2,1)S(1)}, bf16[176,1536]{1,0:T(8,128)(2,1)S(1)}, u32[]{:S(2)}, u32[]{:S(2)}) collective-permute-start(bf16[176,1536]{1,0:T(8,128)(2,1)S(1)} %constant_dynamic-update-slice_fusion.refs_0_), channel_id=1, source_target_pairs={{16,17},{17,16},{18,19},{19,18},{20,21},{21,20},{22,23},{23,22},{2... | collective-permute-start | bytes 1622024 | tf_op jit(solution)/shard_map/ppermute | solution.py:430
  130.2 9.6 %collective-permute-start.20 = (bf16[176,1536]{1,0:T(8,128)(2,1)S(1)}, bf16[176,1536]{1,0:T(8,128)(2,1)S(1)}, u32[]{:S(2)}, u32[]{:S(2)}) collective-permute-start(bf16[176,1536]{1,0:T(8,128)(2,1)S(1)} %constant_dynamic-update-slice_fusion.refs_0_), channel_id=1, source_target_pairs={{16,18},{17,19},{18,16},{19,17},{20,22},{21,23},{22,20},{23,21},{2... | collective-permute-start | bytes 1622024 | tf_op jit(solution)/shard_map/ppermute | solution.py:430
  131.0 9.6 %collective-permute-start.21 = (bf16[176,1536]{1,0:T(8,128)(2,1)S(1)}, bf16[176,1536]{1,0:T(8,128)(2,1)S(1)}, u32[]{:S(2)}, u32[]{:S(2)}) collective-permute-start(bf16[176,1536]{1,0:T(8,128)(2,1)S(1)} %constant_dynamic-update-slice_fusion.refs_0_), channel_id=1, source_target_pairs={{16,19},{17,18},{18,17},{19,16},{20,23},{21,22},{22,21},{23,20},{2... | collective-permute-start | bytes 1622024 | tf_op jit(solution)/shard_map/ppermute | solution.py:430
  131.7 14.0 %collective-permute-start.27 = (bf16[256,640]{1,0:T(8,128)(2,1)S(1)}, bf16[256,640]{1,0:T(8,128)(2,1)S(1)}, u32[]{:S(2)}, u32[]{:S(2)}) collective-permute-start(bf16[256,640]{1,0:T(8,128)(2,1)S(1)} %bitcast.65), channel_id=1, source_target_pairs={{16,17},{17,16},{18,19},{19,18},{20,21},{21,20},{22,23},{23,22},{2... | collective-permute-start | bytes 983048 | tf_op jit(solution)/shard_map/ppermute | solution.py:430
  132.4 14.0 %collective-permute-start.28 = (bf16[256,640]{1,0:T(8,128)(2,1)S(1)}, bf16[256,640]{1,0:T(8,128)(2,1)S(1)}, u32[]{:S(2)}, u32[]{:S(2)}) collective-permute-start(bf16[256,640]{1,0:T(8,128)(2,1)S(1)} %bitcast.66), channel_id=1, source_target_pairs={{16,18},{17,19},{18,16},{19,17},{20,22},{21,23},{22,20},{23,21},{2... | collective-permute-start | bytes 983048 | tf_op jit(solution)/shard_map/ppermute | solution.py:430
  138.5 3.4 collective-permute-start.17
  139.8 10.3 %collective-permute-start.33 = (bf16[512,640]{1,0:T(8,128)(2,1)S(1)}, bf16[512,640]{1,0:T(8,128)(2,1)S(1)}, u32[]{:S(2)}, u32[]{:S(2)}) collective-permute-start(bf16[512,640]{1,0:T(8,128)(2,1)S(1)} %bitcast.55), channel_id=1, source_target_pairs={{16,17},{17,16},{18,19},{19,18},{20,21},{21,20},{22,23},{23,22},{2... | collective-permute-start | bytes 1966088 | tf_op jit(solution)/shard_map/ppermute | solution.py:430
  140.5 8.9 %collective-permute-start.29 = (bf16[256,640]{1,0:T(8,128)(2,1)S(1)}, bf16[256,640]{1,0:T(8,128)(2,1)S(1)}, u32[]{:S(2)}, u32[]{:S(2)}) collective-permute-start(bf16[256,640]{1,0:T(8,128)(2,1)S(1)} %bitcast.67), channel_id=1, source_target_pairs={{16,19},{17,18},{18,17},{19,16},{20,23},{21,22},{22,21},{23,20},{2... | collective-permute-start | bytes 983048 | tf_op jit(solution)/shard_map/ppermute | solution.py:430
  145.0 2.1 collective-permute-start.22
  145.7 2.2 collective-permute-start.23
  146.4 10.5 %collective-permute-start.30 = (bf16[160,4096]{1,0:T(8,128)(2,1)S(1)}, bf16[160,4096]{1,0:T(8,128)(2,1)S(1)}, u32[]{:S(2)}, u32[]{:S(2)}) collective-permute-start(bf16[160,4096]{1,0:T(8,128)(2,1)S(1)} %pad_maximum_fusion.refs_0_), channel_id=1, source_target_pairs={{16,17},{17,16},{18,19},{19,18},{20,21},{21,20},{22,23},{23,22},{2... | collective-permute-start | bytes 3932168 | tf_op jit(solution)/shard_map/ppermute | solution.py:430
  147.2 9.7 %collective-permute-start.31 = (bf16[160,4096]{1,0:T(8,128)(2,1)S(1)}, bf16[160,4096]{1,0:T(8,128)(2,1)S(1)}, u32[]{:S(2)}, u32[]{:S(2)}) collective-permute-start(bf16[160,4096]{1,0:T(8,128)(2,1)S(1)} %pad_maximum_fusion.refs_0_), channel_id=1, source_target_pairs={{16,18},{17,19},{18,16},{19,17},{20,22},{21,23},{22,20},{23,21},{2... | collective-permute-start | bytes 3932168 | tf_op jit(solution)/shard_map/ppermute | solution.py:430
  147.9 9.0 %collective-permute-start.32 = (bf16[160,4096]{1,0:T(8,128)(2,1)S(1)}, bf16[160,4096]{1,0:T(8,128)(2,1)S(1)}, u32[]{:S(2)}, u32[]{:S(2)}) collective-permute-start(bf16[160,4096]{1,0:T(8,128)(2,1)S(1)} %pad_maximum_fusion.refs_0_), channel_id=1, source_target_pairs={{16,19},{17,18},{18,17},{19,16},{20,23},{21,22},{22,21},{23,20},{2... | collective-permute-start | bytes 3932168 | tf_op jit(solution)/shard_map/ppermute | solution.py:430
  149.4 1.4 collective-permute-start.24
  150.1 1.4 collective-permute-start.25
  150.8 1.4 collective-permute-start.26
  151.5 5.3 %collective-permute-start.34 = (bf16[512,640]{1,0:T(8,128)(2,1)S(1)}, bf16[512,640]{1,0:T(8,128)(2,1)S(1)}, u32[]{:S(2)}, u32[]{:S(2)}) collective-permute-start(bf16[512,640]{1,0:T(8,128)(2,1)S(1)} %bitcast.56), channel_id=1, source_target_pairs={{16,18},{17,19},{18,16},{19,17},{20,22},{21,23},{22,20},{23,21},{2... | collective-permute-start | bytes 1966088 | tf_op jit(solution)/shard_map/ppermute | solution.py:430
  152.2 4.6 collective-permute-start.35
  170.5 14.0 %collective-permute-start.45 = (bf16[128,5504]{1,0:T(8,128)(2,1)}, bf16[128,5504]{1,0:T(8,128)(2,1)S(1)}, u32[]{:S(2)}, u32[]{:S(2)}) collective-permute-start(bf16[128,5504]{1,0:T(8,128)(2,1)} %get-tuple-element.173), channel_id=1, source_target_pairs={{16,17},{17,16},{18,19},{19,18},{20,21},{21,20},{22,23},{23,22},{2... | collective-permute-start | bytes 4227080 | tf_op jit(solution)/shard_map/ppermute | solution.py:430
  171.3 14.0 %collective-permute-start.46 = (bf16[128,5504]{1,0:T(8,128)(2,1)}, bf16[128,5504]{1,0:T(8,128)(2,1)S(1)}, u32[]{:S(2)}, u32[]{:S(2)}) collective-permute-start(bf16[128,5504]{1,0:T(8,128)(2,1)} %get-tuple-element.174), channel_id=1, source_target_pairs={{16,18},{17,19},{18,16},{19,17},{20,22},{21,23},{22,20},{23,21},{2... | collective-permute-start | bytes 4227080 | tf_op jit(solution)/shard_map/ppermute | solution.py:430
  172.0 14.8 %collective-permute-start.47 = (bf16[128,5504]{1,0:T(8,128)(2,1)}, bf16[128,5504]{1,0:T(8,128)(2,1)S(1)}, u32[]{:S(2)}, u32[]{:S(2)}) collective-permute-start(bf16[128,5504]{1,0:T(8,128)(2,1)} %get-tuple-element.175), channel_id=1, source_target_pairs={{16,19},{17,18},{18,17},{19,16},{20,23},{21,22},{22,21},{23,20},{2... | collective-permute-start | bytes 4227080 | tf_op jit(solution)/shard_map/ppermute | solution.py:430
  176.7 1.5 collective-permute-start.36
  177.5 1.4 collective-permute-start.37
  178.2 0.7 collective-permute-start.38
  179.7 1.4 collective-permute-start.39
  180.4 0.7 collective-permute-start.40
  183.1 6.5 %collective-permute-start.42 = (bf16[144,2688]{1,0:T(8,128)(2,1)S(1)}, bf16[144,2688]{1,0:T(8,128)(2,1)S(1)}, u32[]{:S(2)}, u32[]{:S(2)}) collective-permute-start(bf16[144,2688]{1,0:T(8,128)(2,1)S(1)} %get-tuple-element.169), channel_id=1, source_target_pairs={{16,17},{17,16},{18,19},{19,18},{20,21},{21,20},{22,23},{23,22},{2... | collective-permute-start | bytes 2322440 | tf_op jit(solution)/shard_map/ppermute | solution.py:430
  183.8 5.8 %collective-permute-start.43 = (bf16[144,2688]{1,0:T(8,128)(2,1)S(1)}, bf16[144,2688]{1,0:T(8,128)(2,1)S(1)}, u32[]{:S(2)}, u32[]{:S(2)}) collective-permute-start(bf16[144,2688]{1,0:T(8,128)(2,1)S(1)} %get-tuple-element.170), channel_id=1, source_target_pairs={{16,18},{17,19},{18,16},{19,17},{20,22},{21,23},{22,20},{23,21},{2... | collective-permute-start | bytes 2322440 | tf_op jit(solution)/shard_map/ppermute | solution.py:430
  184.5 5.0 collective-permute-start.44
  185.3 103.1 %collective-permute-start.41 = (bf16[128,640]{1,0:T(8,128)(2,1)S(1)}, bf16[128,640]{1,0:T(8,128)(2,1)S(1)}, u32[]{:S(2)}, u32[]{:S(2)}) collective-permute-start(bf16[128,640]{1,0:T(8,128)(2,1)S(1)} %get-tuple-element.167), channel_id=1, source_target_pairs={{16,0},{17,1},{18,2},{19,3},{20,4},{21,5},{22,6},{23,7},{24,8},{25... | collective-permute-start | bytes 491528 | tf_op jit(solution)/shard_map/ppermute | solution.py:430
  296.7 59.7 %collective-permute-start.53 = (bf16[128,5504]{1,0:T(8,128)(2,1)}, bf16[128,5504]{1,0:T(8,128)(2,1)}, u32[]{:S(2)}, u32[]{:S(2)}) collective-permute-start(bf16[128,5504]{1,0:T(8,128)(2,1)} %get-tuple-element.197), channel_id=1, source_target_pairs={{0,1},{1,0},{2,3},{3,2},{4,5},{5,4},{6,7},{7,6},{8,9},{9,8},{10,11... | collective-permute-start | bytes 4227080 | tf_op jit(solution)/shard_map/ppermute | solution.py:430
  299.9 57.9 %collective-permute-start.54 = (bf16[128,5504]{1,0:T(8,128)(2,1)}, bf16[128,5504]{1,0:T(8,128)(2,1)}, u32[]{:S(2)}, u32[]{:S(2)}) collective-permute-start(bf16[128,5504]{1,0:T(8,128)(2,1)} %get-tuple-element.198), channel_id=1, source_target_pairs={{0,2},{1,3},{2,0},{3,1},{4,6},{5,7},{6,4},{7,5},{8,10},{9,11},{10,... | collective-permute-start | bytes 4227080 | tf_op jit(solution)/shard_map/ppermute | solution.py:430
  303.2 54.5 %collective-permute-start.55 = (bf16[128,5504]{1,0:T(8,128)(2,1)}, bf16[128,5504]{1,0:T(8,128)(2,1)}, u32[]{:S(2)}, u32[]{:S(2)}) collective-permute-start(bf16[128,5504]{1,0:T(8,128)(2,1)} %get-tuple-element.199), channel_id=1, source_target_pairs={{0,3},{1,2},{2,1},{3,0},{4,7},{5,6},{6,5},{7,4},{8,11},{9,10},{10,... | collective-permute-start | bytes 4227080 | tf_op jit(solution)/shard_map/ppermute | solution.py:430
  306.0 58.2 %collective-permute-start.56 = (bf16[160,4608]{1,0:T(8,128)(2,1)}, bf16[160,4608]{1,0:T(8,128)(2,1)}, u32[]{:S(2)}, u32[]{:S(2)}) collective-permute-start(bf16[160,4608]{1,0:T(8,128)(2,1)} %get-tuple-element.202), channel_id=1, source_target_pairs={{16,0},{17,1},{18,2},{19,3},{20,4},{21,5},{22,6},{23,7},{24,8},{25... | collective-permute-start | bytes 4423688 | tf_op jit(solution)/shard_map/ppermute | solution.py:430
  312.6 22.8 %collective-permute-start.48 = (bf16[2,128,512]{2,1,0:T(8,128)(2,1)S(1)}, bf16[2,128,512]{2,1,0:T(8,128)(2,1)S(1)}, u32[]{:S(2)}, u32[]{:S(2)}) collective-permute-start(bf16[2,128,512]{2,1,0:T(8,128)(2,1)S(1)} %get-tuple-element.190), channel_id=1, source_target_pairs={{0,1},{1,0},{2,3},{3,2},{4,5},{5,4},{6,7},{7,6},{8,9},{9,8},{10,11... | collective-permute-start | bytes 786440 | tf_op jit(solution)/shard_map/ppermute | solution.py:430
  335.5 8.3 %collective-permute-start.49 = (bf16[2,128,512]{2,1,0:T(8,128)(2,1)S(1)}, bf16[2,128,512]{2,1,0:T(8,128)(2,1)S(1)}, u32[]{:S(2)}, u32[]{:S(2)}) collective-permute-start(bf16[2,128,512]{2,1,0:T(8,128)(2,1)S(1)} %get-tuple-element.191), channel_id=1, source_target_pairs={{0,2},{1,3},{2,0},{3,1},{4,6},{5,7},{6,4},{7,5},{8,10},{9,11},{10,... | collective-permute-start | bytes 786440 | tf_op jit(solution)/shard_map/ppermute | solution.py:430
  343.7 9.4 %collective-permute-start.50 = (bf16[2,128,512]{2,1,0:T(8,128)(2,1)}, bf16[2,128,512]{2,1,0:T(8,128)(2,1)S(1)}, u32[]{:S(2)}, u32[]{:S(2)}) collective-permute-start(bf16[2,128,512]{2,1,0:T(8,128)(2,1)} %get-tuple-element.192), channel_id=1, source_target_pairs={{0,3},{1,2},{2,1},{3,0},{4,7},{5,6},{6,5},{7,4},{8,11},{9,10},{10,... | collective-permute-start | bytes 786440 | tf_op jit(solution)/shard_map/ppermute | solution.py:430
  355.1 12.0 %collective-permute-start.51 = (bf16[128,512]{1,0:T(8,128)(2,1)}, bf16[128,512]{1,0:T(8,128)(2,1)}, u32[]{:S(2)}, u32[]{:S(2)}) collective-permute-start(bf16[128,512]{1,0:T(8,128)(2,1)} %get-tuple-element.194), channel_id=1, source_target_pairs={{4,0},{5,1},{6,2},{7,3},{8,4},{9,5},{10,6},{11,7},{12,8},{13,9},{1... | collective-permute-start | bytes 393224 | tf_op jit(solution)/shard_map/ppermute | solution.py:430
  356.4 10.7 %collective-permute-start.52 = (bf16[128,512]{1,0:T(8,128)(2,1)}, bf16[128,512]{1,0:T(8,128)(2,1)}, u32[]{:S(2)}, u32[]{:S(2)}) collective-permute-start(bf16[128,512]{1,0:T(8,128)(2,1)} %get-tuple-element.195), channel_id=1, source_target_pairs={{8,0},{9,1},{10,2},{11,3},{12,4},{13,5},{14,6},{15,7}} | collective-permute-start | bytes 393224 | tf_op jit(solution)/shard_map/ppermute | solution.py:430
  367.1 146.6 %all-reduce.6.cloned.1.call-start = ((), (), s32[]{:S(2)}) async-start(), calls=%async_computation.1 | async-start | bytes 2949120 | tf_op jit(solution)/shard_map/psum | solution.py:649
  376.1 13.7 %collective-permute-start.57 = (bf16[144,2688]{1,0:T(8,128)(2,1)S(1)}, bf16[144,2688]{1,0:T(8,128)(2,1)S(1)}, u32[]{:S(2)}, u32[]{:S(2)}) collective-permute-start(bf16[144,2688]{1,0:T(8,128)(2,1)S(1)} %get-tuple-element.216), channel_id=1, source_target_pairs={{0,1},{1,0},{2,3},{3,2},{4,5},{5,4},{6,7},{7,6},{8,9},{9,8},{10,11... | collective-permute-start | bytes 2322440 | tf_op jit(solution)/shard_map/ppermute | solution.py:430
  379.2 22.0 %collective-permute-start.58 = (bf16[144,2688]{1,0:T(8,128)(2,1)S(1)}, bf16[144,2688]{1,0:T(8,128)(2,1)S(1)}, u32[]{:S(2)}, u32[]{:S(2)}) collective-permute-start(bf16[144,2688]{1,0:T(8,128)(2,1)S(1)} %get-tuple-element.217), channel_id=1, source_target_pairs={{0,2},{1,3},{2,0},{3,1},{4,6},{5,7},{6,4},{7,5},{8,10},{9,11},{10,... | collective-permute-start | bytes 2322440 | tf_op jit(solution)/shard_map/ppermute | solution.py:430
  382.5 18.7 %collective-permute-start.59 = (bf16[144,2688]{1,0:T(8,128)(2,1)S(1)}, bf16[144,2688]{1,0:T(8,128)(2,1)S(1)}, u32[]{:S(2)}, u32[]{:S(2)}) collective-permute-start(bf16[144,2688]{1,0:T(8,128)(2,1)S(1)} %get-tuple-element.218), channel_id=1, source_target_pairs={{0,3},{1,2},{2,1},{3,0},{4,7},{5,6},{6,5},{7,4},{8,11},{9,10},{10,... | collective-permute-start | bytes 2322440 | tf_op jit(solution)/shard_map/ppermute | solution.py:430
  442.3 4.2 collective-permute-start.60
  513.8 3.4 collective-permute-start.61
  (105 other events, 1559.6 us)
Sparse Core Ops, SparseCore 0:
  367.2 69.7 all-reduce.3
  448.0 65.6 all-reduce.5
